TPU v7x, 32 devices: a whole 2x2x4 slice. The times are simulated.
32 devices in a mesh: dp: 8 (over z, y), ctx: 4 (over x, core).
Axes of the slice: x: 2, y: 2, z: 4, core: 2. Of those that a mesh axis runs over, the one named last changes fastest.
Arguments:
- queries: bfloat16 [8, 512, 16, 128], P('dp', 'ctx'), may hold values from -6 to 6
- keys: bfloat16 [8, 512, 16, 128], P('dp', 'ctx'), may hold values from -6 to 6
- values: bfloat16 [8, 512, 16, 128], P('dp', 'ctx'), may hold values from -6 to 6
- out_grad: bfloat16 [8, 512, 16, 128], P('dp', 'ctx'), may hold values from -0.59765625 to 0.59765625
- gate_weight: bfloat16 [16, 128], P(None, 'dp'), may hold values from -0.5 to 0.5
- head_bias: bfloat16 [16], replicated, as said below
Outputs:
- query_grad: bfloat16 [8, 512, 16, 128], P('dp', 'ctx')
- key_grad: bfloat16 [8, 512, 16, 128], P('dp', 'ctx')
- gate_grad: float32 [16, 128], P(None, 'dp')
Inputs may be any that keep to these rules, and one draw needn't show every extreme that they name: `head_bias`: each entry lies between -ln(512) - 1.5 and -3.5.
All inputs are finite; a program needn't handle non-finite values.
Results may differ from a plain program's by a relative error of at most 0.0038.
The roundings to bfloat16 on the way count: a program that leaves them out, or rounds other values in their place, can miss the bound.
Values may be sent and summed in bfloat16 or wider, within the bound.
No kernel may reach another device: no remote copies, remote signals or barrier semaphores. Data moves between devices by JAX's collectives and lax.ppermute only.
A program may use at most 128 MiB of HBM per device.

v0:
```python
import jax
import jax.numpy as jnp
from jax import lax
from jax.sharding import PartitionSpec as P


def carried_in(shard, axis, combine, identity, reverse):
    devices, mine = (lax.axis_size(axis), lax.axis_index(axis))
    everything = jax.tree.map(lambda part: lax.all_gather(part, axis), shard)
    start = jax.tree.map(
        lambda part, zero: jnp.broadcast_to(jnp.asarray(zero, part.dtype), part.shape),
        shard,
        identity,
    )

    def hop(k, before):
        at = devices - 1 - k if reverse else k
        reached = at > mine if reverse else at < mine
        new = combine(before, jax.tree.map(lambda part: part[at], everything))
        return jax.tree.map(lambda a, b: jnp.where(reached, a, b), new, before)

    return lax.fori_loop(0, devices, hop, start)


def gate_logit(keys_block, gate_rows, bias_rows):
    return (
        jnp.sum(keys_block.astype(jnp.float32) * gate_rows.astype(jnp.float32)[None], -1)
        + bias_rows.astype(jnp.float32)[None]
    )


def key_state(keys_block, values_block, cumul):
    tail = jnp.exp(cumul[-1][None] - cumul)[:, :, None]
    scaled = (keys_block.astype(jnp.float32) * tail).astype(jnp.bfloat16)
    return (
        jnp.exp(cumul[-1]),
        jnp.einsum("chd,che->hde", scaled, values_block, preferred_element_type=jnp.float32),
    )


def query_state(queries_block, grads_block, cumul):
    head = jnp.exp(cumul)[:, :, None]
    scaled = (queries_block.astype(jnp.float32) * head).astype(jnp.bfloat16)
    return (
        jnp.exp(cumul[-1]),
        jnp.einsum("chd,che->hde", scaled, grads_block, preferred_element_type=jnp.float32),
    )


def block_grads(
    queries_block, keys_block, values_block, grads_block, cumul, incoming, outgoing, scale
):
    count = queries_block.shape[0]
    rows = lax.broadcasted_iota(jnp.int32, (count, count), 0)
    cols = lax.broadcasted_iota(jnp.int32, (count, count), 1)
    causal = rows >= cols
    trans = cumul.T
    gap = trans[:, :, None] - trans[:, None, :]
    decay = jnp.exp(jnp.where(causal[None], gap, -1e30))
    products = jnp.einsum(
        "the,she->hts", grads_block, values_block, preferred_element_type=jnp.float32
    )
    wround = (scale * products * decay).astype(jnp.bfloat16)
    head = jnp.exp(cumul)[:, :, None]
    tail = jnp.exp(cumul[-1][None] - cumul)[:, :, None]
    in_round = incoming.astype(jnp.bfloat16)
    out_round = outgoing.astype(jnp.bfloat16)
    qgrad = jnp.einsum(
        "hts,shd->thd", wround, keys_block, preferred_element_type=jnp.float32
    ) + scale * head * jnp.einsum(
        "the,hde->thd", grads_block, in_round, preferred_element_type=jnp.float32
    )
    kgrad = jnp.einsum(
        "hts,thd->shd", wround, queries_block, preferred_element_type=jnp.float32
    ) + scale * tail * jnp.einsum(
        "she,hde->shd", values_block, out_round, preferred_element_type=jnp.float32
    )
    dgsum = jnp.sum(queries_block.astype(jnp.float32) * qgrad, -1) - jnp.sum(
        keys_block.astype(jnp.float32) * kgrad, -1
    )
    return (qgrad, kgrad, dgsum)


def finish(qgrad, kgrad, dgsum, after, logit, keys_block, gate_rows):
    total = after[None] + jnp.sum(dgsum, 0)[None] - jnp.cumsum(dgsum, 0) + dgsum
    dlogit = -jax.nn.sigmoid(logit) * total
    rounded = lax.optimization_barrier(kgrad.astype(jnp.bfloat16)).astype(jnp.float32)
    key_out = (rounded + dlogit[:, :, None] * gate_rows.astype(jnp.float32)[None]).astype(
        jnp.bfloat16
    )
    weight_term = jnp.sum(dlogit[:, :, None] * keys_block.astype(jnp.float32), 0)
    return (qgrad.astype(jnp.bfloat16), key_out, weight_term)


def combine(earlier, later):
    return (earlier[0] * later[0], later[0][:, None, None] * earlier[1] + later[1])


def add_totals(earlier, later):
    return earlier + later


def per_device(queries, keys, values, out_grad, gate_weight, head_bias):
    gate_full = lax.all_gather(gate_weight, "dp", axis=1, tiled=True)
    heads, width = (queries.shape[2], queries.shape[3])
    qx, kx, vx, gx = (queries[0], keys[0], values[0], out_grad[0])
    scale = 1.0 / width
    logit = gate_logit(kx, gate_full, head_bias)
    cumul = jnp.cumsum(-jax.nn.softplus(logit), axis=0)
    factor, key_update = key_state(kx, vx, cumul)
    _, query_update = query_state(qx, gx, cumul)
    ones = jnp.ones((heads,), jnp.float32)
    zeros = jnp.zeros((heads, width, width), jnp.float32)
    incoming = carried_in((factor, key_update), "ctx", combine, (ones, zeros), False)[1]
    outgoing = carried_in((factor, query_update), "ctx", combine, (ones, zeros), True)[1]
    qgrad, kgrad, dgsum = block_grads(qx, kx, vx, gx, cumul, incoming, outgoing, scale)
    after = carried_in(jnp.sum(dgsum, 0), "ctx", add_totals, jnp.zeros((heads,), jnp.float32), True)
    qout, kout, term = finish(qgrad, kgrad, dgsum, after, logit, kx, gate_full)
    query_grad, key_grad = (qout[None], kout[None])
    summed = lax.psum(term, ("dp", "ctx"))
    piece = gate_weight.shape[1]
    gate_grad = lax.dynamic_slice_in_dim(summed, lax.axis_index("dp") * piece, piece, 1)
    return (query_grad, key_grad, gate_grad)


def solution(mesh):
    return jax.shard_map(
        per_device,
        mesh=mesh,
        in_specs=(
            P("dp", "ctx", None, None),
            P("dp", "ctx", None, None),
            P("dp", "ctx", None, None),
            P("dp", "ctx", None, None),
            P(None, "dp"),
            P(),
        ),
        out_specs=(P("dp", "ctx", None, None), P("dp", "ctx", None, None), P(None, "dp")),
        check_vma=False,
    )
```

profile of v0, /device:TPU:0, one launch (start us, length us, event | category | flops | bytes accessed | tf_op | source)
XLA Modules:
  0.0 182.0 jit_solution(17282678961639068271)
XLA Ops:
  7.2 1.6 copy.50
  9.6 32.2 %all_gather.27 = bf16[16,128]{0,1:T(8,128)(2,1)S(1)} all-gather(bf16[16,16]{0,1:T(8,128)(2,1)S(1)} %copy.51), channel_id=1, replica_groups=mesh['dp'=8,'ctx'=4] {'dp'}, dimensions={1}, use_global_device_ids=true | all-gather | bytes 4608 | tf_op jit(solution)/shard_map/all_gather | solution.py:104
  43.3 1.3 fusion.15
  45.2 1.4 fusion.17
  48.2 5.0 %all-gather.3 = f32[4,1,16]{2,1,0:T(1,128)S(1)} all-gather(f32[1,1,16]{2,1,0:T(1,128)S(1)} %get-tuple-element.443), channel_id=1, replica_groups=mesh['dp'=8,'ctx'=4] {'ctx'}, dimensions={0}, use_global_device_ids=true | all-gather | bytes 320 | tf_op jit(solution)/shard_map/all_gather | solution.py:9
  53.2 1.6 fusion.7
  55.7 1.5 convolution_bitcast_fusion.3
  57.1 23.1 %all-gather.7.cloned.1.call-done = f32[64,128,128]{2,1,0:T(8,128)} async-done(((f32[16,128,128]{2,1,0:T(8,128)}), f32[64,128,128]{2,1,0:T(8,128)}) %all-gather.7.cloned.1.call-update) | async-done | bytes 4194320 | tf_op jit(solution)/shard_map/all_gather | solution.py:9
  80.2 6.0 %while.46 = (s32[]{:T(128)}, f32[16,128,128]{2,1,0:T(8,128)S(1)}, s32[]{:T(128)}, f32[4,16]{1,0:T(4,128)S(1)}, f32[4,16,128,128]{3,2,1,0:T(8,128)}, /*index=5*/s32[]{:T(128)}, s32[]{:T(128)}) while((s32[]{:T(128)}, f32[16,128,128]{2,1,0:T(8,128)S(1)}, s32[]{:T(128)}, f32[4,16]{1,0:T(4,128)S(1)}, f32[4,16,128,128]{3,2,1,0:T(8,128)}, ...), condition=%wide.region_3.4_spmd.clone, body=%wide.region_2.3_spmd.clone.sunk | while | flops 1048580 | bytes 3146025 | solution.py:22
  80.2 1.5 fusion.44
  81.7 1.5 fusion.44
  83.2 1.5 fusion.44
  84.7 1.5 fusion.44
  86.2 2.9 %fusion.9 = (f32[128,16]{0,1:T(8,128)S(1)}, bf16[1,128,16,128]{1,3,2,0:T(8,128)(2,1)}) fusion(bf16[1,128,16,128]{1,3,2,0:T(8,128)(2,1)} %copy-done.1, f32[128,16,128]{0,2,1:T(8,128)} %convolution_bitcast_fusion.3, bf16[128,16,128]{2,1,0:T(8,128)(2,1)} %bitcast.85, f32[16,128,128]{2,1,0:T(8,128)S(1)} %get-tuple-element.339, f32[128,16]{0,1:T(8,128)S(1)} %copy.56), kind=kOutput, calls=%fused_computation.26 | convolution fusion | flops 68941824 | bytes 3686400 | tf_op jit(solution)/shard_map/the,hde->thd/dot_general | solution.py:70
  89.2 27.1 %all-gather.9.cloned.1.call-done = f32[64,128,128]{2,1,0:T(8,128)} async-done(((f32[16,128,128]{2,1,0:T(8,128)}), f32[64,128,128]{2,1,0:T(8,128)}) %all-gather.9.cloned.1.call-update) | async-done | bytes 4194320 | tf_op jit(solution)/shard_map/all_gather | solution.py:9
  116.3 6.1 %while.47 = (s32[]{:T(128)}, f32[16,128,128]{2,1,0:T(8,128)S(1)}, s32[]{:T(128)}, f32[4,16]{1,0:T(4,128)S(1)}, f32[4,16,128,128]{3,2,1,0:T(8,128)}, /*index=5*/s32[]{:T(128)}, s32[]{:T(128)}, s32[]{:T(128)}, s32[]{:T(128)}) while((s32[]{:T(128)}, f32[16,128,128]{2,1,0:T(8,128)S(1)}, s32[]{:T(128)}, f32[4,16]{1,0:T(4,128)S(1)}, ...), condition=%wide.region_5.6_spmd.clone, body=%wide.region_4.5_spmd.clone.sunk | while | flops 1048584 | bytes 3146087 | solution.py:22
  116.3 1.5 fusion.45
  117.8 1.5 fusion.45
  119.4 1.5 fusion.45
  120.9 1.5 fusion.45
  122.9 1.4 fusion.12
  124.6 5.9 %all-reduce = f32[64]{0:T(128)S(1)} all-reduce(f32[64]{0:T(128)S(1)} %dynamic-update-slice), channel_id=4, replica_groups=mesh['dp'=8,'ctx'=4] {'ctx'}, use_global_device_ids=true, to_apply=%add | all-reduce | flops 64 | bytes 512
  131.7 1.2 copy.69
  132.9 40.5 %psum.7 = f32[16,128]{1,0:T(8,128)S(1)} all-reduce(f32[16,128]{1,0:T(8,128)S(1)} %get-tuple-element.444), channel_id=1, replica_groups=mesh['dp'=8,'ctx'=4] {'dp','ctx'}, use_global_device_ids=true, to_apply=%region_13.14 | all-reduce | flops 2048 | bytes 16384 | tf_op jit(solution)/shard_map/psum | solution.py:120
  (68 shorter events, 8.6 us)
Async XLA Ops:
  7.2 36.2 %copy-start = (bf16[1,128,16,128]{3,2,1,0:T(8,128)(2,1)S(1)}, bf16[1,128,16,128]{3,2,1,0:T(8,128)(2,1)}, u32[]{:S(2)}) copy-start(bf16[1,128,16,128]{3,2,1,0:T(8,128)(2,1)} %param.14) | copy-start | bytes 1572868
  7.2 37.5 %copy-start.6 = (bf16[1,128,16,128]{3,2,1,0:T(8,128)(2,1)S(1)}, bf16[1,128,16,128]{3,2,1,0:T(8,128)(2,1)}, u32[]{:S(2)}) copy-start(bf16[1,128,16,128]{3,2,1,0:T(8,128)(2,1)} %param.12) | copy-start | bytes 1572868
  7.2 38.1 %copy-start.4 = (bf16[1,128,16,128]{3,2,1,0:T(8,128)(2,1)S(1)}, bf16[1,128,16,128]{3,2,1,0:T(8,128)(2,1)}, u32[]{:S(2)}) copy-start(bf16[1,128,16,128]{3,2,1,0:T(8,128)(2,1)} %param.15) | copy-start | bytes 1572868
  7.2 73.0 %all-gather.7.cloned.1.call-start = ((), (), s32[]{:S(2)}) async-start(), calls=%async_computation | async-start | bytes 5242880 | tf_op jit(solution)/shard_map/all_gather | solution.py:9
  42.3 4.6 %copy-start.7 = (u32[32]{0:T(128)S(1)}, u32[32]{0:T(128)}, u32[]{:S(2)}) copy-start(u32[32]{0:T(128)} %constant.145) | copy-start | bytes 388
  44.7 71.6 %all-gather.9.cloned.1.call-start = ((), (), s32[]{:S(2)}) async-start(), calls=%async_computation.1 | async-start | bytes 5242880 | tf_op jit(solution)/shard_map/all_gather | solution.py:9
  45.2 1.5 copy-start.1
  54.9 0.8 copy-start.5
  116.3 6.6 %copy-start.2 = (bf16[1,128,16,128]{1,3,2,0:T(8,128)(2,1)S(1)}, bf16[1,128,16,128]{1,3,2,0:T(8,128)(2,1)}, u32[]{:S(2)}) copy-start(bf16[1,128,16,128]{1,3,2,0:T(8,128)(2,1)} %copy-done.1) | copy-start | bytes 1572868
  122.3 51.0 %copy-start.3 = (bf16[1,128,16,128]{1,3,2,0:T(8,128)(2,1)S(1)}, bf16[1,128,16,128]{1,3,2,0:T(8,128)(2,1)}, u32[]{:S(2)}) copy-start(bf16[1,128,16,128]{1,3,2,0:T(8,128)(2,1)} %get-tuple-element.437) | copy-start | bytes 1572868
Sparse Core Ops, SparseCore 0:
  44.8 35.3 all-gather.6
  81.8 34.4 all-gather.8
where the time goes:
time: 183 us; the launch traced here: 182 us
  blocking collectives  83.6 us (46%)
  waiting for transfers between devices  50.2 us (27%)
  between operations  14.9 us (8%)
  other arithmetic  14 us (8%)
  matrix products  10.6 us (6%)
  local copies, waits for them, and re-layouts  8.38 us (5%)
    all_gather x2, waiting for transfers between devices, carried_in(): everything = jax.tree.map(lambda part: lax.all_gather(part, axis), shard)  50.2 us
    psum x1, blocking collectives, per_device(): summed = lax.psum(term, ('dp', 'ctx'))  40.5 us
    all_gather x1, blocking collectives, per_device(): gate_full = lax.all_gather(gate_weight, 'dp', axis=1, tiled=True)  32.2 us
    select_n x12, other arithmetic, hop(): return jax.tree.map(lambda a, b: jnp.where(reached, a, b), new, before)  11.8 us
    unnamed x24, local copies, waits for them, and re-layouts  6.86 us
    unnamed x1, blocking collectives  5.87 us
    all_gather x1, blocking collectives, carried_in(): everything = jax.tree.map(lambda part: lax.all_gather(part, axis), shard)  5.04 us
  transfers between devices with their start and end apart: 2, of which 2 were waited for; matrix products, arithmetic and copies ran while one was open for 8% of the time, Pallas kernels for 0%

commit v1 on v0

v1 whole, which is shorter than its diff:
```python
import functools

import jax
import jax.numpy as jnp
from jax import lax
from jax.experimental import pallas as pl
from jax.experimental.pallas import tpu as pltpu
from jax.sharding import PartitionSpec as P

F32 = jnp.float32
BF16 = jnp.bfloat16
VMEM = pl.BlockSpec(memory_space=pltpu.VMEM)
ANY = pl.BlockSpec(memory_space=pl.ANY)
LIMIT = 24 * 1024 * 1024


def nn(a, b):
    return lax.dot_general(a, b, (((1,), (0,)), ((), ())), preferred_element_type=F32)


def nt(a, b):
    return lax.dot_general(a, b, (((1,), (1,)), ((), ())), preferred_element_type=F32)


def place():
    mine = lax.axis_index("ctx")
    return lax.rem(mine, 2), lax.div(mine, 2)


def hi_lo(rows):
    hi = rows.astype(BF16)
    return hi, (rows - hi.astype(F32)).astype(BF16)


def params(**more):
    return pltpu.CompilerParams(vmem_limit_bytes=LIMIT, **more)


def split_kernel(k_ref, q_ref, v_ref, g_ref, keep_ref, send_ref, tmp):
    par, _ = place()
    _, count, heads, width = k_ref.shape
    half = heads // 2
    for at, ref in enumerate((k_ref, q_ref, v_ref, g_ref)):
        tmp[...] = ref[0].astype(F32).reshape(count * heads, width)
        for j in range(half):
            for out, base in ((keep_ref, par * half), (send_ref, (1 - par) * half)):
                plane = tmp[pl.ds(base + j, count, stride=heads), :]
                if at < 2:
                    plane = plane.T
                out[at, j] = plane.astype(BF16)


def load_both(keep_ref, recv_ref, buf, sems, par):
    copies = []
    for at in range(4):
        pair = (
            pltpu.make_async_copy(keep_ref.at[at], buf.at[par, at], sems.at[0, at]),
            pltpu.make_async_copy(recv_ref.at[at], buf.at[1 - par, at], sems.at[1, at]),
        )
        for copy in pair:
            copy.start()
        copies.append(pair)
    return copies


def scales(rows):
    end = jnp.broadcast_to(rows[:, -1:], rows.shape)
    return jnp.exp(end - rows), jnp.exp(rows), jnp.exp(end)


def state(buf, scale_ref, side, block, j):
    half = buf.shape[2]
    scaled = buf[block, side, j].astype(F32) * scale_ref[side, pl.ds(block * half + j, 1), :]
    return nn(scaled.astype(BF16), buf[block, 2 + side, j])


def gate_kernel(direct, pair, *refs):
    if direct:
        mine_ref, other_ref = refs[:2]
        refs = refs[2:]
    else:
        full_ref = refs[0]
        refs = refs[1:]
    bias_ref, keep_ref, recv_ref, total_ref, near_ref, rows_ref, gate_ref, buf, scale_ref, sems = refs
    par, chip = place()
    half, width, count = buf.shape[2:]
    copies = load_both(keep_ref, recv_ref, buf, sems, par)
    if direct:
        index = lax.axis_index("dp")
        pieces, _, piece = mine_ref.shape
        sub = lax.broadcasted_iota(jnp.int32, (piece, width), 0)
        lane = lax.broadcasted_iota(jnp.int32, (piece, width), 1)
        full = jnp.zeros((2 * half, width), F32)
        for ref, low in ((mine_ref, par), (other_ref, 1 - par)):
            for k in range(pieces):
                owner = jnp.bitwise_xor(index, 2 * k + low)
                pick = jnp.where(lane == sub + owner * piece, 1.0, 0.0).astype(BF16)
                full = full + nn(ref[k], pick)
    else:
        full = full_ref[...].astype(F32)
    gate_ref[...] = full
    weights = gate_ref[pl.ds(par * half, half), :].astype(BF16)
    bias = bias_ref[pl.ds(par * half, half), :]
    row = lax.broadcasted_iota(jnp.int32, (half, count), 0)
    for copy in copies[0]:
        copy.wait()
    logits = []
    for block in range(2):
        logit = bias
        for j in range(half):
            logit = logit + jnp.where(row == j, nn(weights, buf[block, 0, j]), 0.0)
        logits.append(logit)
    logit = jnp.concatenate(logits, 0)
    decay = -(jnp.maximum(logit, 0.0) + jnp.log1p(jnp.exp(-jnp.abs(logit))))
    until = lax.broadcasted_iota(jnp.int32, (count, count), 0) <= lax.broadcasted_iota(jnp.int32, (count, count), 1)
    cumul = lax.dot_general(
        decay,
        jnp.where(until, 1.0, 0.0),
        (((1,), (0,)), ((), ())),
        precision=lax.Precision.HIGHEST,
        preferred_element_type=F32,
    )
    rows_ref[0] = cumul
    rows_ref[1] = -1.0 / (1.0 + jnp.exp(-logit))
    tail, head, ends = scales(cumul)
    scale_ref[0] = tail
    scale_ref[1] = head
    scale_ref[2] = ends
    for at in (1, 2, 3):
        for copy in copies[at]:
            copy.wait()
    for at, side in enumerate((chip,) if pair else (0, 1)):
        for j in range(half):
            near = state(buf, scale_ref, side, side, j)
            last = state(buf, scale_ref, side, 1 - side, j)
            passed = scale_ref[2, pl.ds((1 - side) * half + j, 1), :] * near + last
            total_ref[at, j] = passed.astype(total_ref.dtype)
            near_ref[at, j] = near.astype(near_ref.dtype)


def put(out, buf, mine_ref, send_ref, at, side, rel, block, j, full):
    rounded = full.astype(BF16)
    (mine_ref if rel == 0 else send_ref)[at, j] = rounded.astype(F32).T.astype(BF16)
    sign = jnp.where(side == 0, 1.0, -1.0)
    out.append(sign * jnp.sum(buf[block, 1 - side, j].astype(F32) * full, 0, keepdims=True))


def weighted_keys(buf, block, rows):
    half = buf.shape[2]
    lhs = jnp.concatenate(hi_lo(rows), 0)
    row = lax.broadcasted_iota(jnp.int32, lhs.shape, 0)
    total = jnp.zeros(lhs.shape, F32)
    for j in range(half):
        total = total + jnp.where((row == j) | (row == j + half), nt(lhs, buf[block, 0, j]), 0.0)
    return total[:half] + total[half:]


def inside_kernel(pair, keep_ref, recv_ref, rows_ref, near_ref, *refs):
    if pair:
        attn_ref, kappa_ref, other_ref, mine_ref, send_ref, dg_ref, buf, scale_ref, sems = refs
    else:
        attn_ref, kappa_ref, buf, scale_ref, sems = refs
    par, chip = place()
    half, width, count = buf.shape[2:]
    const = 1.0 / width
    copies = load_both(keep_ref, recv_ref, buf, sems, par)
    cumul = rows_ref[0]
    columns = cumul.T
    tail, head, ends = scales(cumul)
    scale_ref[0] = tail
    scale_ref[1] = head
    causal = lax.broadcasted_iota(jnp.int32, (count, count), 0) >= lax.broadcasted_iota(jnp.int32, (count, count), 1)
    for loaded in copies:
        for copy in loaded:
            copy.wait()
    kappa = jnp.zeros((half, width), F32)
    for block in range(2):
        kappa = kappa + weighted_keys(buf, block, rows_ref[1, pl.ds(block * half, half), :])
    kappa_ref[...] = kappa
    if pair:
        side = chip
        for j in range(half):
            other_ref[j] = state(buf, scale_ref, 1 - side, 1 - side, j)
    sums = [[], []]
    for rel in range(2):
        block = par if rel == 0 else 1 - par
        for j in range(half):
            at = pl.ds(block * half + j, 1)
            line = rows_ref[0, at, :]
            column = jnp.where(par == rel, columns[:, j : j + 1], columns[:, half + j : half + j + 1])
            decay = jnp.exp(jnp.where(causal, column - line, -1e30))
            weight = (const * nt(buf[block, 3, j], buf[block, 2, j]) * decay).astype(BF16)
            query = nt(buf[block, 0, j], weight)
            key = nn(buf[block, 1, j], weight)
            if pair:
                known = jnp.where(side == 0, query, key)
                attn_ref[0, rel, j] = jnp.where(side == 0, key, query)
                cross = nt(near_ref[0, j], buf[block, 3 - side, j])
                factor = jnp.where(block == side, 0.0, const) * scale_ref[1 - side, at, :]
                put(sums[rel], buf, mine_ref, send_ref, 0, side, rel, block, j, known + factor * cross)
            else:
                attn_ref[0, rel, j] = query
                attn_ref[1, rel, j] = key
    if pair:
        for rel in range(2):
            dg_ref[rel] = jnp.concatenate(sums[rel], 0)
            send_rows = jnp.concatenate(
                hi_lo(rows_ref[1, pl.ds((1 - par) * half, half), :]), 0
            )
        send_ref[0, half, : 2 * half] = send_rows


def outside_kernel(pair, keep_ref, recv_ref, rows_ref, state_ref, near_ref, attn_ref, kappa_ref, *refs):
    if pair:
        dg_ref, mine_ref, send_ref, suffix_ref, pieces_ref, buf, scale_ref, sems = refs
    else:
        mine_ref, send_ref, suffix_ref, pieces_ref, buf, scale_ref, sems = refs
    par, chip = place()
    half, width, count = buf.shape[2:]
    const = 1.0 / width
    copies = load_both(keep_ref, recv_ref, buf, sems, par)
    cumul = rows_ref[0]
    tail, head, ends = scales(cumul)
    scale_ref[0] = tail
    scale_ref[1] = head
    scale_ref[2] = ends
    for loaded in copies:
        for copy in loaded:
            copy.wait()
    if pair:
        slopes = [dg_ref[0], dg_ref[1]]
        sides = (1 - chip,)
    else:
        slopes = [jnp.zeros((half, count), F32)] * 2
        sides = (0, 1)
    for rel in range(2):
        block = par if rel == 0 else 1 - par
        for at, side in enumerate(sides):
            sums = []
            for j in range(half):
                entry = block == side
                come = state_ref[at, j].astype(F32)
                ratio = jnp.where(entry, 1.0, scale_ref[2, pl.ds(side * half + j, 1), :])
                near = near_ref[j] if pair else near_ref[at, j]
                known = (ratio * come + jnp.where(entry, 0.0, 1.0) * near).astype(BF16)
                cross = nt(known, buf[block, 3 - side, j])
                factor = const * scale_ref[1 - side, pl.ds(block * half + j, 1), :]
                full = attn_ref[at, rel, j] + factor * cross
                put(sums, buf, mine_ref, send_ref, at, side, rel, block, j, full)
            slopes[rel] = slopes[rel] + jnp.concatenate(sums, 0)
    slope = jnp.concatenate(slopes, 0)
    later = lax.broadcasted_iota(jnp.int32, (count, count), 0) >= lax.broadcasted_iota(jnp.int32, (count, count), 1)
    suffix = lax.dot_general(
        slope,
        jnp.where(later, 1.0, 0.0),
        (((1,), (0,)), ((), ())),
        precision=lax.Precision.HIGHEST,
        preferred_element_type=F32,
    )
    sums = jnp.broadcast_to(suffix[:, :1], suffix.shape)
    first = (par == 0).astype(F32)
    mine = suffix[:half] + first * sums[half:]
    other = suffix[half:] + (1.0 - first) * sums[:half]
    suffix_ref[0] = mine
    suffix_ref[1] = rows_ref[1, pl.ds(par * half, half), :]
    last = send_ref.shape[0] - 1
    send_ref[last, half, : 2 * half] = jnp.concatenate(hi_lo(other), 0)
    if not pair:
        send_ref[0, half, : 2 * half] = jnp.concatenate(
            hi_lo(rows_ref[1, pl.ds((1 - par) * half, half), :]), 0
        )
    partial = weighted_keys(buf, par, mine * rows_ref[1, pl.ds(par * half, half), :])
    partial = partial + weighted_keys(buf, 1 - par, other * rows_ref[1, pl.ds((1 - par) * half, half), :])
    kappa = kappa_ref[...]
    total = sums[:half] + sums[half:]
    parts = lax.axis_size("dp")
    copies_of = pieces_ref.shape[0] // parts
    piece = width // parts
    lane = lax.broadcasted_iota(jnp.int32, (half, width), 1)
    for i in range(parts):
        gates = partial if i == 0 else pltpu.roll(partial, width - i * piece, 1)
        shift = (width - i * piece + piece) % width
        slopes_of = kappa if shift == 0 else pltpu.roll(kappa, shift, 1)
        sent = jnp.where(lane < piece, gates, jnp.where(lane < 2 * piece, slopes_of, total))
        pieces_ref[pl.ds(i * copies_of, copies_of)] = jnp.broadcast_to(sent[None], (copies_of, half, width))


def last_kernel(pair, mine_refs, recv_refs, suffix_ref, pieces_ref, gate_ref, refs):
    query_ref, key_ref, grad_ref, buf, tmp, line_ref, sems = refs
    par, chip = place()
    index = lax.axis_index("dp")
    half = suffix_ref.shape[1]
    _, count, heads, width = query_ref.shape
    parts, ranks = lax.axis_size("dp"), lax.axis_size("ctx")
    piece = width // parts

    def copies(side):
        local = pair and (lambda source: source)
        del local
        return None

    def start(side, source_mine, source_recv):
        pltpu.make_async_copy(source_mine, buf.at[side, par, pl.ds(0, half)], sems.at[side, 0]).start()
        pltpu.make_async_copy(source_recv, buf.at[side, 1 - par], sems.at[side, 1]).start()

    if pair:
        for side in range(2):

            @pl.when(chip == side)
            def _(side=side):
                start(side, mine_refs[0].at[0], recv_refs[0].at[0])

            @pl.when(chip != side)
            def _(side=side):
                start(side, mine_refs[1].at[0], recv_refs[1].at[0])
    else:
        for side in range(2):
            start(side, mine_refs[0].at[side], recv_refs[0].at[side])

    def wait(side):
        source_mine = mine_refs[0].at[0]
        source_recv = recv_refs[0].at[0]
        pltpu.make_async_copy(source_mine, buf.at[side, par, pl.ds(0, half)], sems.at[side, 0]).wait()
        pltpu.make_async_copy(source_recv, buf.at[side, 1 - par], sems.at[side, 1]).wait()

    groups = ranks // 2
    total = jnp.zeros((2, half, width), F32)
    everything = pieces_ref[...].reshape(parts, groups, 2, half, width)
    after = jnp.zeros((parts, 2, half, 1), F32)
    for m in reversed(range(groups)):
        got = everything[:, m]
        slopes = pltpu.roll(got.reshape(parts * 2 * half, width), width - piece, 1).reshape(got.shape)
        total = total + jnp.sum(got + slopes * after, 0)
        after = after + got[..., 2 * piece : 2 * piece + 1]
    grad_ref[...] = total.reshape(heads, width)[:, :piece]

    own = pieces_ref[pl.ds(index * ranks, ranks)].reshape(groups, 2, half, width)
    beyond = jnp.zeros((2, half, 1), F32)
    for m in range(groups):
        beyond = beyond + jnp.where(m > chip, 1.0, 0.0) * own[m, :, :, 2 * piece : 2 * piece + 1]

    wait(0)
    wait(1)
    for side, ref in ((0, query_ref), (1, key_ref)):
        if side == 1:
            local, remote = (chip, 1 - chip) if pair else (0, 1)
            slope_rows = buf[local, 1 - par, half, : 2 * half].astype(F32)
            suffix_rows = buf[remote, 1 - par, half, : 2 * half].astype(F32)
            line_ref[0, pl.ds(par * half, half), :] = suffix_ref[0]
            line_ref[0, pl.ds((1 - par) * half, half), :] = suffix_rows[:half] + suffix_rows[half:]
            line_ref[1, pl.ds(par * half, half), :] = suffix_ref[1]
            line_ref[1, pl.ds((1 - par) * half, half), :] = slope_rows[:half] + slope_rows[half:]
            slope = line_ref[1] * (line_ref[0] + beyond.reshape(heads, 1))
            columns = slope.T
        for h in range(heads):
            plane = buf[side, h // half, h % half].astype(F32)
            if side == 1:
                plane = plane + columns[:, h : h + 1] * gate_ref[h : h + 1, :]
            tmp[side, pl.ds(h, count, stride=heads), :] = plane
        ref[0] = tmp[side].reshape(count, heads, width).astype(BF16)


def across_chips(total, ends, ranks, reverse):
    step = -1 if reverse else 1

    def shift(value, chips):
        hops = [(i, i + 2 * chips * step) for i in range(ranks) if 0 <= i + 2 * chips * step < ranks]
        return lax.ppermute(value, "ctx", hops)

    value, factor = shift(total, 1), shift(ends, 1)
    reach = 1
    while 2 * reach < ranks:
        value = value + factor * shift(value, reach)
        factor = factor * shift(factor, reach)
        reach *= 2
    return value


def per_device(mesh, queries, keys, values, out_grad, gate_weight, head_bias):
    _, count, heads, width = queries.shape
    parts, ranks = mesh.shape["dp"], mesh.shape["ctx"]
    half = heads // 2
    pair = ranks == 4
    direct = parts == 8
    swap = [(i, i ^ 1) for i in range(ranks)]
    plane = (half, width, count)

    if direct:
        got = []
        for k in range(parts // 2):
            hops = [
                (d * ranks + c, (d ^ (2 * k + c % 2)) * ranks + c)
                for d in range(parts)
                for c in range(ranks)
            ]
            got.append(lax.ppermute(gate_weight, ("dp", "ctx"), hops))
        mine_gate = jnp.stack(got)
        gates = (mine_gate, lax.ppermute(mine_gate, "ctx", swap))
    else:
        gates = (lax.all_gather(gate_weight, "dp", axis=1, tiled=True),)
    bias = jnp.broadcast_to(head_bias.astype(F32)[:, None], (heads, count))

    quad = jax.ShapeDtypeStruct((4, *plane), BF16)
    keep, send = pl.pallas_call(
        split_kernel,
        out_shape=(quad, quad),
        in_specs=[VMEM] * 4,
        out_specs=(VMEM, VMEM),
        scratch_shapes=[pltpu.VMEM((count * heads, width), F32)],
        compiler_params=params(),
        name="split_heads",
    )(keys, queries, values, out_grad)
    recv = lax.ppermute(send, "ctx", swap)

    buffers = [
        pltpu.VMEM((2, 4, *plane), BF16),
        pltpu.VMEM((3, heads, count), F32),
        pltpu.SemaphoreType.DMA((2, 4)),
    ]
    sides = 1 if pair else 2
    square = (half, width, width)
    total, near, rows, gate_full = pl.pallas_call(
        functools.partial(gate_kernel, direct, pair),
        out_shape=(
            jax.ShapeDtypeStruct((sides, *square), BF16 if pair else F32),
            jax.ShapeDtypeStruct((sides, *square), BF16 if pair else F32),
            jax.ShapeDtypeStruct((2, heads, count), F32),
            jax.ShapeDtypeStruct((heads, width), F32),
        ),
        in_specs=[VMEM] * (len(gates) + 1) + [ANY, ANY],
        out_specs=(VMEM,) * 4,
        scratch_shapes=buffers,
        compiler_params=params(),
        name="gate_states",
    )(*gates, bias, keep, recv)

    attn_shape = jax.ShapeDtypeStruct((sides, 2, *plane), F32)
    kappa_shape = jax.ShapeDtypeStruct((half, width), F32)
    mine_shape = jax.ShapeDtypeStruct((sides, half, count, width), BF16)
    send_shape = jax.ShapeDtypeStruct((sides, half + 1, count, width), BF16)
    slope_shape = jax.ShapeDtypeStruct((2, half, count), F32)
    pieces_shape = jax.ShapeDtypeStruct((parts * ranks, half, width), F32)
    inside = pl.pallas_call(
        functools.partial(inside_kernel, pair),
        out_shape=(attn_shape, kappa_shape)
        + ((jax.ShapeDtypeStruct(square, F32), mine_shape, send_shape, slope_shape) if pair else ()),
        in_specs=[ANY, ANY, VMEM, VMEM],
        out_specs=(VMEM,) * (6 if pair else 2),
        scratch_shapes=buffers,
        compiler_params=params(),
        name="inside_block",
    )
    if pair:
        states = lax.ppermute(total, "ctx", [(i, i ^ 2) for i in range(ranks)])
        attn, kappa, near, mine_local, send_local, slopes = inside(keep, recv, rows, near)
        recv_local = lax.ppermute(send_local, "ctx", swap)
        extra = (slopes,)
    else:
        ends = jnp.exp(rows[0, :half, -1] + rows[0, half:, -1])[:, None, None]
        states = jnp.stack(
            [across_chips(total[0], ends, ranks, False), across_chips(total[1], ends, ranks, True)]
        )
        attn, kappa = inside(keep, recv, rows, near)
        extra = ()
    mine, send, suffix, pieces = pl.pallas_call(
        functools.partial(outside_kernel, pair),
        out_shape=(mine_shape, send_shape, slope_shape, pieces_shape),
        in_specs=[ANY, ANY] + [VMEM] * (5 + len(extra)),
        out_specs=(VMEM,) * 4,
        scratch_shapes=buffers,
        compiler_params=params(),
        name="outside_block",
    )(keep, recv, rows, states, near, attn, kappa, *extra)
    recv_out = lax.ppermute(send, "ctx", swap)
    pieces = lax.all_to_all(pieces, ("dp", "ctx"), 0, 0, tiled=True)

    mines = (mine_local, mine) if pair else (mine,)
    recvs = (recv_local, recv_out) if pair else (recv_out,)

    def last(*refs):
        n = len(mines)
        last_kernel(pair, refs[:n], refs[n : 2 * n], *refs[2 * n : 2 * n + 3], refs[2 * n + 3 :])

    piece = width // parts
    return pl.pallas_call(
        last,
        out_shape=(
            jax.ShapeDtypeStruct((1, count, heads, width), BF16),
            jax.ShapeDtypeStruct((1, count, heads, width), BF16),
            jax.ShapeDtypeStruct((heads, piece), F32),
        ),
        in_specs=[ANY] * (2 * len(mines)) + [VMEM] * 3,
        out_specs=(VMEM,) * 3,
        scratch_shapes=[
            pltpu.VMEM((2, 2, half + 1, count, width), BF16),
            pltpu.VMEM((2, count * heads, width), F32),
            pltpu.VMEM((2, heads, count), F32),
            pltpu.SemaphoreType.DMA((2, 2)),
        ],
        compiler_params=params(),
        name="last",
    )(*mines, *recvs, suffix, pieces, gate_full)


def solution(mesh):
    return jax.shard_map(
        functools.partial(per_device, mesh),
        mesh=mesh,
        in_specs=(
            P("dp", "ctx", None, None),
            P("dp", "ctx", None, None),
            P("dp", "ctx", None, None),
            P("dp", "ctx", None, None),
            P(None, "dp"),
            P(),
        ),
        out_specs=(P("dp", "ctx", None, None), P("dp", "ctx", None, None), P(None, "dp")),
        check_vma=False,
    )
```

time: 183 us -> 48.6 us (0.27)
  blocking collectives: 83.6 us -> 0 us
  waiting for transfers between devices: 50.2 us -> 16.3 us
  between operations: 14.9 us -> 0.71 us
  starting transfers between devices: 0.08 us -> 14.1 us
  other arithmetic: 14 us -> 0.01 us
  Pallas kernels: 0 us -> 12.9 us
  matrix products: 10.6 us -> 0 us
  local copies, waits for them, and re-layouts: 8.38 us -> 4.24 us
    all_gather x2 -> x0, waiting for transfers between devices: 50.2 us -> none  [carried_in(): everything = jax.tree.map(lambda part: lax.all_gather(part, axis), shard)]
    psum x1 -> x0, blocking collectives: 40.5 us -> none  [per_device(): summed = lax.psum(term, ('dp', 'ctx'))]
    all_gather x2 -> x0, blocking collectives: 37.2 us -> none  [the longest x1 32.2 us: per_device(): gate_full = lax.all_gather(gate_weight, 'dp', axis=1, tiled=True)]
    pallas_call x0 -> x5, Pallas kernels: none -> 12.9 us  [the longest x1 4.01 us: per_device(): inside(keep, recv, rows, near)]
    select_n x12 -> x0, other arithmetic: 11.8 us -> none  [hop(): return jax.tree.map(lambda a, b: jnp.where(reached, a, b), new, before)]
    ppermute x0 -> x9, starting transfers between devices: none -> 11.4 us  [the longest x4 6.05 us: per_device(): got.append(lax.ppermute(gate_weight, ('dp', 'ctx'), hops))]
    dot_general x7 -> x0, matrix products: 10.6 us -> none  [the longest x1 2.94 us: block_grads(): jnp.einsum('the,hde->thd', grads_block, in_round, preferred_element_type=...]
    all_to_all x0 -> x1, waiting for transfers between devices: none -> 8.22 us  [per_device(): pieces = lax.all_to_all(pieces, ('dp', 'ctx'), 0, 0, tiled=True)]
  transfers between devices with their start and end apart: 2 -> 10, of which waited for: 2 -> 5; matrix products, arithmetic and copies ran while one was open for 8% -> 0% of each run, Pallas kernels for 0% -> 13%
where the time goes in v1:
time: 48.6 us; the launch traced here: 48.3 us
  waiting for transfers between devices  16.3 us (34%)
  starting transfers between devices  14.1 us (29%)
  Pallas kernels  12.9 us (27%)
  local copies, waits for them, and re-layouts  4.24 us (9%)
  between operations  0.71 us (1%)
    all_to_all x1, waiting for transfers between devices, per_device(): pieces = lax.all_to_all(pieces, ('dp', 'ctx'), 0, 0, tiled=True)  8.22 us
    ppermute x4, starting transfers between devices, per_device(): got.append(lax.ppermute(gate_weight, ('dp', 'ctx'), hops))  6.05 us
    ppermute x4, waiting for transfers between devices, per_device(): got.append(lax.ppermute(gate_weight, ('dp', 'ctx'), hops))  4.31 us
    unnamed x12, local copies, waits for them, and re-layouts  4.17 us
    pallas_call x1, Pallas kernels, per_device(): inside(keep, recv, rows, near)  4.01 us
    ppermute x1, starting transfers between devices, per_device(): gates = (mine_gate, lax.ppermute(mine_gate, 'ctx', swap))  3.06 us
    ppermute x1, waiting for transfers between devices, per_device(): states = lax.ppermute(total, 'ctx', [(i, i ^ 2) for i in range(ranks)])  2.92 us
    pallas_call x1, Pallas kernels, per_device(): pl.pallas_call(split_kernel, out_shape=(quad, quad), in_specs=[VMEM] * 4,...  2.91 us
  transfers between devices with their start and end apart: 10, of which 5 were waited for; matrix products, arithmetic and copies ran while one was open for 0% of the time, Pallas kernels for 13%

profile of v1, /device:TPU:0, one launch (start us, length us, event | category | flops | bytes accessed | tf_op | source)
XLA Modules:
  0.0 48.3 jit_solution(16364406275032673664)
XLA Ops:
  0.6 1.0 %copy-done = bf16[1,128,16,128]{3,2,1,0:T(8,128)(2,1)S(1)} copy-done((bf16[1,128,16,128]{3,2,1,0:T(8,128)(2,1)S(1)}, bf16[1,128,16,128]{3,2,1,0:T(8,128)(2,1)}, u32[]{:S(2)}) %copy-start) | copy-done | bytes 524312
  1.7 1.0 %copy-done.1 = bf16[1,128,16,128]{3,2,1,0:T(8,128)(2,1)S(1)} copy-done((bf16[1,128,16,128]{3,2,1,0:T(8,128)(2,1)S(1)}, bf16[1,128,16,128]{3,2,1,0:T(8,128)(2,1)}, u32[]{:S(2)}) %copy-start.1) | copy-done | bytes 524312
  2.7 1.0 %copy-done.2 = bf16[1,128,16,128]{3,2,1,0:T(8,128)(2,1)S(1)} copy-done((bf16[1,128,16,128]{3,2,1,0:T(8,128)(2,1)S(1)}, bf16[1,128,16,128]{3,2,1,0:T(8,128)(2,1)}, u32[]{:S(2)}) %copy-start.2) | copy-done | bytes 524312
  3.8 1.0 %copy-done.3 = bf16[1,128,16,128]{3,2,1,0:T(8,128)(2,1)S(1)} copy-done((bf16[1,128,16,128]{3,2,1,0:T(8,128)(2,1)S(1)}, bf16[1,128,16,128]{3,2,1,0:T(8,128)(2,1)}, u32[]{:S(2)}) %copy-start.3) | copy-done | bytes 524312
  4.8 2.9 %split_heads.1 = (bf16[4,8,128,128]{3,2,1,0:T(8,128)(2,1)S(1)}, bf16[4,8,128,128]{3,2,1,0:T(8,128)(2,1)S(1)}) custom-call(bf16[1,128,16,128]{3,2,1,0:T(8,128)(2,1)S(1)} %copy-done, bf16[1,128,16,128]{3,2,1,0:T(8,128)(2,1)S(1)} %copy-done.1, bf16[1,128,16,128]{3,2,1,0:T(8,128)(2,1)S(1)} %copy-done.2, bf16[1,128,16,128]{3,2,1,0:T(8,128)(2,1)S(1)} %copy-done.3), custom_call_target="tpu_custom_call" | custom-call | tf_op jit(solution)/shard_map/split_heads/pallas_call | solution.py:404
  7.7 0.5 %collective-permute-start = (bf16[4,8,128,128]{3,2,1,0:T(8,128)(2,1)S(1)}, bf16[4,8,128,128]{3,2,1,0:T(8,128)(2,1)S(1)}, u32[]{:S(2)}, u32[]{:S(2)}) collective-permute-start(bf16[4,8,128,128]{3,2,1,0:T(8,128)(2,1)S(1)} %get-tuple-element.20), channel_id=1, source_target_pairs={{0,1},{1,0},{2,3},{3,2},{4,5},{5,4},{6,7},{7,6},{8,9},{9,8},{10,11... | collective-permute-start | bytes 3145736 | tf_op jit(solution)/shard_map/ppermute | solution.py:413
  8.2 2.7 %collective-permute-start.2 = (bf16[16,16]{1,0:T(8,128)(2,1)S(1)}, bf16[16,16]{1,0:T(8,128)(2,1)S(1)}, u32[]{:S(2)}, u32[]{:S(2)}) collective-permute-start(bf16[16,16]{1,0:T(8,128)(2,1)S(1)} %copy-done.5), channel_id=1, source_target_pairs={{0,8},{1,13},{2,10},{3,15},{4,12},{5,9},{6,14},{7,11},{8,0},{9,5},... | collective-permute-start | bytes 1544 | tf_op jit(solution)/shard_map/ppermute | solution.py:396
  10.9 0.6 %collective-permute-start.1 = (bf16[16,16]{1,0:T(8,128)(2,1)S(1)}, bf16[16,16]{1,0:T(8,128)(2,1)S(1)}, u32[]{:S(2)}, u32[]{:S(2)}) collective-permute-start(bf16[16,16]{1,0:T(8,128)(2,1)S(1)} %copy-done.5), channel_id=1, source_target_pairs={{0,0},{1,5},{2,2},{3,7},{4,4},{5,1},{6,6},{7,3},{8,8},{9,13},{10,1... | collective-permute-start | bytes 1544 | tf_op jit(solution)/shard_map/ppermute | solution.py:396
  11.6 2.5 %collective-permute-start.4 = (bf16[16,16]{1,0:T(8,128)(2,1)S(1)}, bf16[16,16]{1,0:T(8,128)(2,1)S(1)}, u32[]{:S(2)}, u32[]{:S(2)}) collective-permute-start(bf16[16,16]{1,0:T(8,128)(2,1)S(1)} %copy-done.5), channel_id=1, source_target_pairs={{0,24},{1,29},{2,26},{3,31},{4,28},{5,25},{6,30},{7,27},{8,16},{9,... | collective-permute-start | bytes 1544 | tf_op jit(solution)/shard_map/ppermute | solution.py:396
  14.1 0.2 collective-permute-start.3
  14.3 2.7 %collective-permute-done.4 = bf16[16,16]{1,0:T(8,128)(2,1)S(1)} collective-permute-done((bf16[16,16]{1,0:T(8,128)(2,1)S(1)}, bf16[16,16]{1,0:T(8,128)(2,1)S(1)}, u32[]{:S(2)}, u32[]{:S(2)}) %collective-permute-start.4) | collective-permute-done | bytes 544 | tf_op jit(solution)/shard_map/ppermute | solution.py:396
  17.0 1.6 %collective-permute-done.3 = bf16[16,16]{1,0:T(8,128)(2,1)S(1)} collective-permute-done((bf16[16,16]{1,0:T(8,128)(2,1)S(1)}, bf16[16,16]{1,0:T(8,128)(2,1)S(1)}, u32[]{:S(2)}, u32[]{:S(2)}) %collective-permute-start.3) | collective-permute-done | bytes 544 | tf_op jit(solution)/shard_map/ppermute | solution.py:396
  18.6 3.1 %collective-permute-start.5 = (bf16[4,16,16]{2,1,0:T(8,128)(2,1)S(1)}, bf16[4,16,16]{2,1,0:T(8,128)(2,1)S(1)}, u32[]{:S(2)}, u32[]{:S(2)}) collective-permute-start(bf16[4,16,16]{2,1,0:T(8,128)(2,1)S(1)} %pad_maximum_fusion.refs_0_), channel_id=1, source_target_pairs={{0,1},{1,0},{2,3},{3,2},{4,5},{5,4},{6,7},{7,6},{8,9},{9,8},{10,11... | collective-permute-start | bytes 6152 | tf_op jit(solution)/shard_map/ppermute | solution.py:398
  21.7 0.8 %collective-permute-done.5.refs_1_ = bf16[4,16,16]{2,1,0:T(8,128)(2,1)S(1)} collective-permute-done((bf16[4,16,16]{2,1,0:T(8,128)(2,1)S(1)}, bf16[4,16,16]{2,1,0:T(8,128)(2,1)S(1)}, u32[]{:S(2)}, u32[]{:S(2)}) %collective-permute-start.5) | collective-permute-done | bytes 2080 | tf_op jit(solution)/shard_map/ppermute | solution.py:398
  22.6 1.3 %gate_states.1 = (bf16[1,8,128,128]{3,2,1,0:T(8,128)(2,1)S(1)}, bf16[1,8,128,128]{3,2,1,0:T(8,128)(2,1)S(1)}, f32[2,16,128]{2,1,0:T(8,128)S(1)}, f32[16,128]{1,0:T(8,128)S(1)}) custom-call(bf16[4,16,16]{2,1,0:T(8,128)(2,1)S(1)} %pad_maximum_fusion.refs_0_, bf16[4,16,16]{2,1,0:T(8,128)(2,1)S(1)} %collective-permute-done.5.refs_1_, ...), custom_call_target="tpu_custom_call" | custom-call | tf_op jit(solution)/shard_map/gate_states/pallas_call | solution.py:422
  23.9 1.6 %collective-permute-start.6 = (bf16[1,8,128,128]{3,2,1,0:T(8,128)(2,1)S(1)}, bf16[1,8,128,128]{3,2,1,0:T(8,128)(2,1)S(1)}, u32[]{:S(2)}, u32[]{:S(2)}) collective-permute-start(bf16[1,8,128,128]{3,2,1,0:T(8,128)(2,1)S(1)} %get-tuple-element.24), channel_id=1, source_target_pairs={{0,2},{1,3},{2,0},{3,1},{4,6},{5,7},{6,4},{7,5},{8,10},{9,11},{10,... | collective-permute-start | bytes 786440 | tf_op jit(solution)/shard_map/ppermute | solution.py:454
  25.5 4.0 %inside_block.1 = (f32[1,2,8,128,128]{4,3,2,1,0:T(8,128)S(1)}, f32[8,128]{1,0:T(8,128)S(1)}, f32[8,128,128]{2,1,0:T(8,128)S(1)}, bf16[1,8,128,128]{3,2,1,0:T(8,1...) custom-call(bf16[4,8,128,128]{3,2,1,0:T(8,128)(2,1)S(1)} %get-tuple-element.19.refs_3_.keep_ref, ...), custom_call_target="tpu_custom_call" | custom-call | tf_op jit(solution)/shard_map/inside_block/pallas_call | solution.py:455
  29.5 0.1 collective-permute-start.7
  29.6 2.9 %collective-permute-done.6.state_ref = bf16[1,8,128,128]{3,2,1,0:T(8,128)(2,1)S(1)} collective-permute-done((bf16[1,8,128,128]{3,2,1,0:T(8,128)(2,1)S(1)}, bf16[1,8,128,128]{3,2,1,0:T(8,128)(2,1)S(1)}, u32[]{:S(2)}, u32[]{:S(2)}) %collective-permute-start.6) | collective-permute-done | bytes 262176 | tf_op jit(solution)/shard_map/ppermute | solution.py:454
  32.5 2.2 %outside_block.1 = (bf16[1,8,128,128]{3,2,1,0:T(8,128)(2,1)S(1)}, bf16[1,9,128,128]{3,2,1,0:T(8,128)(2,1)S(1)}, f32[2,8,128]{2,1,0:T(8,128)S(1)}, f32[32,8,128]{2,1,0:T(8,128)}) custom-call(bf16[4,8,128,128]{3,2,1,0:T(8,128)(2,1)S(1)} %get-tuple-element.19.refs_3_.keep_ref, bf16[4,8,128,128]{3,2,1,0:T(8,128)(2,1)S(1)} %collective-permute-done.refs_4_.recv_ref, ...), custom_call_target="tpu_custom_call" | custom-call | tf_op jit(solution)/shard_map/outside_block/pallas_call | solution.py:465
  34.8 0.1 collective-permute-start.8
  34.9 2.7 %all-to-all-start = ((f32[32,8,128]{2,1,0:T(8,128)}), f32[32,8,128]{2,1,0:T(8,128)S(1)}, u32[]{:S(2)}, u32[]{:S(2)}) async-start(f32[32,8,128]{2,1,0:T(8,128)} %get-tuple-element.33), calls=%async_computation | async-start | bytes 262144 | tf_op jit(solution)/shard_map/all_to_all | solution.py:475
  37.6 8.2 %all-to-all-done.refs_5_ = f32[32,8,128]{2,1,0:T(8,128)S(1)} async-done(((f32[32,8,128]{2,1,0:T(8,128)}), f32[32,8,128]{2,1,0:T(8,128)S(1)}, u32[]{:S(2)}, u32[]{:S(2)}) %all-to-all-start) | async-done | bytes 131104 | tf_op jit(solution)/shard_map/all_to_all | solution.py:475
  45.8 2.4 %last.1 = (bf16[1,128,16,128]{3,2,1,0:T(8,128)(2,1)}, bf16[1,128,16,128]{3,2,1,0:T(8,128)(2,1)}, f32[16,16]{1,0:T(8,128)}) custom-call(bf16[1,8,128,128]{3,2,1,0:T(8,128)(2,1)S(1)} %get-tuple-element.23.refs_0_, bf16[1,8,128,128]{3,2,1,0:T(8,128)(2,1)S(1)} %get-tuple-element.29.refs_1_, bf16[1,9,128,128]{3,2,1,0:T(8,128)(2,1)S(1)} %collective-permute-done.7.refs_2_, ...), custom_call_target="tpu_custom_call" | custom-call | tf_op jit(solution)/shard_map/last/pallas_call | solution.py:485
  (15 shorter events, 0.1 us)
Async XLA Ops:
  0.6 1.0 %copy-start = (bf16[1,128,16,128]{3,2,1,0:T(8,128)(2,1)S(1)}, bf16[1,128,16,128]{3,2,1,0:T(8,128)(2,1)}, u32[]{:S(2)}) copy-start(bf16[1,128,16,128]{3,2,1,0:T(8,128)(2,1)} %k_ref.1) | copy-start | bytes 1572868
  1.7 1.0 %copy-start.1 = (bf16[1,128,16,128]{3,2,1,0:T(8,128)(2,1)S(1)}, bf16[1,128,16,128]{3,2,1,0:T(8,128)(2,1)}, u32[]{:S(2)}) copy-start(bf16[1,128,16,128]{3,2,1,0:T(8,128)(2,1)} %q_ref.1) | copy-start | bytes 1572868
  2.7 1.0 %copy-start.2 = (bf16[1,128,16,128]{3,2,1,0:T(8,128)(2,1)S(1)}, bf16[1,128,16,128]{3,2,1,0:T(8,128)(2,1)}, u32[]{:S(2)}) copy-start(bf16[1,128,16,128]{3,2,1,0:T(8,128)(2,1)} %v_ref.1) | copy-start | bytes 1572868
  3.8 1.0 %copy-start.3 = (bf16[1,128,16,128]{3,2,1,0:T(8,128)(2,1)S(1)}, bf16[1,128,16,128]{3,2,1,0:T(8,128)(2,1)}, u32[]{:S(2)}) copy-start(bf16[1,128,16,128]{3,2,1,0:T(8,128)(2,1)} %g_ref.1) | copy-start | bytes 1572868
  4.8 3.4 %copy-start.5 = (bf16[16,16]{1,0:T(8,128)(2,1)S(1)}, bf16[16,16]{1,0:T(8,128)(2,1)}, u32[]{:S(2)}) copy-start(bf16[16,16]{1,0:T(8,128)(2,1)} %param.10) | copy-start | bytes 1540
  7.7 14.8 %collective-permute-start = (bf16[4,8,128,128]{3,2,1,0:T(8,128)(2,1)S(1)}, bf16[4,8,128,128]{3,2,1,0:T(8,128)(2,1)S(1)}, u32[]{:S(2)}, u32[]{:S(2)}) collective-permute-start(bf16[4,8,128,128]{3,2,1,0:T(8,128)(2,1)S(1)} %get-tuple-element.20), channel_id=1, source_target_pairs={{0,1},{1,0},{2,3},{3,2},{4,5},{5,4},{6,7},{7,6},{8,9},{9,8},{10,11... | collective-permute-start | bytes 3145736 | tf_op jit(solution)/shard_map/ppermute | solution.py:413
  8.2 6.1 %collective-permute-start.2 = (bf16[16,16]{1,0:T(8,128)(2,1)S(1)}, bf16[16,16]{1,0:T(8,128)(2,1)S(1)}, u32[]{:S(2)}, u32[]{:S(2)}) collective-permute-start(bf16[16,16]{1,0:T(8,128)(2,1)S(1)} %copy-done.5), channel_id=1, source_target_pairs={{0,8},{1,13},{2,10},{3,15},{4,12},{5,9},{6,14},{7,11},{8,0},{9,5},... | collective-permute-start | bytes 1544 | tf_op jit(solution)/shard_map/ppermute | solution.py:396
  10.9 3.4 %collective-permute-start.1 = (bf16[16,16]{1,0:T(8,128)(2,1)S(1)}, bf16[16,16]{1,0:T(8,128)(2,1)S(1)}, u32[]{:S(2)}, u32[]{:S(2)}) collective-permute-start(bf16[16,16]{1,0:T(8,128)(2,1)S(1)} %copy-done.5), channel_id=1, source_target_pairs={{0,0},{1,5},{2,2},{3,7},{4,4},{5,1},{6,6},{7,3},{8,8},{9,13},{10,1... | collective-permute-start | bytes 1544 | tf_op jit(solution)/shard_map/ppermute | solution.py:396
  11.6 5.5 %collective-permute-start.4 = (bf16[16,16]{1,0:T(8,128)(2,1)S(1)}, bf16[16,16]{1,0:T(8,128)(2,1)S(1)}, u32[]{:S(2)}, u32[]{:S(2)}) collective-permute-start(bf16[16,16]{1,0:T(8,128)(2,1)S(1)} %copy-done.5), channel_id=1, source_target_pairs={{0,24},{1,29},{2,26},{3,31},{4,28},{5,25},{6,30},{7,27},{8,16},{9,... | collective-permute-start | bytes 1544 | tf_op jit(solution)/shard_map/ppermute | solution.py:396
  14.1 4.5 %collective-permute-start.3 = (bf16[16,16]{1,0:T(8,128)(2,1)S(1)}, bf16[16,16]{1,0:T(8,128)(2,1)S(1)}, u32[]{:S(2)}, u32[]{:S(2)}) collective-permute-start(bf16[16,16]{1,0:T(8,128)(2,1)S(1)} %copy-done.5), channel_id=1, source_target_pairs={{0,16},{1,21},{2,18},{3,23},{4,20},{5,17},{6,22},{7,19},{8,24},{9,... | collective-permute-start | bytes 1544 | tf_op jit(solution)/shard_map/ppermute | solution.py:396
  18.6 3.9 %copy-start.4 = (bf16[16]{0:T(256)(128)(2,1)S(1)}, bf16[16]{0:T(256)(128)(2,1)}, u32[]{:S(2)}) copy-start(bf16[16]{0:T(256)(128)(2,1)} %param.11) | copy-start | bytes 100
  18.6 3.9 %collective-permute-start.5 = (bf16[4,16,16]{2,1,0:T(8,128)(2,1)S(1)}, bf16[4,16,16]{2,1,0:T(8,128)(2,1)S(1)}, u32[]{:S(2)}, u32[]{:S(2)}) collective-permute-start(bf16[4,16,16]{2,1,0:T(8,128)(2,1)S(1)} %pad_maximum_fusion.refs_0_), channel_id=1, source_target_pairs={{0,1},{1,0},{2,3},{3,2},{4,5},{5,4},{6,7},{7,6},{8,9},{9,8},{10,11... | collective-permute-start | bytes 6152 | tf_op jit(solution)/shard_map/ppermute | solution.py:398
  23.9 8.6 %collective-permute-start.6 = (bf16[1,8,128,128]{3,2,1,0:T(8,128)(2,1)S(1)}, bf16[1,8,128,128]{3,2,1,0:T(8,128)(2,1)S(1)}, u32[]{:S(2)}, u32[]{:S(2)}) collective-permute-start(bf16[1,8,128,128]{3,2,1,0:T(8,128)(2,1)S(1)} %get-tuple-element.24), channel_id=1, source_target_pairs={{0,2},{1,3},{2,0},{3,1},{4,6},{5,7},{6,4},{7,5},{8,10},{9,11},{10,... | collective-permute-start | bytes 786440 | tf_op jit(solution)/shard_map/ppermute | solution.py:454
  29.5 8.1 %collective-permute-start.7 = (bf16[1,9,128,128]{3,2,1,0:T(8,128)(2,1)S(1)}, bf16[1,9,128,128]{3,2,1,0:T(8,128)(2,1)S(1)}, u32[]{:S(2)}, u32[]{:S(2)}) collective-permute-start(bf16[1,9,128,128]{3,2,1,0:T(8,128)(2,1)S(1)} %get-tuple-element.30), channel_id=1, source_target_pairs={{0,1},{1,0},{2,3},{3,2},{4,5},{5,4},{6,7},{7,6},{8,9},{9,8},{10,11... | collective-permute-start | bytes 884744 | tf_op jit(solution)/shard_map/ppermute | solution.py:456
  34.8 11.1 %collective-permute-start.8 = (bf16[1,9,128,128]{3,2,1,0:T(8,128)(2,1)S(1)}, bf16[1,9,128,128]{3,2,1,0:T(8,128)(2,1)S(1)}, u32[]{:S(2)}, u32[]{:S(2)}) collective-permute-start(bf16[1,9,128,128]{3,2,1,0:T(8,128)(2,1)S(1)} %get-tuple-element.31), channel_id=1, source_target_pairs={{0,1},{1,0},{2,3},{3,2},{4,5},{5,4},{6,7},{7,6},{8,9},{9,8},{10,11... | collective-permute-start | bytes 884744 | tf_op jit(solution)/shard_map/ppermute | solution.py:474
  34.9 11.0 %all-to-all-start = ((f32[32,8,128]{2,1,0:T(8,128)}), f32[32,8,128]{2,1,0:T(8,128)S(1)}, u32[]{:S(2)}, u32[]{:S(2)}) async-start(f32[32,8,128]{2,1,0:T(8,128)} %get-tuple-element.33), calls=%async_computation | async-start | bytes 262144 | tf_op jit(solution)/shard_map/all_to_all | solution.py:475

commit v2 on v0

v2 whole, which is shorter than its diff:
```python
import functools

import jax
import jax.numpy as jnp
from jax import lax
from jax.experimental import pallas as pl
from jax.experimental.pallas import tpu as pltpu
from jax.sharding import PartitionSpec as P

F32 = jnp.float32
BF16 = jnp.bfloat16
VMEM = pl.BlockSpec(memory_space=pltpu.VMEM)
ANY = pl.BlockSpec(memory_space=pl.ANY)
HBM = pl.BlockSpec(memory_space=pltpu.HBM)
LIMIT = 24 * 1024 * 1024


def nn(a, b):
    return lax.dot_general(a, b, (((1,), (0,)), ((), ())), preferred_element_type=F32)


def nt(a, b):
    return lax.dot_general(a, b, (((1,), (1,)), ((), ())), preferred_element_type=F32)


def exact(a, b):
    return lax.dot_general(
        a, b, (((1,), (0,)), ((), ())), precision=lax.Precision.HIGHEST, preferred_element_type=F32
    )


def iota(shape, dim):
    return lax.broadcasted_iota(jnp.int32, shape, dim)


def place():
    mine = lax.axis_index("ctx")
    return lax.rem(mine, 2), lax.div(mine, 2)


def hi_lo(rows):
    hi = rows.astype(BF16)
    return jnp.concatenate([hi, (rows - hi.astype(F32)).astype(BF16)], 0)


def call(kernel, name, out_shape, operands, scratch=(), micros=1.0, in_specs=None, out_specs=None, limit=LIMIT):
    outs = len(out_shape)
    return pl.pallas_call(
        kernel,
        out_shape=out_shape,
        in_specs=in_specs or [VMEM] * len(operands),
        out_specs=out_specs or (VMEM,) * outs,
        scratch_shapes=list(scratch),
        compiler_params=pltpu.CompilerParams(vmem_limit_bytes=limit),
        cost_estimate=pl.CostEstimate(
            flops=0, bytes_accessed=int(micros * 3_000_000), transcendentals=0
        ),
        name=name,
    )(*operands)


def split_kernel(k_ref, q_ref, v_ref, g_ref, keep_ref, send_ref, buf, planes, sems, out_sems):
    par, _ = place()
    _, count, heads, width = k_ref.shape
    half = heads // 2
    loads = [
        pltpu.make_async_copy(ref.at[0], buf.at[at], sems.at[at])
        for at, ref in enumerate((k_ref, q_ref, v_ref, g_ref))
    ]
    for load in loads:
        load.start()
    stores = []
    for at, load in enumerate(loads):
        load.wait()
        turned = jnp.swapaxes(buf[at], 0, 1)
        for h in range(heads):
            plane = turned[h]
            planes[at, h // half, h % half] = plane.T if at < 2 else plane
        for out, which, side in ((send_ref, 1 - par, 0), (keep_ref, par, 1)):
            store = pltpu.make_async_copy(planes.at[at, which], out.at[at], out_sems.at[at, side])
            store.start()
            stores.append(store)
    for store in stores:
        store.wait()


def scales(rows):
    end = jnp.broadcast_to(rows[:, -1:], rows.shape)
    return jnp.exp(end - rows), jnp.exp(rows), jnp.exp(end)


def weight_kernel(direct, *refs):
    *gates, bias_ref, gate_ref = refs
    heads, width = gate_ref.shape[1:]
    if direct:
        index = lax.axis_index("dp")
        full = jnp.zeros((heads, width), F32)
        for r, ref in enumerate(gates):
            for low in range(2):
                piece = ref.shape[2]
                owner = jnp.bitwise_xor(index, 2 * r + low)
                pick = iota((piece, width), 1) == iota((piece, width), 0) + owner * piece
                full = full + nn(ref[low], jnp.where(pick, 1.0, 0.0).astype(BF16))
    else:
        full = gates[0][...].astype(F32)
    gate_ref[0] = full
    gate_ref[1] = bias_ref[...]


def gate_kernel(pair, gate_ref, keep_ref, recv_ref, total_ref, near_ref, rows_ref, scale_ref):
    par, chip = place()
    _, half, width, count = keep_ref.shape
    weights = gate_ref[0, pl.ds(par * half, half), :].astype(BF16)
    bias = gate_ref[1, pl.ds(par * half, half), :]
    row = iota((half, count), 0)
    logits = []
    for ref in (keep_ref, recv_ref):
        logit = bias
        for j in range(half):
            logit = logit + jnp.where(row == j, nn(weights, ref[0, j]), 0.0)
        logits.append(logit)
    logit = jnp.concatenate(logits, 0)
    decay = -(jnp.maximum(logit, 0.0) + jnp.log1p(jnp.exp(-jnp.abs(logit))))
    cumul = exact(decay, jnp.where(iota((count, count), 0) <= iota((count, count), 1), 1.0, 0.0))
    rows_ref[0] = cumul
    rows_ref[1] = -1.0 / (1.0 + jnp.exp(-logit))
    tail, head, ends = scales(cumul)
    scale_ref[0] = tail
    scale_ref[1] = head
    for at, side in enumerate((chip,) if pair else (0, 1)):
        enters = par == side
        for j in range(half):
            states = []
            for rel, ref in enumerate((keep_ref, recv_ref)):
                line = scale_ref[side, rel * half + j : rel * half + j + 1, :]
                scaled = (ref[side, j].astype(F32) * line).astype(BF16)
                states.append(nn(scaled, ref[2 + side, j]))
            own, other = states
            passed = (
                jnp.where(enters, ends[half + j : half + j + 1], 1.0) * own
                + jnp.where(enters, 1.0, ends[j : j + 1]) * other
            )
            total_ref[at, j] = passed.astype(total_ref.dtype)
            near_ref[at, j] = jnp.where(enters, own, other).astype(near_ref.dtype)


def weighted_keys(ref, rows):
    half = rows.shape[0]
    lhs = hi_lo(rows)
    row = iota(lhs.shape, 0)
    total = jnp.zeros(lhs.shape, F32)
    for j in range(half):
        total = total + jnp.where((row == j) | (row == j + half), nt(lhs, ref[0, j]), 0.0)
    return total[:half] + total[half:]


def slope_row(ref, side, j, full):
    sign = jnp.where(side == 0, 1.0, -1.0)
    return sign * jnp.sum(ref[1 - side, j].astype(F32) * full, 0, keepdims=True)


def product_kernel(keep_ref, out_ref):
    for j in range(out_ref.shape[0]):
        out_ref[j] = nt(keep_ref[3, j], keep_ref[2, j])


def kappa_kernel(keep_ref, recv_ref, rows_ref, kappa_ref):
    half = kappa_ref.shape[0]
    kappa_ref[...] = weighted_keys(keep_ref, rows_ref[1, :half, :]) + weighted_keys(recv_ref, rows_ref[1, half:, :])


def inside_kernel(pair, keep_ref, recv_ref, rows_ref, near_ref, product_ref, attn_ref, *refs):
    if pair:
        other_ref, mine_ref, send_ref, dg_ref, scale_ref = refs
    else:
        (scale_ref,) = refs
    par, chip = place()
    _, half, width, count = keep_ref.shape
    const = 1.0 / width
    cumul = rows_ref[0]
    columns = cumul.T
    tail, head, _ = scales(cumul)
    scale_ref[0] = tail
    scale_ref[1] = head
    causal = iota((count, count), 0) >= iota((count, count), 1)
    both = (keep_ref, recv_ref)
    side = chip
    if pair:
        enters = par == 1 - side
        for j in range(half):
            line = jnp.where(
                enters, scale_ref[1 - side, j : j + 1, :], scale_ref[1 - side, half + j : half + j + 1, :]
            )
            left = jnp.where(enters, keep_ref[1 - side, j], recv_ref[1 - side, j])
            right = jnp.where(enters, keep_ref[3 - side, j], recv_ref[3 - side, j])
            other_ref[0, j] = nn((left.astype(F32) * line).astype(BF16), right)
        send_ref[0, half] = jnp.zeros((count, width), BF16)
        send_ref[0, half, : 2 * half] = hi_lo(rows_ref[1, half:, :])
    for rel, ref in enumerate(both):
        block = par if rel == 0 else 1 - par
        slopes = []
        for j in range(half):
            at = rel * half + j
            decay = jnp.exp(jnp.where(causal, columns[:, at : at + 1] - cumul[at : at + 1], -1e30))
            product = product_ref[j] if rel == 0 else nt(ref[3, j], ref[2, j])
            weight = (const * product * decay).astype(BF16)
            query = nt(ref[0, j], weight)
            key = nn(ref[1, j], weight)
            if pair:
                attn_ref[0, rel, j] = jnp.where(side == 0, key, query)
                cross = nt(near_ref[0, j], ref[3 - side, j])
                factor = jnp.where(block == side, 0.0, const) * scale_ref[1 - side, at : at + 1, :]
                full = jnp.where(side == 0, query, key) + factor * cross
                (mine_ref if rel == 0 else send_ref)[0, j] = full.astype(BF16).T
                slopes.append(slope_row(ref, side, j, full))
            else:
                attn_ref[0, rel, j] = query
                attn_ref[1, rel, j] = key
        if pair:
            dg_ref[rel] = jnp.concatenate(slopes, 0)


def outside_kernel(pair, keep_ref, recv_ref, rows_ref, state_ref, near_ref, attn_ref, kappa_ref, *refs):
    if pair:
        dg_ref, full_ref, suffix_ref, pieces_ref, scale_ref = refs
    else:
        full_ref, suffix_ref, pieces_ref, scale_ref = refs
    par, chip = place()
    _, half, width, count = keep_ref.shape
    const = 1.0 / width
    cumul = rows_ref[0]
    tail, head, ends = scales(cumul)
    scale_ref[0] = tail
    scale_ref[1] = head
    both = (keep_ref, recv_ref)
    all_slopes = []
    for rel, ref in enumerate(both):
        block = par if rel == 0 else 1 - par
        slopes = dg_ref[rel] if pair else jnp.zeros((half, count), F32)
        for at, side in enumerate((1 - chip,) if pair else (0, 1)):
            enters = block == side
            lines = []
            for j in range(half):
                come = state_ref[at, j].astype(F32)
                passed = (1 - rel) * half + j
                ratio = jnp.where(enters, 1.0, ends[passed : passed + 1])
                known = ratio * come + jnp.where(enters, 0.0, 1.0) * near_ref[at, j]
                cross = nt(known.astype(BF16), ref[3 - side, j])
                factor = const * scale_ref[1 - side, rel * half + j : rel * half + j + 1, :]
                full = attn_ref[at, rel, j] + factor * cross
                full_ref[at, rel, j] = full.astype(BF16)
                lines.append(slope_row(ref, side, j, full))
            slopes = slopes + jnp.concatenate(lines, 0)
        all_slopes.append(slopes)
    slope = jnp.concatenate(all_slopes, 0)
    suffix = exact(slope, jnp.where(iota((count, count), 0) >= iota((count, count), 1), 1.0, 0.0))
    sums = jnp.broadcast_to(suffix[:, :1], suffix.shape)
    first = jnp.where(par == 0, 1.0, 0.0)
    mine = suffix[:half] + first * sums[half:]
    other = suffix[half:] + (1.0 - first) * sums[:half]
    suffix_ref[0] = mine
    suffix_ref[1] = other
    total = sums[:half] + sums[half:]
    before = jnp.where(chip == 1, 1.0, 0.0) if pair else 1.0
    partial = (
        weighted_keys(keep_ref, mine * rows_ref[1, :half, :])
        + weighted_keys(recv_ref, other * rows_ref[1, half:, :])
        + before * (total * kappa_ref[...])
    )
    parts = lax.axis_size("dp")
    ranks = pieces_ref.shape[0] // parts
    piece, slot = width // parts, width // half
    here = iota((half, width), 1) // slot == iota((half, width), 0)
    totals = jnp.sum(jnp.where(here, total, 0.0), 0, keepdims=True)
    for i in range(parts):
        turned = partial if i == 0 else pltpu.roll(partial, width - i * piece, 1)
        turned = pltpu.roll(turned, 0, 1, stride=slot, stride_axis=0)
        line = jnp.sum(jnp.where(here, turned, 0.0), 0, keepdims=True)
        sent = jnp.concatenate([line, totals], 0)
        pieces_ref[pl.ds(i * ranks, ranks)] = jnp.broadcast_to(sent[None], (ranks, 2, width))


def turn_kernel(full_ref, suffix_ref, rows_ref, mine_ref, send_ref):
    sides, _, half, width, count = full_ref.shape
    for at in range(sides):
        for j in range(half):
            mine_ref[at, j] = full_ref[at, 0, j].T
            send_ref[at, j] = full_ref[at, 1, j].T
        send_ref[at, half] = jnp.zeros((count, width), BF16)
    if sides == 2:
        send_ref[0, half, : 2 * half] = hi_lo(rows_ref[1, half:, :])
    send_ref[sides - 1, half, : 2 * half] = hi_lo(suffix_ref[1])


def merge_kernel(pair, suffix_ref, rows_ref, *refs):
    if pair:
        mine0, recv0, mine1, recv1, query_ref, key_ref, line_ref, tmp = refs
        sources = ((mine0, recv0, 0), (mine1, recv1, 0))
    else:
        mine0, recv0, query_ref, key_ref, line_ref, tmp = refs
        sources = ((mine0, recv0, 0), (mine0, recv0, 1))
    par, chip = place()
    _, count, heads, width = query_ref.shape
    half = heads // 2
    for at, (mine, recv, side) in enumerate(sources):
        for j in range(half):
            for ref, base in ((mine, par * half), (recv, (1 - par) * half)):
                tmp[at, pl.ds(base + j, count, stride=heads), :] = ref[side, j].astype(F32)
        got = recv[side, half, : 2 * half].astype(F32)
        line_ref[at, pl.ds((1 - par) * half, half), :] = got[:half] + got[half:]
    line_ref[0, pl.ds(par * half, half), :] = rows_ref[1, :half, :]
    line_ref[1, pl.ds(par * half, half), :] = suffix_ref[0]
    first = chip if pair else 0
    query_ref[0] = tmp[first].reshape(count, heads, width).astype(BF16)
    key_ref[0] = tmp[1 - first].reshape(count, heads, width).astype(BF16)


def last_kernel(lines_ref, key_ref, gate_ref, pieces_ref, out_ref, grad_ref, buf, sems):
    _, chip = place()
    _, count, heads, width = key_ref.shape
    half = heads // 2
    parts, ranks = lax.axis_size("dp"), lax.axis_size("ctx")
    groups, slot = ranks // 2, width // half
    own = pieces_ref[pl.ds(lax.axis_index("dp") * ranks, ranks)].reshape(groups, 2, 2, width)
    beyond = sum(jnp.where(m > chip, 1.0, 0.0) * own[m, :, 1] for m in range(groups))
    lane, sub = iota((half, width), 1), iota((half, width), 0)
    chosen = [
        jnp.sum(jnp.where(lane == sub * slot, beyond[c : c + 1], 0.0), 1, keepdims=True) for c in range(2)
    ]
    after = jnp.concatenate(chosen, 0)
    slope = lines_ref[0] * (lines_ref[1] + after)
    gate = gate_ref[0]
    chunks = sems.shape[0]
    rows = count // chunks
    copies = []
    for c in range(chunks):
        for t in range(c * rows, (c + 1) * rows):
            buf[t] = (key_ref[0, t].astype(F32) + slope[:, t : t + 1] * gate).astype(BF16)
        part = pl.ds(c * rows, rows)
        copy = pltpu.make_async_copy(buf.at[part], out_ref.at[0, part], sems.at[c])
        copy.start()
        copies.append(copy)
    total = jnp.sum(pieces_ref[...].reshape(parts * groups, 2, 2, width)[:, :, 0], 0)
    fold = jnp.where(iota((width, slot), 0) % slot == iota((width, slot), 1), 1.0, 0.0)
    lines = [jnp.where(lane // slot == sub, total[c : c + 1], 0.0) for c in range(2)]
    grad_ref[...] = exact(jnp.concatenate(lines, 0), fold)[:, : width // parts]
    for copy in copies:
        copy.wait()


def across_chips(total, ends, ranks, reverse):
    step = -1 if reverse else 1

    def shift(value, chips):
        hops = [(i, i + 2 * chips * step) for i in range(ranks) if 0 <= i + 2 * chips * step < ranks]
        return lax.ppermute(value, "ctx", hops)

    value, factor = shift(total, 1), shift(ends, 1)
    reach = 1
    while 2 * reach < ranks:
        value = value + factor * shift(value, reach)
        factor = factor * shift(factor, reach)
        reach *= 2
    return value


def per_device(mesh, queries, keys, values, out_grad, gate_weight, head_bias):
    _, count, heads, width = queries.shape
    parts, ranks = mesh.shape["dp"], mesh.shape["ctx"]
    half = heads // 2
    pair = ranks == 4
    direct = parts == 8
    swap = [(i, i ^ 1) for i in range(ranks)]

    def shape(*dims, dtype=BF16):
        return jax.ShapeDtypeStruct(dims, dtype)

    bias = jnp.broadcast_to(head_bias.astype(F32)[:, None], (heads, width))

    quad = shape(4, half, width, count)
    keep, send = call(
        split_kernel,
        "split_heads",
        (quad, quad),
        (keys, queries, values, out_grad),
        [
            pltpu.VMEM((4, count, heads, width), BF16),
            pltpu.VMEM((4, 2, half, width, count), BF16),
            pltpu.SemaphoreType.DMA((4,)),
            pltpu.SemaphoreType.DMA((4, 2)),
        ],
        3.0,
        in_specs=[HBM] * 4,
        out_specs=(HBM, HBM),
        limit=60 * 1024 * 1024,
    )
    if direct:
        nearby = lax.ppermute(gate_weight, "dp", [(i, i ^ 1) for i in range(parts)])
        nearby, send = lax.optimization_barrier((nearby, send))
        two = jnp.stack([gate_weight, nearby])
        gates = [two] + [
            lax.ppermute(two, "dp", [(i, i ^ far) for i in range(parts)]) for far in range(2, parts, 2)
        ]
    else:
        gates = [lax.all_gather(gate_weight, "dp", axis=1, tiled=True)]
    recv = lax.ppermute(send, "ctx", swap)
    (products,) = call(
        product_kernel, "products", (shape(half, count, count, dtype=F32),), (keep,), (), 1.0
    )
    *gates, products = lax.optimization_barrier((*gates, products))

    sides = 1 if pair else 2
    lines = pltpu.VMEM((2, heads, count), F32)
    state = shape(sides, half, width, width, dtype=BF16 if pair else F32)
    (gate_full,) = call(
        functools.partial(weight_kernel, direct),
        "gate_weights",
        (shape(2, heads, width, dtype=F32),),
        (*gates, bias),
        (),
        10.0,
    )
    total, near, rows = call(
        functools.partial(gate_kernel, pair),
        "gate_states",
        (state, state, shape(2, heads, count, dtype=F32)),
        (gate_full, keep, recv),
        [lines],
        1.3,
    )

    attn_shape = shape(sides, 2, half, width, count, dtype=F32)
    mine_shape = shape(sides, half, count, width)
    send_shape = shape(sides, half + 1, count, width)
    slope_shape = shape(2, half, count, dtype=F32)

    def inside(*outs):
        return call(
            functools.partial(inside_kernel, pair),
            "inside_block",
            (attn_shape, *outs),
            (keep, recv, rows, near, products),
            [lines],
            4.0,
        )

    (kappa,) = call(
        kappa_kernel, "kappa", (shape(half, width, dtype=F32),), (keep, recv, rows), (), 0.3
    )
    if pair:
        opposite = [(i, i ^ 2) for i in range(ranks)]
        states = lax.ppermute(total, "ctx", opposite)
        near_shape = shape(1, half, width, width, dtype=F32)
        attn, near, mine_local, send_local, slopes = inside(near_shape, mine_shape, send_shape, slope_shape)
        kappa = lax.ppermute(kappa, "ctx", opposite)
        recv_local = lax.ppermute(send_local, "ctx", swap)
        more = (slopes,)
        local = (mine_local, recv_local)
    else:
        ends = jnp.exp(rows[0, :half, -1] + rows[0, half:, -1])[:, None, None]
        states = jnp.stack(
            [across_chips(total[0], ends, ranks, False), across_chips(total[1], ends, ranks, True)]
        )
        (attn,) = inside()
        kappa = across_chips(kappa, jnp.ones((half, 1), F32), ranks, False)
        more = ()
        local = ()
    full, suffix, pieces = call(
        functools.partial(outside_kernel, pair),
        "outside_block",
        (shape(sides, 2, half, width, count), slope_shape, shape(parts * ranks, 2, width, dtype=F32)),
        (keep, recv, rows, states, near, attn, kappa, *more),
        [lines],
        1.5,
    )
    pieces = lax.all_to_all(pieces, ("dp", "ctx"), 0, 0, tiled=True)

    mine, send = call(turn_kernel, "turn_planes", (mine_shape, send_shape), (full, suffix, rows), (), 1.0)
    recv_out = lax.ppermute(send, "ctx", swap)
    whole = shape(1, count, heads, width)
    query_grad, key_part, out_lines = call(
        functools.partial(merge_kernel, pair),
        "merge_heads",
        (whole, whole, shape(2, heads, count, dtype=F32)),
        (suffix, rows, *local, mine, recv_out),
        [pltpu.VMEM((2, count * heads, width), F32)],
        2.0,
    )
    key_grad, gate_grad = call(
        last_kernel,
        "key_gradient",
        (whole, shape(heads, width // parts, dtype=F32)),
        (out_lines, key_part, gate_full, pieces),
        [pltpu.VMEM((count, heads, width), BF16), pltpu.SemaphoreType.DMA((4,))],
        1.0,
        out_specs=(ANY, VMEM),
    )
    return query_grad, key_grad, gate_grad


def solution(mesh):
    return jax.shard_map(
        functools.partial(per_device, mesh),
        mesh=mesh,
        in_specs=(
            P("dp", "ctx", None, None),
            P("dp", "ctx", None, None),
            P("dp", "ctx", None, None),
            P("dp", "ctx", None, None),
            P(None, "dp"),
            P(),
        ),
        out_specs=(P("dp", "ctx", None, None), P("dp", "ctx", None, None), P(None, "dp")),
        check_vma=False,
    )
```

time: 183 us -> 39.5 us (0.22)
  blocking collectives: 83.6 us -> 0 us
  waiting for transfers between devices: 50.2 us -> 10.7 us
  between operations: 14.9 us -> 0.75 us
  other arithmetic: 14 us -> 0.01 us
  Pallas kernels: 0 us -> 13 us
  starting transfers between devices: 0.08 us -> 13 us
  matrix products: 10.6 us -> 0 us
  local copies, waits for them, and re-layouts: 8.38 us -> 1.9 us
    all_gather x2 -> x0, waiting for transfers between devices: 50.2 us -> none  [carried_in(): everything = jax.tree.map(lambda part: lax.all_gather(part, axis), shard)]
    psum x1 -> x0, blocking collectives: 40.5 us -> none  [per_device(): summed = lax.psum(term, ('dp', 'ctx'))]
    all_gather x2 -> x0, blocking collectives: 37.2 us -> none  [the longest x1 32.2 us: per_device(): gate_full = lax.all_gather(gate_weight, 'dp', axis=1, tiled=True)]
    pallas_call x0 -> x10, Pallas kernels: none -> 13 us  [call(): pl.pallas_call(kernel, out_shape=out_shape, in_specs=in_specs or [VMEM] *...]
    select_n x12 -> x0, other arithmetic: 11.8 us -> none  [hop(): return jax.tree.map(lambda a, b: jnp.where(reached, a, b), new, before)]
    dot_general x7 -> x0, matrix products: 10.6 us -> none  [the longest x1 2.94 us: block_grads(): jnp.einsum('the,hde->thd', grads_block, in_round, preferred_element_type=...]
    ppermute x0 -> x9, starting transfers between devices: none -> 9.75 us  [the longest x3 4.39 us: per_device(): lax.ppermute(two, 'dp', [(i, i ^ far) for i in range(parts)])]
    unnamed x1 -> x0, blocking collectives: 5.87 us -> none
  transfers between devices with their start and end apart: 2 -> 10, of which waited for: 2 -> 4; matrix products, arithmetic and copies ran while one was open for 8% -> 0% of each run, Pallas kernels for 0% -> 26%
where the time goes in v2:
time: 39.5 us; the launch traced here: 39.3 us
  starting transfers between devices  13 us (33%)
  Pallas kernels  13 us (33%)
  waiting for transfers between devices  10.7 us (27%)
  local copies, waits for them, and re-layouts  1.9 us (5%)
  between operations  0.75 us (2%)
    pallas_call x10, Pallas kernels, call(): pl.pallas_call(kernel, out_shape=out_shape, in_specs=in_specs or [VMEM] *...  13 us
    all_to_all x1, waiting for transfers between devices, per_device(): pieces = lax.all_to_all(pieces, ('dp', 'ctx'), 0, 0, tiled=True)  5.28 us
    ppermute x3, starting transfers between devices, per_device(): lax.ppermute(two, 'dp', [(i, i ^ far) for i in range(parts)])  4.39 us
    ppermute x3, waiting for transfers between devices, per_device(): lax.ppermute(two, 'dp', [(i, i ^ far) for i in range(parts)])  3.69 us
    all_to_all x1, starting transfers between devices, per_device(): pieces = lax.all_to_all(pieces, ('dp', 'ctx'), 0, 0, tiled=True)  3.23 us
    ppermute x1, starting transfers between devices, per_device(): nearby = lax.ppermute(gate_weight, 'dp', [(i, i ^ 1) for i in range(parts)])  3.03 us
    unnamed x8, local copies, waits for them, and re-layouts  1.82 us
    ppermute x1, waiting for transfers between devices, per_device(): kappa = lax.ppermute(kappa, 'ctx', opposite)  1.71 us
  transfers between devices with their start and end apart: 10, of which 4 were waited for; matrix products, arithmetic and copies ran while one was open for 0% of the time, Pallas kernels for 26%

profile of v2, /device:TPU:0, one launch (start us, length us, event | category | flops | bytes accessed | tf_op | source)
XLA Modules:
  0.0 39.3 jit_solution(1308611920828317585)
XLA Ops:
  0.6 3.0 %collective-permute-start = (bf16[16,16]{1,0:T(8,128)(2,1)}, bf16[16,16]{1,0:T(8,128)(2,1)S(1)}, u32[]{:S(2)}, u32[]{:S(2)}) collective-permute-start(bf16[16,16]{1,0:T(8,128)(2,1)} %param.10), channel_id=1, source_target_pairs={{0,4},{4,0},{8,12},{12,8},{16,20},{20,16},{24,28},{28,24},{1,5},{5... | collective-permute-start | bytes 1544 | tf_op jit(solution)/shard_map/ppermute | solution.py:398
  3.7 2.8 %split_heads.1 = (bf16[4,8,128,128]{3,2,1,0:T(8,128)(2,1)}, bf16[4,8,128,128]{3,2,1,0:T(8,128)(2,1)}) custom-call(bf16[1,128,16,128]{3,2,1,0:T(8,128)(2,1)} %k_ref.1, bf16[1,128,16,128]{3,2,1,0:T(8,128)(2,1)} %q_ref.1, bf16[1,128,16,128]{3,2,1,0:T(8,128)(2,1)} %v_ref.1, bf16[1,128,16,128]{3,2,1,0:T(8,128)(2,1)} %g_ref.1), custom_call_target="tpu_custom_call" | custom-call | bytes 9000000 | tf_op jit(solution)/shard_map/split_heads/pallas_call | solution.py:48
  6.6 0.6 %copy-done.2 = bf16[16,16]{1,0:T(8,128)(2,1)S(1)} copy-done((bf16[16,16]{1,0:T(8,128)(2,1)S(1)}, bf16[16,16]{1,0:T(8,128)(2,1)}, u32[]{:S(2)}) %copy-start.2) | copy-done | bytes 536
  7.2 1.6 %collective-permute-start.2 = (bf16[2,16,16]{2,1,0:T(8,128)(2,1)S(1)}, bf16[2,16,16]{2,1,0:T(8,128)(2,1)S(1)}, u32[]{:S(2)}, u32[]{:S(2)}) collective-permute-start(bf16[2,16,16]{2,1,0:T(8,128)(2,1)S(1)} %pad_maximum_fusion.refs_0_), channel_id=1, source_target_pairs={{0,8},{4,12},{8,0},{12,4},{16,24},{20,28},{24,16},{28,20},{1,9},{5... | collective-permute-start | bytes 3080 | tf_op jit(solution)/shard_map/ppermute | solution.py:402
  8.7 2.6 %collective-permute-start.3 = (bf16[2,16,16]{2,1,0:T(8,128)(2,1)S(1)}, bf16[2,16,16]{2,1,0:T(8,128)(2,1)S(1)}, u32[]{:S(2)}, u32[]{:S(2)}) collective-permute-start(bf16[2,16,16]{2,1,0:T(8,128)(2,1)S(1)} %pad_maximum_fusion.refs_0_), channel_id=1, source_target_pairs={{0,16},{4,20},{8,24},{12,28},{16,0},{20,4},{24,8},{28,12},{1,17},{... | collective-permute-start | bytes 3080 | tf_op jit(solution)/shard_map/ppermute | solution.py:402
  11.3 0.2 collective-permute-start.4
  11.6 1.2 %copy-done = bf16[4,8,128,128]{3,2,1,0:T(8,128)(2,1)S(1)} copy-done((bf16[4,8,128,128]{3,2,1,0:T(8,128)(2,1)S(1)}, bf16[4,8,128,128]{3,2,1,0:T(8,128)(2,1)}, u32[]{:S(2)}) %copy-start) | copy-done | bytes 1048600
  12.8 0.3 products.1.product_ref
  13.1 0.3 collective-permute-done.3.refs_2_
  13.4 3.4 %collective-permute-done.4.refs_3_ = bf16[2,16,16]{2,1,0:T(8,128)(2,1)S(1)} collective-permute-done((bf16[2,16,16]{2,1,0:T(8,128)(2,1)S(1)}, bf16[2,16,16]{2,1,0:T(8,128)(2,1)S(1)}, u32[]{:S(2)}, u32[]{:S(2)}) %collective-permute-start.4) | collective-permute-done | bytes 1056 | tf_op jit(solution)/shard_map/ppermute | solution.py:402
  16.9 0.1 gate_weights.1.gate_ref
  17.0 0.9 %gate_states.1 = (bf16[1,8,128,128]{3,2,1,0:T(8,128)(2,1)S(1)}, bf16[1,8,128,128]{3,2,1,0:T(8,128)(2,1)S(1)}, f32[2,16,128]{2,1,0:T(8,128)S(1)}) custom-call(f32[2,16,128]{2,1,0:T(8,128)S(1)} %gate_weights.1.gate_ref, bf16[4,8,128,128]{3,2,1,0:T(8,128)(2,1)S(1)} %copy-done.1, bf16[4,8,128,128]{3,2,1,0:T(8,128)(2,1)S(1)} %collective-permute-done.1.recv_ref), custom_call_target="tpu_custom_call" | custom-call | bytes 3900000 | tf_op jit(solution)/shard_map/gate_states/pallas_call | solution.py:48
  17.9 1.6 %collective-permute-start.5 = (bf16[1,8,128,128]{3,2,1,0:T(8,128)(2,1)S(1)}, bf16[1,8,128,128]{3,2,1,0:T(8,128)(2,1)S(1)}, u32[]{:S(2)}, u32[]{:S(2)}) collective-permute-start(bf16[1,8,128,128]{3,2,1,0:T(8,128)(2,1)S(1)} %get-tuple-element.39), channel_id=1, source_target_pairs={{0,2},{1,3},{2,0},{3,1},{4,6},{5,7},{6,4},{7,5},{8,10},{9,11},{10,... | collective-permute-start | bytes 786440 | tf_op jit(solution)/shard_map/ppermute | solution.py:452
  19.5 0.4 kappa.1
  19.8 0.6 %collective-permute-start.6 = (f32[8,128]{1,0:T(8,128)S(1)}, f32[8,128]{1,0:T(8,128)S(1)}, u32[]{:S(2)}, u32[]{:S(2)}) collective-permute-start(f32[8,128]{1,0:T(8,128)S(1)} %kappa.1), channel_id=1, source_target_pairs={{0,2},{1,3},{2,0},{3,1},{4,6},{5,7},{6,4},{7,5},{8,10},{9,11},{10,... | collective-permute-start | bytes 12296 | tf_op jit(solution)/shard_map/ppermute | solution.py:455
  20.4 2.4 %inside_block.1 = (f32[1,2,8,128,128]{4,3,2,1,0:T(8,128)S(1)}, f32[1,8,128,128]{3,2,1,0:T(8,128)S(1)}, bf16[1,8,128,128]{3,2,1,0:T(8,128)(2,1)S(1)}, bf16[1,9,12...) custom-call(bf16[4,8,128,128]{3,2,1,0:T(8,128)(2,1)S(1)} %copy-done.1, ...), custom_call_target="tpu_custom_call" | custom-call | bytes 12000000 | tf_op jit(solution)/shard_map/inside_block/pallas_call | solution.py:48
  22.8 0.1 collective-permute-start.7
  22.8 1.7 %collective-permute-done.6.kappa_ref = f32[8,128]{1,0:T(8,128)S(1)} collective-permute-done((f32[8,128]{1,0:T(8,128)S(1)}, f32[8,128]{1,0:T(8,128)S(1)}, u32[]{:S(2)}, u32[]{:S(2)}) %collective-permute-start.6) | collective-permute-done | bytes 4128 | tf_op jit(solution)/shard_map/ppermute | solution.py:455
  24.5 2.0 %outside_block.1 = (bf16[1,2,8,128,128]{4,3,2,1,0:T(8,128)(2,1)S(1)}, f32[2,8,128]{2,1,0:T(8,128)S(1)}, f32[32,2,128]{2,1,0:T(2,128)}) custom-call(bf16[4,8,128,128]{3,2,1,0:T(8,128)(2,1)S(1)} %copy-done.1, bf16[4,8,128,128]{3,2,1,0:T(8,128)(2,1)S(1)} %collective-permute-done.1.recv_ref, f32[2,16,128]{2,1,0:T(8,128)S(1)} %get-tuple-element.38.rows_ref, ...), custom_call_target="tpu_custom_call" | custom-call | bytes 4500000 | tf_op jit(solution)/shard_map/outside_block/pallas_call | solution.py:48
  26.6 0.2 turn_planes.1
  26.9 3.2 %all-to-all-start = ((f32[32,2,128]{2,1,0:T(2,128)}), f32[32,2,128]{2,1,0:T(2,128)S(1)}, u32[]{:S(2)}, u32[]{:S(2)}) async-start(f32[32,2,128]{2,1,0:T(2,128)} %get-tuple-element.54), calls=%async_computation | async-start | bytes 65536 | tf_op jit(solution)/shard_map/all_to_all | solution.py:476
  30.1 1.9 %merge_heads.1 = (bf16[1,128,16,128]{3,2,1,0:T(8,128)(2,1)}, bf16[1,128,16,128]{3,2,1,0:T(8,128)(2,1)S(1)}, f32[2,16,128]{2,1,0:T(8,128)S(1)}) custom-call(f32[2,8,128]{2,1,0:T(8,128)S(1)} %get-tuple-element.45.suffix_ref, f32[2,16,128]{2,1,0:T(8,128)S(1)} %get-tuple-element.38.rows_ref, bf16[1,8,128,128]{3,2,1,0:T(8,128)(2,1)S(1)} %get-tuple-element.46.refs_0_, ...), custom_call_target="tpu_custom_call" | custom-call | bytes 6000000 | tf_op jit(solution)/shard_map/merge_heads/pallas_call | solution.py:48
  32.1 5.3 %all-to-all-done.pieces_ref = f32[32,2,128]{2,1,0:T(2,128)S(1)} async-done(((f32[32,2,128]{2,1,0:T(2,128)}), f32[32,2,128]{2,1,0:T(2,128)S(1)}, u32[]{:S(2)}, u32[]{:S(2)}) %all-to-all-start) | async-done | bytes 32800 | tf_op jit(solution)/shard_map/all_to_all | solution.py:476
  37.3 2.0 %key_gradient.1 = (bf16[1,128,16,128]{3,2,1,0:T(8,128)(2,1)}, f32[16,16]{1,0:T(8,128)}) custom-call(f32[2,16,128]{2,1,0:T(8,128)S(1)} %get-tuple-element.52.lines_ref, bf16[1,128,16,128]{3,2,1,0:T(8,128)(2,1)S(1)} %get-tuple-element.53.key_ref, f32[2,16,128]{2,1,0:T(8,128)S(1)} %gate_weights.1.gate_ref, f32[32,2,128]{2,1,0:T(2,128)S(1)} %all-to-all-done.pieces_ref), custom_call_target="tpu_custom_call" | custom-call | bytes 3000000 | tf_op jit(solution)/shard_map/key_gradient/pallas_call | solution.py:48
  (16 shorter events, 0.2 us)
Async XLA Ops:
  0.6 5.9 %collective-permute-start = (bf16[16,16]{1,0:T(8,128)(2,1)}, bf16[16,16]{1,0:T(8,128)(2,1)S(1)}, u32[]{:S(2)}, u32[]{:S(2)}) collective-permute-start(bf16[16,16]{1,0:T(8,128)(2,1)} %param.10), channel_id=1, source_target_pairs={{0,4},{4,0},{8,12},{12,8},{16,20},{20,16},{24,28},{28,24},{1,5},{5... | collective-permute-start | bytes 1544 | tf_op jit(solution)/shard_map/ppermute | solution.py:398
  6.5 0.7 %copy-start.2 = (bf16[16,16]{1,0:T(8,128)(2,1)S(1)}, bf16[16,16]{1,0:T(8,128)(2,1)}, u32[]{:S(2)}) copy-start(bf16[16,16]{1,0:T(8,128)(2,1)} %param.10) | copy-start | bytes 1540
  6.5 10.5 %collective-permute-start.1 = (bf16[4,8,128,128]{3,2,1,0:T(8,128)(2,1)}, bf16[4,8,128,128]{3,2,1,0:T(8,128)(2,1)S(1)}, u32[]{:S(2)}, u32[]{:S(2)}) collective-permute-start(bf16[4,8,128,128]{3,2,1,0:T(8,128)(2,1)} %get-tuple-element.32), channel_id=1, source_target_pairs={{0,1},{1,0},{2,3},{3,2},{4,5},{5,4},{6,7},{7,6},{8,9},{9,8},{10,11... | collective-permute-start | bytes 3145736 | tf_op jit(solution)/shard_map/ppermute | solution.py:406
  7.2 5.9 %collective-permute-start.2 = (bf16[2,16,16]{2,1,0:T(8,128)(2,1)S(1)}, bf16[2,16,16]{2,1,0:T(8,128)(2,1)S(1)}, u32[]{:S(2)}, u32[]{:S(2)}) collective-permute-start(bf16[2,16,16]{2,1,0:T(8,128)(2,1)S(1)} %pad_maximum_fusion.refs_0_), channel_id=1, source_target_pairs={{0,8},{4,12},{8,0},{12,4},{16,24},{20,28},{24,16},{28,20},{1,9},{5... | collective-permute-start | bytes 3080 | tf_op jit(solution)/shard_map/ppermute | solution.py:402
  8.7 4.6 %collective-permute-start.3 = (bf16[2,16,16]{2,1,0:T(8,128)(2,1)S(1)}, bf16[2,16,16]{2,1,0:T(8,128)(2,1)S(1)}, u32[]{:S(2)}, u32[]{:S(2)}) collective-permute-start(bf16[2,16,16]{2,1,0:T(8,128)(2,1)S(1)} %pad_maximum_fusion.refs_0_), channel_id=1, source_target_pairs={{0,16},{4,20},{8,24},{12,28},{16,0},{20,4},{24,8},{28,12},{1,17},{... | collective-permute-start | bytes 3080 | tf_op jit(solution)/shard_map/ppermute | solution.py:402
  11.3 5.4 %collective-permute-start.4 = (bf16[2,16,16]{2,1,0:T(8,128)(2,1)S(1)}, bf16[2,16,16]{2,1,0:T(8,128)(2,1)S(1)}, u32[]{:S(2)}, u32[]{:S(2)}) collective-permute-start(bf16[2,16,16]{2,1,0:T(8,128)(2,1)S(1)} %pad_maximum_fusion.refs_0_), channel_id=1, source_target_pairs={{0,24},{4,28},{8,16},{12,20},{16,8},{20,12},{24,0},{28,4},{1,25},{... | collective-permute-start | bytes 3080 | tf_op jit(solution)/shard_map/ppermute | solution.py:402
  11.6 1.2 %copy-start = (bf16[4,8,128,128]{3,2,1,0:T(8,128)(2,1)S(1)}, bf16[4,8,128,128]{3,2,1,0:T(8,128)(2,1)}, u32[]{:S(2)}) copy-start(bf16[4,8,128,128]{3,2,1,0:T(8,128)(2,1)} %get-tuple-element.30.keep_ref) | copy-start | bytes 3145732
  12.8 4.0 %copy-start.3 = (bf16[16]{0:T(256)(128)(2,1)S(1)}, bf16[16]{0:T(256)(128)(2,1)}, u32[]{:S(2)}) copy-start(bf16[16]{0:T(256)(128)(2,1)} %param.11) | copy-start | bytes 100
  12.8 4.2 %copy-start.1 = (bf16[4,8,128,128]{3,2,1,0:T(8,128)(2,1)S(1)}, bf16[4,8,128,128]{3,2,1,0:T(8,128)(2,1)}, u32[]{:S(2)}) copy-start(bf16[4,8,128,128]{3,2,1,0:T(8,128)(2,1)} %get-tuple-element.30.keep_ref) | copy-start | bytes 3145732
  17.9 6.6 %collective-permute-start.5 = (bf16[1,8,128,128]{3,2,1,0:T(8,128)(2,1)S(1)}, bf16[1,8,128,128]{3,2,1,0:T(8,128)(2,1)S(1)}, u32[]{:S(2)}, u32[]{:S(2)}) collective-permute-start(bf16[1,8,128,128]{3,2,1,0:T(8,128)(2,1)S(1)} %get-tuple-element.39), channel_id=1, source_target_pairs={{0,2},{1,3},{2,0},{3,1},{4,6},{5,7},{6,4},{7,5},{8,10},{9,11},{10,... | collective-permute-start | bytes 786440 | tf_op jit(solution)/shard_map/ppermute | solution.py:452
  19.8 4.7 %collective-permute-start.6 = (f32[8,128]{1,0:T(8,128)S(1)}, f32[8,128]{1,0:T(8,128)S(1)}, u32[]{:S(2)}, u32[]{:S(2)}) collective-permute-start(f32[8,128]{1,0:T(8,128)S(1)} %kappa.1), channel_id=1, source_target_pairs={{0,2},{1,3},{2,0},{3,1},{4,6},{5,7},{6,4},{7,5},{8,10},{9,11},{10,... | collective-permute-start | bytes 12296 | tf_op jit(solution)/shard_map/ppermute | solution.py:455
  22.8 7.3 %collective-permute-start.7 = (bf16[1,9,128,128]{3,2,1,0:T(8,128)(2,1)S(1)}, bf16[1,9,128,128]{3,2,1,0:T(8,128)(2,1)S(1)}, u32[]{:S(2)}, u32[]{:S(2)}) collective-permute-start(bf16[1,9,128,128]{3,2,1,0:T(8,128)(2,1)S(1)} %get-tuple-element.47), channel_id=1, source_target_pairs={{0,1},{1,0},{2,3},{3,2},{4,5},{5,4},{6,7},{7,6},{8,9},{9,8},{10,11... | collective-permute-start | bytes 884744 | tf_op jit(solution)/shard_map/ppermute | solution.py:456
  26.8 3.3 %collective-permute-start.8 = (bf16[1,9,128,128]{3,2,1,0:T(8,128)(2,1)S(1)}, bf16[1,9,128,128]{3,2,1,0:T(8,128)(2,1)S(1)}, u32[]{:S(2)}, u32[]{:S(2)}) collective-permute-start(bf16[1,9,128,128]{3,2,1,0:T(8,128)(2,1)S(1)} %get-tuple-element.50), channel_id=1, source_target_pairs={{0,1},{1,0},{2,3},{3,2},{4,5},{5,4},{6,7},{7,6},{8,9},{9,8},{10,11... | collective-permute-start | bytes 884744 | tf_op jit(solution)/shard_map/ppermute | solution.py:479
  26.9 10.5 %all-to-all-start = ((f32[32,2,128]{2,1,0:T(2,128)}), f32[32,2,128]{2,1,0:T(2,128)S(1)}, u32[]{:S(2)}, u32[]{:S(2)}) async-start(f32[32,2,128]{2,1,0:T(2,128)} %get-tuple-element.54), calls=%async_computation | async-start | bytes 65536 | tf_op jit(solution)/shard_map/all_to_all | solution.py:476

commit v3 on v2

--- a/solution.py
+++ b/solution.py
@@ -59,29 +59,27 @@
     )(*operands)
 
 
-def split_kernel(k_ref, q_ref, v_ref, g_ref, keep_ref, send_ref, buf, planes, sems, out_sems):
+def split_kernel(k_ref, q_ref, v_ref, g_ref, gate_ref, keep_ref, send_ref, copy_ref, buf, sems):
     par, _ = place()
-    _, count, heads, width = k_ref.shape
-    half = heads // 2
+    half = keep_ref.shape[1]
     loads = [
         pltpu.make_async_copy(ref.at[0], buf.at[at], sems.at[at])
         for at, ref in enumerate((k_ref, q_ref, v_ref, g_ref))
     ]
     for load in loads:
         load.start()
-    stores = []
+    gate = pltpu.make_async_copy(gate_ref, copy_ref, sems.at[len(loads)])
+    gate.start()
     for at, load in enumerate(loads):
         load.wait()
-        turned = jnp.swapaxes(buf[at], 0, 1)
-        for h in range(heads):
-            plane = turned[h]
-            planes[at, h // half, h % half] = plane.T if at < 2 else plane
-        for out, which, side in ((send_ref, 1 - par, 0), (keep_ref, par, 1)):
-            store = pltpu.make_async_copy(planes.at[at, which], out.at[at], out_sems.at[at, side])
-            store.start()
-            stores.append(store)
-    for store in stores:
-        store.wait()
+        planes = jnp.swapaxes(buf[at], 0, 1)
+        for j in range(half):
+            first, second = planes[j], planes[half + j]
+            if at < 2:
+                first, second = first.T, second.T
+            keep_ref[at, j] = jnp.where(par == 0, first, second)
+            send_ref[at, j] = jnp.where(par == 0, second, first)
+    gate.wait()
 
 
 def scales(rows):
@@ -211,7 +209,7 @@
                 cross = nt(near_ref[0, j], ref[3 - side, j])
                 factor = jnp.where(block == side, 0.0, const) * scale_ref[1 - side, at : at + 1, :]
                 full = jnp.where(side == 0, query, key) + factor * cross
-                (mine_ref if rel == 0 else send_ref)[0, j] = full.astype(BF16).T
+                (mine_ref if rel == 0 else send_ref)[0, j] = full.astype(BF16)
                 slopes.append(slope_row(ref, side, j, full))
             else:
                 attn_ref[0, rel, j] = query
@@ -222,9 +220,9 @@
 
 def outside_kernel(pair, keep_ref, recv_ref, rows_ref, state_ref, near_ref, attn_ref, kappa_ref, *refs):
     if pair:
-        dg_ref, full_ref, suffix_ref, pieces_ref, scale_ref = refs
+        dg_ref, mine_ref, send_ref, suffix_ref, pieces_ref, scale_ref = refs
     else:
-        full_ref, suffix_ref, pieces_ref, scale_ref = refs
+        mine_ref, send_ref, suffix_ref, pieces_ref, scale_ref = refs
     par, chip = place()
     _, half, width, count = keep_ref.shape
     const = 1.0 / width
@@ -248,7 +246,7 @@
                 cross = nt(known.astype(BF16), ref[3 - side, j])
                 factor = const * scale_ref[1 - side, rel * half + j : rel * half + j + 1, :]
                 full = attn_ref[at, rel, j] + factor * cross
-                full_ref[at, rel, j] = full.astype(BF16)
+                (mine_ref if rel == 0 else send_ref)[at, j] = full.astype(BF16)
                 lines.append(slope_row(ref, side, j, full))
             slopes = slopes + jnp.concatenate(lines, 0)
         all_slopes.append(slopes)
@@ -258,8 +256,13 @@
     first = jnp.where(par == 0, 1.0, 0.0)
     mine = suffix[:half] + first * sums[half:]
     other = suffix[half:] + (1.0 - first) * sums[:half]
-    suffix_ref[0] = mine
-    suffix_ref[1] = other
+    suffix_ref[...] = mine
+    sides = send_ref.shape[0]
+    for at in range(sides):
+        send_ref[at, half] = jnp.zeros((width, count), BF16)
+    if sides == 2:
+        send_ref[0, half, : 2 * half] = hi_lo(rows_ref[1, half:, :])
+    send_ref[sides - 1, half, : 2 * half] = hi_lo(other)
     total = sums[:half] + sums[half:]
     before = jnp.where(chip == 1, 1.0, 0.0) if pair else 1.0
     partial = (
@@ -278,18 +281,6 @@
         line = jnp.sum(jnp.where(here, turned, 0.0), 0, keepdims=True)
         sent = jnp.concatenate([line, totals], 0)
         pieces_ref[pl.ds(i * ranks, ranks)] = jnp.broadcast_to(sent[None], (ranks, 2, width))
-
-
-def turn_kernel(full_ref, suffix_ref, rows_ref, mine_ref, send_ref):
-    sides, _, half, width, count = full_ref.shape
-    for at in range(sides):
-        for j in range(half):
-            mine_ref[at, j] = full_ref[at, 0, j].T
-            send_ref[at, j] = full_ref[at, 1, j].T
-        send_ref[at, half] = jnp.zeros((count, width), BF16)
-    if sides == 2:
-        send_ref[0, half, : 2 * half] = hi_lo(rows_ref[1, half:, :])
-    send_ref[sides - 1, half, : 2 * half] = hi_lo(suffix_ref[1])
 
 
 def merge_kernel(pair, suffix_ref, rows_ref, *refs):
@@ -305,17 +296,17 @@
     for at, (mine, recv, side) in enumerate(sources):
         for j in range(half):
             for ref, base in ((mine, par * half), (recv, (1 - par) * half)):
-                tmp[at, pl.ds(base + j, count, stride=heads), :] = ref[side, j].astype(F32)
+                tmp[at, pl.ds(base + j, count, stride=heads), :] = ref[side, j].T.astype(F32)
         got = recv[side, half, : 2 * half].astype(F32)
         line_ref[at, pl.ds((1 - par) * half, half), :] = got[:half] + got[half:]
     line_ref[0, pl.ds(par * half, half), :] = rows_ref[1, :half, :]
-    line_ref[1, pl.ds(par * half, half), :] = suffix_ref[0]
+    line_ref[1, pl.ds(par * half, half), :] = suffix_ref[...]
     first = chip if pair else 0
     query_ref[0] = tmp[first].reshape(count, heads, width).astype(BF16)
     key_ref[0] = tmp[1 - first].reshape(count, heads, width).astype(BF16)
 
 
-def last_kernel(lines_ref, key_ref, gate_ref, pieces_ref, out_ref, grad_ref, buf, sems):
+def last_kernel(lines_ref, key_ref, gate_ref, pieces_ref, out_ref, grad_ref, buf, small, sems):
     _, chip = place()
     _, count, heads, width = key_ref.shape
     half = heads // 2
@@ -330,22 +321,18 @@
     after = jnp.concatenate(chosen, 0)
     slope = lines_ref[0] * (lines_ref[1] + after)
     gate = gate_ref[0]
-    chunks = sems.shape[0]
-    rows = count // chunks
-    copies = []
-    for c in range(chunks):
-        for t in range(c * rows, (c + 1) * rows):
-            buf[t] = (key_ref[0, t].astype(F32) + slope[:, t : t + 1] * gate).astype(BF16)
-        part = pl.ds(c * rows, rows)
-        copy = pltpu.make_async_copy(buf.at[part], out_ref.at[0, part], sems.at[c])
-        copy.start()
-        copies.append(copy)
+    for t in range(count):
+        buf[t] = (key_ref[0, t].astype(F32) + slope[:, t : t + 1] * gate).astype(BF16)
+    key_copy = pltpu.make_async_copy(buf, out_ref.at[0], sems.at[0])
+    key_copy.start()
     total = jnp.sum(pieces_ref[...].reshape(parts * groups, 2, 2, width)[:, :, 0], 0)
     fold = jnp.where(iota((width, slot), 0) % slot == iota((width, slot), 1), 1.0, 0.0)
     lines = [jnp.where(lane // slot == sub, total[c : c + 1], 0.0) for c in range(2)]
-    grad_ref[...] = exact(jnp.concatenate(lines, 0), fold)[:, : width // parts]
-    for copy in copies:
-        copy.wait()
+    small[...] = exact(jnp.concatenate(lines, 0), fold)[:, : width // parts]
+    grad_copy = pltpu.make_async_copy(small, grad_ref, sems.at[1])
+    grad_copy.start()
+    key_copy.wait()
+    grad_copy.wait()
 
 
 def across_chips(total, ends, ranks, reverse):
@@ -378,28 +365,26 @@
     bias = jnp.broadcast_to(head_bias.astype(F32)[:, None], (heads, width))
 
     quad = shape(4, half, width, count)
-    keep, send = call(
+    pinned = [
+        pltpu.with_memory_space_constraint(x, pltpu.HBM)
+        for x in (keys, queries, values, out_grad, gate_weight)
+    ]
+    keep, send, gate_copy = call(
         split_kernel,
         "split_heads",
-        (quad, quad),
-        (keys, queries, values, out_grad),
-        [
-            pltpu.VMEM((4, count, heads, width), BF16),
-            pltpu.VMEM((4, 2, half, width, count), BF16),
-            pltpu.SemaphoreType.DMA((4,)),
-            pltpu.SemaphoreType.DMA((4, 2)),
-        ],
+        (quad, quad, shape(*gate_weight.shape)),
+        pinned,
+        [pltpu.VMEM((4, count, heads, width), BF16), pltpu.SemaphoreType.DMA((5,))],
         3.0,
-        in_specs=[HBM] * 4,
-        out_specs=(HBM, HBM),
-        limit=60 * 1024 * 1024,
+        in_specs=[HBM] * 5,
     )
     if direct:
         nearby = lax.ppermute(gate_weight, "dp", [(i, i ^ 1) for i in range(parts)])
         nearby, send = lax.optimization_barrier((nearby, send))
-        two = jnp.stack([gate_weight, nearby])
-        gates = [two] + [
-            lax.ppermute(two, "dp", [(i, i ^ far) for i in range(parts)]) for far in range(2, parts, 2)
+        two = jnp.stack([gate_copy, nearby])
+        gates = [
+            lax.ppermute(two, "dp", [(i, i ^ far) for i in range(parts)])
+            for far in (4, 6, 2)
         ]
     else:
         gates = [lax.all_gather(gate_weight, "dp", axis=1, tiled=True)]
@@ -408,6 +393,8 @@
         product_kernel, "products", (shape(half, count, count, dtype=F32),), (keep,), (), 1.0
     )
     *gates, products = lax.optimization_barrier((*gates, products))
+    if direct:
+        gates = [two, gates[2], gates[0], gates[1]]
 
     sides = 1 if pair else 2
     lines = pltpu.VMEM((2, heads, count), F32)
@@ -430,8 +417,8 @@
     )
 
     attn_shape = shape(sides, 2, half, width, count, dtype=F32)
-    mine_shape = shape(sides, half, count, width)
-    send_shape = shape(sides, half + 1, count, width)
+    mine_shape = shape(sides, half, width, count)
+    send_shape = shape(sides, half + 1, width, count)
     slope_shape = shape(2, half, count, dtype=F32)
 
     def inside(*outs):
@@ -465,17 +452,15 @@
         kappa = across_chips(kappa, jnp.ones((half, 1), F32), ranks, False)
         more = ()
         local = ()
-    full, suffix, pieces = call(
+    mine, send, suffix, pieces = call(
         functools.partial(outside_kernel, pair),
         "outside_block",
-        (shape(sides, 2, half, width, count), slope_shape, shape(parts * ranks, 2, width, dtype=F32)),
+        (mine_shape, send_shape, shape(half, count, dtype=F32), shape(parts * ranks, 2, width, dtype=F32)),
         (keep, recv, rows, states, near, attn, kappa, *more),
         [lines],
         1.5,
     )
     pieces = lax.all_to_all(pieces, ("dp", "ctx"), 0, 0, tiled=True)
-
-    mine, send = call(turn_kernel, "turn_planes", (mine_shape, send_shape), (full, suffix, rows), (), 1.0)
     recv_out = lax.ppermute(send, "ctx", swap)
     whole = shape(1, count, heads, width)
     query_grad, key_part, out_lines = call(
@@ -491,9 +476,13 @@
         "key_gradient",
         (whole, shape(heads, width // parts, dtype=F32)),
         (out_lines, key_part, gate_full, pieces),
-        [pltpu.VMEM((count, heads, width), BF16), pltpu.SemaphoreType.DMA((4,))],
+        [
+            pltpu.VMEM((count, heads, width), BF16),
+            pltpu.VMEM((heads, width // parts), F32),
+            pltpu.SemaphoreType.DMA((2,)),
+        ],
         1.0,
-        out_specs=(ANY, VMEM),
+        out_specs=(ANY, ANY),
     )
     return query_grad, key_grad, gate_grad
 

time: 39.5 us -> 37.9 us (0.959)
  local copies, waits for them, and re-layouts: 1.9 us -> 0.07 us
  Pallas kernels: 13 us -> 11.4 us
  starting transfers between devices: 13 us -> 14 us
  waiting for transfers between devices: 10.7 us -> 11.5 us
    unnamed x8 -> x2, local copies, waits for them, and re-layouts: 1.82 us -> 0.01 us
    pallas_call x10 -> x9, Pallas kernels: 13 us -> 11.4 us  [call(): pl.pallas_call(kernel, out_shape=out_shape, in_specs=in_specs or [VMEM] *...]
    all_to_all x1, starting transfers between devices: 3.23 us -> 4.39 us  [per_device(): pieces = lax.all_to_all(pieces, ('dp', 'ctx'), 0, 0, tiled=True)]
    ppermute x1, waiting for transfers between devices: 1.71 us -> 2.52 us  [per_device(): kappa = lax.ppermute(kappa, 'ctx', opposite)]
  transfers between devices with their start and end apart: 10 -> 10, of which waited for: 4 -> 3; matrix products, arithmetic and copies ran while one was open for 0% -> 0% of each run, Pallas kernels for 26% -> 24%
where the time goes in v3:
time: 37.9 us; the launch traced here: 37.8 us
  starting transfers between devices  14 us (37%)
  waiting for transfers between devices  11.5 us (30%)
  Pallas kernels  11.4 us (30%)
  between operations  0.73 us (2%)
    pallas_call x9, Pallas kernels, call(): pl.pallas_call(kernel, out_shape=out_shape, in_specs=in_specs or [VMEM] *...  11.4 us
    all_to_all x1, waiting for transfers between devices, per_device(): pieces = lax.all_to_all(pieces, ('dp', 'ctx'), 0, 0, tiled=True)  5.39 us
    all_to_all x1, starting transfers between devices, per_device(): pieces = lax.all_to_all(pieces, ('dp', 'ctx'), 0, 0, tiled=True)  4.39 us
    ppermute x3, starting transfers between devices, per_device(): lax.ppermute(two, 'dp', [(i, i ^ far) for i in range(parts)])  4.35 us
    ppermute x3, waiting for transfers between devices, per_device(): lax.ppermute(two, 'dp', [(i, i ^ far) for i in range(parts)])  3.57 us
    ppermute x1, starting transfers between devices, per_device(): nearby = lax.ppermute(gate_weight, 'dp', [(i, i ^ 1) for i in range(parts)])  3.03 us
    ppermute x1, waiting for transfers between devices, per_device(): kappa = lax.ppermute(kappa, 'ctx', opposite)  2.52 us
    ppermute x1, starting transfers between devices, per_device(): states = lax.ppermute(total, 'ctx', opposite)  1.56 us
  transfers between devices with their start and end apart: 10, of which 3 were waited for; matrix products, arithmetic and copies ran while one was open for 0% of the time, Pallas kernels for 24%

profile of v3, /device:TPU:0, one launch (start us, length us, event | category | flops | bytes accessed | tf_op | source)
XLA Modules:
  0.0 37.8 jit_solution(8416224167850188661)
XLA Ops:
  0.6 3.0 %collective-permute-start = (bf16[16,16]{1,0:T(8,128)(2,1)}, bf16[16,16]{1,0:T(8,128)(2,1)S(1)}, u32[]{:S(2)}, u32[]{:S(2)}) collective-permute-start(bf16[16,16]{1,0:T(8,128)(2,1)} %gate_ref.1), channel_id=1, source_target_pairs={{0,4},{4,0},{8,12},{12,8},{16,20},{20,16},{24,28},{28,24},{1,5},{5... | collective-permute-start | bytes 1544 | tf_op jit(solution)/shard_map/ppermute | solution.py:382
  3.7 2.1 %split_heads.1 = (bf16[4,8,128,128]{3,2,1,0:T(8,128)(2,1)S(1)}, bf16[4,8,128,128]{3,2,1,0:T(8,128)(2,1)S(1)}, bf16[16,16]{1,0:T(8,128)(2,1)S(1)}) custom-call(bf16[1,128,16,128]{3,2,1,0:T(8,128)(2,1)} %k_ref.1, bf16[1,128,16,128]{3,2,1,0:T(8,128)(2,1)} %q_ref.1, bf16[1,128,16,128]{3,2,1,0:T(8,128)(2,1)} %v_ref.1, bf16[1,128,16,128]{3,2,1,0:T(8,128)(2,1)} %g_ref.1, ...), custom_call_target="tpu_custom_call" | custom-call | bytes 9000000 | tf_op jit(solution)/shard_map/split_heads/pallas_call | solution.py:48
  5.8 0.1 collective-permute-start.1
  5.9 2.8 %collective-permute-start.2 = (bf16[2,16,16]{2,1,0:T(8,128)(2,1)S(1)}, bf16[2,16,16]{2,1,0:T(8,128)(2,1)S(1)}, u32[]{:S(2)}, u32[]{:S(2)}) collective-permute-start(bf16[2,16,16]{2,1,0:T(8,128)(2,1)S(1)} %pad_maximum_fusion.refs_0_), channel_id=1, source_target_pairs={{0,16},{4,20},{8,24},{12,28},{16,0},{20,4},{24,8},{28,12},{1,17},{... | collective-permute-start | bytes 3080 | tf_op jit(solution)/shard_map/ppermute | solution.py:386
  8.6 1.3 %collective-permute-start.3 = (bf16[2,16,16]{2,1,0:T(8,128)(2,1)S(1)}, bf16[2,16,16]{2,1,0:T(8,128)(2,1)S(1)}, u32[]{:S(2)}, u32[]{:S(2)}) collective-permute-start(bf16[2,16,16]{2,1,0:T(8,128)(2,1)S(1)} %pad_maximum_fusion.refs_0_), channel_id=1, source_target_pairs={{0,24},{4,28},{8,16},{12,20},{16,8},{20,12},{24,0},{28,4},{1,25},{... | collective-permute-start | bytes 3080 | tf_op jit(solution)/shard_map/ppermute | solution.py:386
  10.0 0.2 collective-permute-start.4
  10.2 0.3 products.1.product_ref
  10.5 0.0 collective-permute-done.2.refs_2_
  10.5 3.6 %collective-permute-done.3.refs_3_ = bf16[2,16,16]{2,1,0:T(8,128)(2,1)S(1)} collective-permute-done((bf16[2,16,16]{2,1,0:T(8,128)(2,1)S(1)}, bf16[2,16,16]{2,1,0:T(8,128)(2,1)S(1)}, u32[]{:S(2)}, u32[]{:S(2)}) %collective-permute-start.3) | collective-permute-done | bytes 1056 | tf_op jit(solution)/shard_map/ppermute | solution.py:386
  14.1 0.1 broadcast_in_dim.2.refs_4_
  14.2 0.1 gate_weights.1.gate_ref
  14.3 0.9 %gate_states.1 = (bf16[1,8,128,128]{3,2,1,0:T(8,128)(2,1)S(1)}, bf16[1,8,128,128]{3,2,1,0:T(8,128)(2,1)S(1)}, f32[2,16,128]{2,1,0:T(8,128)S(1)}) custom-call(f32[2,16,128]{2,1,0:T(8,128)S(1)} %gate_weights.1.gate_ref, bf16[4,8,128,128]{3,2,1,0:T(8,128)(2,1)S(1)} %get-tuple-element.29.keep_ref, bf16[4,8,128,128]{3,2,1,0:T(8,128)(2,1)S(1)} %collective-permute-done.1.recv_ref), custom_call_target="tpu_custom_call" | custom-call | bytes 3900000 | tf_op jit(solution)/shard_map/gate_states/pallas_call | solution.py:48
  15.2 1.6 %collective-permute-start.5 = (bf16[1,8,128,128]{3,2,1,0:T(8,128)(2,1)S(1)}, bf16[1,8,128,128]{3,2,1,0:T(8,128)(2,1)S(1)}, u32[]{:S(2)}, u32[]{:S(2)}) collective-permute-start(bf16[1,8,128,128]{3,2,1,0:T(8,128)(2,1)S(1)} %get-tuple-element.38), channel_id=1, source_target_pairs={{0,2},{1,3},{2,0},{3,1},{4,6},{5,7},{6,4},{7,5},{8,10},{9,11},{10,... | collective-permute-start | bytes 786440 | tf_op jit(solution)/shard_map/ppermute | solution.py:439
  16.8 0.4 kappa.1
  17.1 0.6 %collective-permute-start.6 = (f32[8,128]{1,0:T(8,128)S(1)}, f32[8,128]{1,0:T(8,128)S(1)}, u32[]{:S(2)}, u32[]{:S(2)}) collective-permute-start(f32[8,128]{1,0:T(8,128)S(1)} %kappa.1), channel_id=1, source_target_pairs={{0,2},{1,3},{2,0},{3,1},{4,6},{5,7},{6,4},{7,5},{8,10},{9,11},{10,... | collective-permute-start | bytes 12296 | tf_op jit(solution)/shard_map/ppermute | solution.py:442
  17.7 2.3 %inside_block.1 = (f32[1,2,8,128,128]{4,3,2,1,0:T(8,128)S(1)}, f32[1,8,128,128]{3,2,1,0:T(8,128)S(1)}, bf16[1,8,128,128]{3,2,1,0:T(8,128)(2,1)S(1)}, bf16[1,9,12...) custom-call(bf16[4,8,128,128]{3,2,1,0:T(8,128)(2,1)S(1)} %get-tuple-element.29.keep_ref, ...), custom_call_target="tpu_custom_call" | custom-call | bytes 12000000 | tf_op jit(solution)/shard_map/inside_block/pallas_call | solution.py:48
  20.0 0.1 collective-permute-start.7
  20.1 2.5 %collective-permute-done.6.kappa_ref = f32[8,128]{1,0:T(8,128)S(1)} collective-permute-done((f32[8,128]{1,0:T(8,128)S(1)}, f32[8,128]{1,0:T(8,128)S(1)}, u32[]{:S(2)}, u32[]{:S(2)}) %collective-permute-start.6) | collective-permute-done | bytes 4128 | tf_op jit(solution)/shard_map/ppermute | solution.py:442
  22.6 2.1 %outside_block.1 = (bf16[1,8,128,128]{3,2,1,0:T(8,128)(2,1)S(1)}, bf16[1,9,128,128]{3,2,1,0:T(8,128)(2,1)S(1)}, f32[8,128]{1,0:T(8,128)S(1)}, f32[32,2,128]{2,1,0:T(2,128)}) custom-call(bf16[4,8,128,128]{3,2,1,0:T(8,128)(2,1)S(1)} %get-tuple-element.29.keep_ref, bf16[4,8,128,128]{3,2,1,0:T(8,128)(2,1)S(1)} %collective-permute-done.1.recv_ref, ...), custom_call_target="tpu_custom_call" | custom-call | bytes 4500000 | tf_op jit(solution)/shard_map/outside_block/pallas_call | solution.py:48
  24.6 4.4 %all-to-all-start = ((f32[32,2,128]{2,1,0:T(2,128)}), f32[32,2,128]{2,1,0:T(2,128)S(1)}, u32[]{:S(2)}, u32[]{:S(2)}) async-start(f32[32,2,128]{2,1,0:T(2,128)} %get-tuple-element.52), calls=%async_computation | async-start | bytes 65536 | tf_op jit(solution)/shard_map/all_to_all | solution.py:463
  29.1 0.0 collective-permute-done.8.refs_3_
  29.1 1.8 %merge_heads.1 = (bf16[1,128,16,128]{3,2,1,0:T(8,128)(2,1)}, bf16[1,128,16,128]{3,2,1,0:T(8,128)(2,1)S(1)}, f32[2,16,128]{2,1,0:T(8,128)S(1)}) custom-call(f32[8,128]{1,0:T(8,128)S(1)} %get-tuple-element.44.suffix_ref, f32[2,16,128]{2,1,0:T(8,128)S(1)} %get-tuple-element.37.rows_ref, bf16[1,8,128,128]{3,2,1,0:T(8,128)(2,1)S(1)} %get-tuple-element.45.refs_0_, ...), custom_call_target="tpu_custom_call" | custom-call | bytes 6000000 | tf_op jit(solution)/shard_map/merge_heads/pallas_call | solution.py:48
  30.9 5.4 %all-to-all-done.pieces_ref = f32[32,2,128]{2,1,0:T(2,128)S(1)} async-done(((f32[32,2,128]{2,1,0:T(2,128)}), f32[32,2,128]{2,1,0:T(2,128)S(1)}, u32[]{:S(2)}, u32[]{:S(2)}) %all-to-all-start) | async-done | bytes 32800 | tf_op jit(solution)/shard_map/all_to_all | solution.py:463
  36.3 1.5 %key_gradient.1 = (bf16[1,128,16,128]{3,2,1,0:T(8,128)(2,1)}, f32[16,16]{1,0:T(8,128)}) custom-call(f32[2,16,128]{2,1,0:T(8,128)S(1)} %get-tuple-element.50.lines_ref, bf16[1,128,16,128]{3,2,1,0:T(8,128)(2,1)S(1)} %get-tuple-element.51.key_ref, f32[2,16,128]{2,1,0:T(8,128)S(1)} %gate_weights.1.gate_ref, f32[32,2,128]{2,1,0:T(2,128)S(1)} %all-to-all-done.pieces_ref), custom_call_target="tpu_custom_call" | custom-call | bytes 3000000 | tf_op jit(solution)/shard_map/key_gradient/pallas_call | solution.py:48
  (9 shorter events, 0.0 us)
Async XLA Ops:
  0.6 5.1 %collective-permute-start = (bf16[16,16]{1,0:T(8,128)(2,1)}, bf16[16,16]{1,0:T(8,128)(2,1)S(1)}, u32[]{:S(2)}, u32[]{:S(2)}) collective-permute-start(bf16[16,16]{1,0:T(8,128)(2,1)} %gate_ref.1), channel_id=1, source_target_pairs={{0,4},{4,0},{8,12},{12,8},{16,20},{20,16},{24,28},{28,24},{1,5},{5... | collective-permute-start | bytes 1544 | tf_op jit(solution)/shard_map/ppermute | solution.py:382
  5.8 8.5 %collective-permute-start.1 = (bf16[4,8,128,128]{3,2,1,0:T(8,128)(2,1)S(1)}, bf16[4,8,128,128]{3,2,1,0:T(8,128)(2,1)S(1)}, u32[]{:S(2)}, u32[]{:S(2)}) collective-permute-start(bf16[4,8,128,128]{3,2,1,0:T(8,128)(2,1)S(1)} %get-tuple-element.31), channel_id=1, source_target_pairs={{0,1},{1,0},{2,3},{3,2},{4,5},{5,4},{6,7},{7,6},{8,9},{9,8},{10,11... | collective-permute-start | bytes 3145736 | tf_op jit(solution)/shard_map/ppermute | solution.py:391
  5.9 4.7 %collective-permute-start.2 = (bf16[2,16,16]{2,1,0:T(8,128)(2,1)S(1)}, bf16[2,16,16]{2,1,0:T(8,128)(2,1)S(1)}, u32[]{:S(2)}, u32[]{:S(2)}) collective-permute-start(bf16[2,16,16]{2,1,0:T(8,128)(2,1)S(1)} %pad_maximum_fusion.refs_0_), channel_id=1, source_target_pairs={{0,16},{4,20},{8,24},{12,28},{16,0},{20,4},{24,8},{28,12},{1,17},{... | collective-permute-start | bytes 3080 | tf_op jit(solution)/shard_map/ppermute | solution.py:386
  8.6 5.4 %collective-permute-start.3 = (bf16[2,16,16]{2,1,0:T(8,128)(2,1)S(1)}, bf16[2,16,16]{2,1,0:T(8,128)(2,1)S(1)}, u32[]{:S(2)}, u32[]{:S(2)}) collective-permute-start(bf16[2,16,16]{2,1,0:T(8,128)(2,1)S(1)} %pad_maximum_fusion.refs_0_), channel_id=1, source_target_pairs={{0,24},{4,28},{8,16},{12,20},{16,8},{20,12},{24,0},{28,4},{1,25},{... | collective-permute-start | bytes 3080 | tf_op jit(solution)/shard_map/ppermute | solution.py:386
  10.0 4.1 %collective-permute-start.4 = (bf16[2,16,16]{2,1,0:T(8,128)(2,1)S(1)}, bf16[2,16,16]{2,1,0:T(8,128)(2,1)S(1)}, u32[]{:S(2)}, u32[]{:S(2)}) collective-permute-start(bf16[2,16,16]{2,1,0:T(8,128)(2,1)S(1)} %pad_maximum_fusion.refs_0_), channel_id=1, source_target_pairs={{0,8},{4,12},{8,0},{12,4},{16,24},{20,28},{24,16},{28,20},{1,9},{5... | collective-permute-start | bytes 3080 | tf_op jit(solution)/shard_map/ppermute | solution.py:386
  10.2 3.9 %copy-start = (bf16[16]{0:T(256)(128)(2,1)S(1)}, bf16[16]{0:T(256)(128)(2,1)}, u32[]{:S(2)}) copy-start(bf16[16]{0:T(256)(128)(2,1)} %param.11) | copy-start | bytes 100
  15.2 7.4 %collective-permute-start.5 = (bf16[1,8,128,128]{3,2,1,0:T(8,128)(2,1)S(1)}, bf16[1,8,128,128]{3,2,1,0:T(8,128)(2,1)S(1)}, u32[]{:S(2)}, u32[]{:S(2)}) collective-permute-start(bf16[1,8,128,128]{3,2,1,0:T(8,128)(2,1)S(1)} %get-tuple-element.38), channel_id=1, source_target_pairs={{0,2},{1,3},{2,0},{3,1},{4,6},{5,7},{6,4},{7,5},{8,10},{9,11},{10,... | collective-permute-start | bytes 786440 | tf_op jit(solution)/shard_map/ppermute | solution.py:439
  17.1 5.4 %collective-permute-start.6 = (f32[8,128]{1,0:T(8,128)S(1)}, f32[8,128]{1,0:T(8,128)S(1)}, u32[]{:S(2)}, u32[]{:S(2)}) collective-permute-start(f32[8,128]{1,0:T(8,128)S(1)} %kappa.1), channel_id=1, source_target_pairs={{0,2},{1,3},{2,0},{3,1},{4,6},{5,7},{6,4},{7,5},{8,10},{9,11},{10,... | collective-permute-start | bytes 12296 | tf_op jit(solution)/shard_map/ppermute | solution.py:442
  20.0 9.1 %collective-permute-start.7 = (bf16[1,9,128,128]{3,2,1,0:T(8,128)(2,1)S(1)}, bf16[1,9,128,128]{3,2,1,0:T(8,128)(2,1)S(1)}, u32[]{:S(2)}, u32[]{:S(2)}) collective-permute-start(bf16[1,9,128,128]{3,2,1,0:T(8,128)(2,1)S(1)} %get-tuple-element.46), channel_id=1, source_target_pairs={{0,1},{1,0},{2,3},{3,2},{4,5},{5,4},{6,7},{7,6},{8,9},{9,8},{10,11... | collective-permute-start | bytes 884744 | tf_op jit(solution)/shard_map/ppermute | solution.py:443
  24.6 4.4 %collective-permute-start.8 = (bf16[1,9,128,128]{3,2,1,0:T(8,128)(2,1)S(1)}, bf16[1,9,128,128]{3,2,1,0:T(8,128)(2,1)S(1)}, u32[]{:S(2)}, u32[]{:S(2)}) collective-permute-start(bf16[1,9,128,128]{3,2,1,0:T(8,128)(2,1)S(1)} %get-tuple-element.48), channel_id=1, source_target_pairs={{0,1},{1,0},{2,3},{3,2},{4,5},{5,4},{6,7},{7,6},{8,9},{9,8},{10,11... | collective-permute-start | bytes 884744 | tf_op jit(solution)/shard_map/ppermute | solution.py:464
  24.6 11.6 %all-to-all-start = ((f32[32,2,128]{2,1,0:T(2,128)}), f32[32,2,128]{2,1,0:T(2,128)S(1)}, u32[]{:S(2)}, u32[]{:S(2)}) async-start(f32[32,2,128]{2,1,0:T(2,128)} %get-tuple-element.52), calls=%async_computation | async-start | bytes 65536 | tf_op jit(solution)/shard_map/all_to_all | solution.py:463

commit v4 on v3

--- a/solution.py
+++ b/solution.py
@@ -23,10 +23,15 @@
     return lax.dot_general(a, b, (((1,), (1,)), ((), ())), preferred_element_type=F32)
 
 
-def exact(a, b):
-    return lax.dot_general(
-        a, b, (((1,), (0,)), ((), ())), precision=lax.Precision.HIGHEST, preferred_element_type=F32
-    )
+def exact(rows, mask):
+    count = rows.shape[0]
+    parts, rest = [], rows
+    for _ in range(3):
+        part = rest.astype(BF16)
+        parts.append(part)
+        rest = rest - part.astype(F32)
+    out = nn(jnp.concatenate(parts, 0), jnp.where(mask, 1.0, 0.0).astype(BF16))
+    return out[:count] + (out[count : 2 * count] + out[2 * count :])
 
 
 def iota(shape, dim):
@@ -87,39 +92,40 @@
     return jnp.exp(end - rows), jnp.exp(rows), jnp.exp(end)
 
 
-def weight_kernel(direct, *refs):
-    *gates, bias_ref, gate_ref = refs
-    heads, width = gate_ref.shape[1:]
-    if direct:
-        index = lax.axis_index("dp")
-        full = jnp.zeros((heads, width), F32)
-        for r, ref in enumerate(gates):
-            for low in range(2):
-                piece = ref.shape[2]
-                owner = jnp.bitwise_xor(index, 2 * r + low)
-                pick = iota((piece, width), 1) == iota((piece, width), 0) + owner * piece
-                full = full + nn(ref[low], jnp.where(pick, 1.0, 0.0).astype(BF16))
-    else:
-        full = gates[0][...].astype(F32)
-    gate_ref[0] = full
-    gate_ref[1] = bias_ref[...]
-
-
-def gate_kernel(pair, gate_ref, keep_ref, recv_ref, total_ref, near_ref, rows_ref, scale_ref):
+def whole_gate(direct, gates):
+    index = lax.axis_index("dp")
+    if not direct:
+        return gates[0][...].astype(F32)
+    heads, piece = gates[0].shape[1:]
+    width = piece * lax.axis_size("dp")
+    full = jnp.zeros((heads, width), F32)
+    for r, ref in enumerate(gates):
+        for low in range(2):
+            owner = jnp.bitwise_xor(index, 2 * r + low)
+            pick = iota((piece, width), 1) == iota((piece, width), 0) + owner * piece
+            full = full + nn(ref[low], jnp.where(pick, 1.0, 0.0).astype(BF16))
+    return full
+
+
+def gate_kernel(direct, pair, *refs):
+    *gates, bias_ref, keep_ref, recv_ref, total_ref, near_ref, rows_ref, gate_ref, scale_ref = refs
     par, chip = place()
     _, half, width, count = keep_ref.shape
-    weights = gate_ref[0, pl.ds(par * half, half), :].astype(BF16)
+    gate_ref[0] = whole_gate(direct, gates)
+    same = iota((2 * half, 2 * half), 0) == iota((2 * half, 2 * half), 1)
+    spread = jnp.where(same, bias_ref[...].astype(F32), 0.0).astype(BF16)
+    gate_ref[1] = nn(spread, jnp.ones((2 * half, width), BF16))
+    weights = gate_ref[0, pl.ds(par * half, half), :]
     bias = gate_ref[1, pl.ds(par * half, half), :]
-    row = iota((half, count), 0)
-    logits = []
-    for ref in (keep_ref, recv_ref):
-        logit = bias
-        for j in range(half):
-            logit = logit + jnp.where(row == j, nn(weights, ref[0, j]), 0.0)
-        logits.append(logit)
-    logit = jnp.concatenate(logits, 0)
+    row, side_of = iota((half, 2 * width), 0), iota((half, 2 * width), 1) // width
+    twice = jnp.concatenate([weights, weights], 1)
+    logit = jnp.zeros((half, 2 * count), F32)
+    for j in range(0, half, 2):
+        planes = [ref[0, j : j + 2].reshape(2 * width, count) for ref in (keep_ref, recv_ref)]
+        logit = logit + nn(jnp.where(row == j + side_of, twice, 0.0).astype(BF16), jnp.concatenate(planes, 1))
+    logit = jnp.concatenate([bias + logit[:, :count], bias + logit[:, count:]], 0)
     decay = -(jnp.maximum(logit, 0.0) + jnp.log1p(jnp.exp(-jnp.abs(logit))))
-    cumul = exact(decay, jnp.where(iota((count, count), 0) <= iota((count, count), 1), 1.0, 0.0))
+    cumul = exact(decay, iota((count, count), 0) <= iota((count, count), 1))
     rows_ref[0] = cumul
     rows_ref[1] = -1.0 / (1.0 + jnp.exp(-logit))
     tail, head, ends = scales(cumul)
@@ -142,13 +148,16 @@
             near_ref[at, j] = jnp.where(enters, own, other).astype(near_ref.dtype)
 
 
-def weighted_keys(ref, rows):
-    half = rows.shape[0]
-    lhs = hi_lo(rows)
-    row = iota(lhs.shape, 0)
-    total = jnp.zeros(lhs.shape, F32)
-    for j in range(half):
-        total = total + jnp.where((row == j) | (row == j + half), nt(lhs, ref[0, j]), 0.0)
+def weighted_keys(keep_ref, recv_ref, own, other):
+    half, count = own.shape
+    width = keep_ref.shape[2]
+    lhs = jnp.concatenate([hi_lo(own), hi_lo(other)], 1)
+    row = iota((2 * half, width), 0) % half
+    total = jnp.zeros((2 * half, width), F32)
+    for j in range(0, half, 2):
+        planes = [ref[0, j : j + 2].reshape(2 * width, count) for ref in (keep_ref, recv_ref)]
+        got = nt(lhs, jnp.concatenate(planes, 1))
+        total = total + jnp.where(row == j, got[:, :width], 0.0) + jnp.where(row == j + 1, got[:, width:], 0.0)
     return total[:half] + total[half:]
 
 
@@ -164,7 +173,7 @@
 
 def kappa_kernel(keep_ref, recv_ref, rows_ref, kappa_ref):
     half = kappa_ref.shape[0]
-    kappa_ref[...] = weighted_keys(keep_ref, rows_ref[1, :half, :]) + weighted_keys(recv_ref, rows_ref[1, half:, :])
+    kappa_ref[...] = weighted_keys(keep_ref, recv_ref, rows_ref[1, :half, :], rows_ref[1, half:, :])
 
 
 def inside_kernel(pair, keep_ref, recv_ref, rows_ref, near_ref, product_ref, attn_ref, *refs):
@@ -239,10 +248,9 @@
             enters = block == side
             lines = []
             for j in range(half):
-                come = state_ref[at, j].astype(F32)
                 passed = (1 - rel) * half + j
-                ratio = jnp.where(enters, 1.0, ends[passed : passed + 1])
-                known = ratio * come + jnp.where(enters, 0.0, 1.0) * near_ref[at, j]
+                moved = ends[passed : passed + 1] * state_ref[at, j].astype(F32) + near_ref[at, j]
+                known = jnp.where(enters, state_ref[at, j].astype(F32), moved)
                 cross = nt(known.astype(BF16), ref[3 - side, j])
                 factor = const * scale_ref[1 - side, rel * half + j : rel * half + j + 1, :]
                 full = attn_ref[at, rel, j] + factor * cross
@@ -251,7 +259,7 @@
             slopes = slopes + jnp.concatenate(lines, 0)
         all_slopes.append(slopes)
     slope = jnp.concatenate(all_slopes, 0)
-    suffix = exact(slope, jnp.where(iota((count, count), 0) >= iota((count, count), 1), 1.0, 0.0))
+    suffix = exact(slope, iota((count, count), 0) >= iota((count, count), 1))
     sums = jnp.broadcast_to(suffix[:, :1], suffix.shape)
     first = jnp.where(par == 0, 1.0, 0.0)
     mine = suffix[:half] + first * sums[half:]
@@ -266,8 +274,7 @@
     total = sums[:half] + sums[half:]
     before = jnp.where(chip == 1, 1.0, 0.0) if pair else 1.0
     partial = (
-        weighted_keys(keep_ref, mine * rows_ref[1, :half, :])
-        + weighted_keys(recv_ref, other * rows_ref[1, half:, :])
+        weighted_keys(keep_ref, recv_ref, mine * rows_ref[1, :half, :], other * rows_ref[1, half:, :])
         + before * (total * kappa_ref[...])
     )
     parts = lax.axis_size("dp")
@@ -283,12 +290,12 @@
         pieces_ref[pl.ds(i * ranks, ranks)] = jnp.broadcast_to(sent[None], (ranks, 2, width))
 
 
-def merge_kernel(pair, suffix_ref, rows_ref, *refs):
+def merge_kernel(pair, gate_ref, suffix_ref, rows_ref, *refs):
     if pair:
-        mine0, recv0, mine1, recv1, query_ref, key_ref, line_ref, tmp = refs
+        mine0, recv0, mine1, recv1, query_ref, base_ref, rise_ref, line_ref, tmp = refs
         sources = ((mine0, recv0, 0), (mine1, recv1, 0))
     else:
-        mine0, recv0, query_ref, key_ref, line_ref, tmp = refs
+        mine0, recv0, query_ref, base_ref, rise_ref, line_ref, tmp = refs
         sources = ((mine0, recv0, 0), (mine0, recv0, 1))
     par, chip = place()
     _, count, heads, width = query_ref.shape
@@ -303,12 +310,18 @@
     line_ref[1, pl.ds(par * half, half), :] = suffix_ref[...]
     first = chip if pair else 0
     query_ref[0] = tmp[first].reshape(count, heads, width).astype(BF16)
-    key_ref[0] = tmp[1 - first].reshape(count, heads, width).astype(BF16)
-
-
-def last_kernel(lines_ref, key_ref, gate_ref, pieces_ref, out_ref, grad_ref, buf, small, sems):
+    rise = line_ref[0]
+    slope = rise * line_ref[1]
+    gate = gate_ref[0]
+    for t in range(count):
+        known = tmp[1 - first, t * heads : (t + 1) * heads, :]
+        base_ref[t] = known + slope[:, t : t + 1] * gate
+        rise_ref[t] = rise[:, t : t + 1] * gate
+
+
+def last_kernel(base_ref, rise_ref, pieces_ref, out_ref, grad_ref, buf, small, sems):
     _, chip = place()
-    _, count, heads, width = key_ref.shape
+    count, heads, width = base_ref.shape
     half = heads // 2
     parts, ranks = lax.axis_size("dp"), lax.axis_size("ctx")
     groups, slot = ranks // 2, width // half
@@ -318,15 +331,13 @@
     chosen = [
         jnp.sum(jnp.where(lane == sub * slot, beyond[c : c + 1], 0.0), 1, keepdims=True) for c in range(2)
     ]
-    after = jnp.concatenate(chosen, 0)
-    slope = lines_ref[0] * (lines_ref[1] + after)
-    gate = gate_ref[0]
+    after = jnp.broadcast_to(jnp.concatenate(chosen, 0), (heads, width))
     for t in range(count):
-        buf[t] = (key_ref[0, t].astype(F32) + slope[:, t : t + 1] * gate).astype(BF16)
+        buf[t] = (base_ref[t] + after * rise_ref[t]).astype(BF16)
     key_copy = pltpu.make_async_copy(buf, out_ref.at[0], sems.at[0])
     key_copy.start()
     total = jnp.sum(pieces_ref[...].reshape(parts * groups, 2, 2, width)[:, :, 0], 0)
-    fold = jnp.where(iota((width, slot), 0) % slot == iota((width, slot), 1), 1.0, 0.0)
+    fold = iota((width, slot), 0) % slot == iota((width, slot), 1)
     lines = [jnp.where(lane // slot == sub, total[c : c + 1], 0.0) for c in range(2)]
     small[...] = exact(jnp.concatenate(lines, 0), fold)[:, : width // parts]
     grad_copy = pltpu.make_async_copy(small, grad_ref, sems.at[1])
@@ -362,7 +373,7 @@
     def shape(*dims, dtype=BF16):
         return jax.ShapeDtypeStruct(dims, dtype)
 
-    bias = jnp.broadcast_to(head_bias.astype(F32)[:, None], (heads, width))
+    bias = head_bias.reshape(1, heads)
 
     quad = shape(4, half, width, count)
     pinned = [
@@ -384,7 +395,7 @@
         two = jnp.stack([gate_copy, nearby])
         gates = [
             lax.ppermute(two, "dp", [(i, i ^ far) for i in range(parts)])
-            for far in (4, 6, 2)
+            for far in (2, 6, 4)
         ]
     else:
         gates = [lax.all_gather(gate_weight, "dp", axis=1, tiled=True)]
@@ -394,24 +405,16 @@
     )
     *gates, products = lax.optimization_barrier((*gates, products))
     if direct:
-        gates = [two, gates[2], gates[0], gates[1]]
+        gates = [two, gates[0], gates[2], gates[1]]
 
     sides = 1 if pair else 2
     lines = pltpu.VMEM((2, heads, count), F32)
     state = shape(sides, half, width, width, dtype=BF16 if pair else F32)
-    (gate_full,) = call(
-        functools.partial(weight_kernel, direct),
-        "gate_weights",
-        (shape(2, heads, width, dtype=F32),),
-        (*gates, bias),
-        (),
-        10.0,
-    )
-    total, near, rows = call(
-        functools.partial(gate_kernel, pair),
+    total, near, rows, gate_full = call(
+        functools.partial(gate_kernel, direct, pair),
         "gate_states",
-        (state, state, shape(2, heads, count, dtype=F32)),
-        (gate_full, keep, recv),
+        (state, state, shape(2, heads, count, dtype=F32), shape(2, heads, width, dtype=F32)),
+        (*gates, bias, keep, recv),
         [lines],
         1.3,
     )
@@ -463,19 +466,20 @@
     pieces = lax.all_to_all(pieces, ("dp", "ctx"), 0, 0, tiled=True)
     recv_out = lax.ppermute(send, "ctx", swap)
     whole = shape(1, count, heads, width)
-    query_grad, key_part, out_lines = call(
+    plain = shape(count, heads, width, dtype=F32)
+    query_grad, base, rise = call(
         functools.partial(merge_kernel, pair),
         "merge_heads",
-        (whole, whole, shape(2, heads, count, dtype=F32)),
-        (suffix, rows, *local, mine, recv_out),
-        [pltpu.VMEM((2, count * heads, width), F32)],
+        (whole, plain, plain),
+        (gate_full, suffix, rows, *local, mine, recv_out),
+        [pltpu.VMEM((2, heads, count), F32), pltpu.VMEM((2, count * heads, width), F32)],
         2.0,
     )
     key_grad, gate_grad = call(
         last_kernel,
         "key_gradient",
         (whole, shape(heads, width // parts, dtype=F32)),
-        (out_lines, key_part, gate_full, pieces),
+        (base, rise, pieces),
         [
             pltpu.VMEM((count, heads, width), BF16),
             pltpu.VMEM((heads, width // parts), F32),

time: 37.9 us -> 36.7 us (0.968)
  Pallas kernels: 11.4 us -> 10.6 us
  starting transfers between devices: 14 us -> 13.4 us
    pallas_call x9 -> x8, Pallas kernels: 11.4 us -> 10.6 us  [call(): pl.pallas_call(kernel, out_shape=out_shape, in_specs=in_specs or [VMEM] *...]
    all_to_all x1, starting transfers between devices: 4.39 us -> 3.81 us  [per_device(): pieces = lax.all_to_all(pieces, ('dp', 'ctx'), 0, 0, tiled=True)]
    ppermute x3, waiting for transfers between devices: 3.57 us -> 4.12 us  [per_device(): lax.ppermute(two, 'dp', [(i, i ^ far) for i in range(parts)])]
  transfers between devices with their start and end apart: 10 -> 10, of which waited for: 3 -> 4; matrix products, arithmetic and copies ran while one was open for 0% -> 0% of each run, Pallas kernels for 24% -> 24%
where the time goes in v4:
time: 36.7 us; the launch traced here: 36.5 us
  starting transfers between devices  13.4 us (37%)
  waiting for transfers between devices  11.8 us (32%)
  Pallas kernels  10.6 us (29%)
  between operations  0.73 us (2%)
    pallas_call x8, Pallas kernels, call(): pl.pallas_call(kernel, out_shape=out_shape, in_specs=in_specs or [VMEM] *...  10.6 us
    all_to_all x1, waiting for transfers between devices, per_device(): pieces = lax.all_to_all(pieces, ('dp', 'ctx'), 0, 0, tiled=True)  5.29 us
    ppermute x3, starting transfers between devices, per_device(): lax.ppermute(two, 'dp', [(i, i ^ far) for i in range(parts)])  4.35 us
    ppermute x3, waiting for transfers between devices, per_device(): lax.ppermute(two, 'dp', [(i, i ^ far) for i in range(parts)])  4.12 us
    all_to_all x1, starting transfers between devices, per_device(): pieces = lax.all_to_all(pieces, ('dp', 'ctx'), 0, 0, tiled=True)  3.81 us
    ppermute x1, starting transfers between devices, per_device(): nearby = lax.ppermute(gate_weight, 'dp', [(i, i ^ 1) for i in range(parts)])  3.03 us
    ppermute x1, waiting for transfers between devices, per_device(): kappa = lax.ppermute(kappa, 'ctx', opposite)  2.35 us
    ppermute x1, starting transfers between devices, per_device(): states = lax.ppermute(total, 'ctx', opposite)  1.55 us
  transfers between devices with their start and end apart: 10, of which 4 were waited for; matrix products, arithmetic and copies ran while one was open for 0% of the time, Pallas kernels for 24%

profile of v4, /device:TPU:0, one launch (start us, length us, event | category | flops | bytes accessed | tf_op | source)
XLA Modules:
  0.0 36.5 jit_solution(4469557162475110475)
XLA Ops:
  0.6 3.0 %collective-permute-start = (bf16[16,16]{1,0:T(8,128)(2,1)}, bf16[16,16]{1,0:T(8,128)(2,1)S(1)}, u32[]{:S(2)}, u32[]{:S(2)}) collective-permute-start(bf16[16,16]{1,0:T(8,128)(2,1)} %gate_ref.1), channel_id=1, source_target_pairs={{0,4},{4,0},{8,12},{12,8},{16,20},{20,16},{24,28},{28,24},{1,5},{5... | collective-permute-start | bytes 1544 | tf_op jit(solution)/shard_map/ppermute | solution.py:393
  3.7 2.1 %split_heads.1 = (bf16[4,8,128,128]{3,2,1,0:T(8,128)(2,1)S(1)}, bf16[4,8,128,128]{3,2,1,0:T(8,128)(2,1)S(1)}, bf16[16,16]{1,0:T(8,128)(2,1)S(1)}) custom-call(bf16[1,128,16,128]{3,2,1,0:T(8,128)(2,1)} %k_ref.1, bf16[1,128,16,128]{3,2,1,0:T(8,128)(2,1)} %q_ref.1, bf16[1,128,16,128]{3,2,1,0:T(8,128)(2,1)} %v_ref.1, bf16[1,128,16,128]{3,2,1,0:T(8,128)(2,1)} %g_ref.1, ...), custom_call_target="tpu_custom_call" | custom-call | bytes 9000000 | tf_op jit(solution)/shard_map/split_heads/pallas_call | solution.py:53
  5.8 0.1 collective-permute-start.4
  5.9 1.8 %collective-permute-start.1 = (bf16[2,16,16]{2,1,0:T(8,128)(2,1)S(1)}, bf16[2,16,16]{2,1,0:T(8,128)(2,1)S(1)}, u32[]{:S(2)}, u32[]{:S(2)}) collective-permute-start(bf16[2,16,16]{2,1,0:T(8,128)(2,1)S(1)} %pad_maximum_fusion.refs_0_), channel_id=1, source_target_pairs={{0,8},{4,12},{8,0},{12,4},{16,24},{20,28},{24,16},{28,20},{1,9},{5... | collective-permute-start | bytes 3080 | tf_op jit(solution)/shard_map/ppermute | solution.py:397
  7.6 2.5 %collective-permute-start.2 = (bf16[2,16,16]{2,1,0:T(8,128)(2,1)S(1)}, bf16[2,16,16]{2,1,0:T(8,128)(2,1)S(1)}, u32[]{:S(2)}, u32[]{:S(2)}) collective-permute-start(bf16[2,16,16]{2,1,0:T(8,128)(2,1)S(1)} %pad_maximum_fusion.refs_0_), channel_id=1, source_target_pairs={{0,24},{4,28},{8,16},{12,20},{16,8},{20,12},{24,0},{28,4},{1,25},{... | collective-permute-start | bytes 3080 | tf_op jit(solution)/shard_map/ppermute | solution.py:397
  10.1 0.1 collective-permute-start.3
  10.2 0.3 products.1.product_ref
  10.5 0.0 copy-start
  10.5 0.0 collective-permute-done.1.refs_1_
  10.5 2.5 %collective-permute-done.2.refs_3_ = bf16[2,16,16]{2,1,0:T(8,128)(2,1)S(1)} collective-permute-done((bf16[2,16,16]{2,1,0:T(8,128)(2,1)S(1)}, bf16[2,16,16]{2,1,0:T(8,128)(2,1)S(1)}, u32[]{:S(2)}, u32[]{:S(2)}) %collective-permute-start.2) | collective-permute-done | bytes 1056 | tf_op jit(solution)/shard_map/ppermute | solution.py:397
  13.1 1.6 %collective-permute-done.3.refs_2_ = bf16[2,16,16]{2,1,0:T(8,128)(2,1)S(1)} collective-permute-done((bf16[2,16,16]{2,1,0:T(8,128)(2,1)S(1)}, bf16[2,16,16]{2,1,0:T(8,128)(2,1)S(1)}, u32[]{:S(2)}, u32[]{:S(2)}) %collective-permute-start.3) | collective-permute-done | bytes 1056 | tf_op jit(solution)/shard_map/ppermute | solution.py:397
  14.6 0.0 collective-permute-done.4.refs_6_.recv_ref
  14.6 0.9 %gate_states.1 = (bf16[1,8,128,128]{3,2,1,0:T(8,128)(2,1)S(1)}, bf16[1,8,128,128]{3,2,1,0:T(8,128)(2,1)S(1)}, f32[2,16,128]{2,1,0:T(8,128)S(1)}, f32[2,16,128]{2,1,0:T(8,128)S(1)}) custom-call(bf16[2,16,16]{2,1,0:T(8,128)(2,1)S(1)} %pad_maximum_fusion.refs_0_, bf16[2,16,16]{2,1,0:T(8,128)(2,1)S(1)} %collective-permute-done.1.refs_1_, ...), custom_call_target="tpu_custom_call" | custom-call | bytes 3900000 | tf_op jit(solution)/shard_map/gate_states/pallas_call | solution.py:53
  15.5 1.6 %collective-permute-start.5 = (bf16[1,8,128,128]{3,2,1,0:T(8,128)(2,1)S(1)}, bf16[1,8,128,128]{3,2,1,0:T(8,128)(2,1)S(1)}, u32[]{:S(2)}, u32[]{:S(2)}) collective-permute-start(bf16[1,8,128,128]{3,2,1,0:T(8,128)(2,1)S(1)} %get-tuple-element.40), channel_id=1, source_target_pairs={{0,2},{1,3},{2,0},{3,1},{4,6},{5,7},{6,4},{7,5},{8,10},{9,11},{10,... | collective-permute-start | bytes 786440 | tf_op jit(solution)/shard_map/ppermute | solution.py:442
  17.1 0.3 kappa.1
  17.3 0.6 %collective-permute-start.6 = (f32[8,128]{1,0:T(8,128)S(1)}, f32[8,128]{1,0:T(8,128)S(1)}, u32[]{:S(2)}, u32[]{:S(2)}) collective-permute-start(f32[8,128]{1,0:T(8,128)S(1)} %kappa.1), channel_id=1, source_target_pairs={{0,2},{1,3},{2,0},{3,1},{4,6},{5,7},{6,4},{7,5},{8,10},{9,11},{10,... | collective-permute-start | bytes 12296 | tf_op jit(solution)/shard_map/ppermute | solution.py:445
  17.9 2.3 %inside_block.1 = (f32[1,2,8,128,128]{4,3,2,1,0:T(8,128)S(1)}, f32[1,8,128,128]{3,2,1,0:T(8,128)S(1)}, bf16[1,8,128,128]{3,2,1,0:T(8,128)(2,1)S(1)}, bf16[1,9,12...) custom-call(bf16[4,8,128,128]{3,2,1,0:T(8,128)(2,1)S(1)} %get-tuple-element.33.keep_ref.refs_5_, ...), custom_call_target="tpu_custom_call" | custom-call | bytes 12000000 | tf_op jit(solution)/shard_map/inside_block/pallas_call | solution.py:53
  20.2 0.1 collective-permute-start.7
  20.3 2.3 %collective-permute-done.6.kappa_ref = f32[8,128]{1,0:T(8,128)S(1)} collective-permute-done((f32[8,128]{1,0:T(8,128)S(1)}, f32[8,128]{1,0:T(8,128)S(1)}, u32[]{:S(2)}, u32[]{:S(2)}) %collective-permute-start.6) | collective-permute-done | bytes 4128 | tf_op jit(solution)/shard_map/ppermute | solution.py:445
  22.6 1.8 %outside_block.1 = (bf16[1,8,128,128]{3,2,1,0:T(8,128)(2,1)S(1)}, bf16[1,9,128,128]{3,2,1,0:T(8,128)(2,1)S(1)}, f32[8,128]{1,0:T(8,128)S(1)}, f32[32,2,128]{2,1,0:T(2,128)}) custom-call(bf16[4,8,128,128]{3,2,1,0:T(8,128)(2,1)S(1)} %get-tuple-element.33.keep_ref.refs_5_, bf16[4,8,128,128]{3,2,1,0:T(8,128)(2,1)S(1)} %collective-permute-done.4.refs_6_.recv_ref, ...), custom_call_target="tpu_custom_call" | custom-call | bytes 4500000 | tf_op jit(solution)/shard_map/outside_block/pallas_call | solution.py:53
  24.4 3.8 %all-to-all-start = ((f32[32,2,128]{2,1,0:T(2,128)}), f32[32,2,128]{2,1,0:T(2,128)S(1)}, u32[]{:S(2)}, u32[]{:S(2)}) async-start(f32[32,2,128]{2,1,0:T(2,128)} %get-tuple-element.54), calls=%async_computation | async-start | bytes 65536 | tf_op jit(solution)/shard_map/all_to_all | solution.py:466
  28.2 1.9 %merge_heads.1 = (bf16[1,128,16,128]{3,2,1,0:T(8,128)(2,1)}, f32[128,16,128]{2,1,0:T(8,128)S(1)}, f32[128,16,128]{2,1,0:T(8,128)S(1)}) custom-call(f32[2,16,128]{2,1,0:T(8,128)S(1)} %get-tuple-element.38.gate_ref, f32[8,128]{1,0:T(8,128)S(1)} %get-tuple-element.46.suffix_ref, f32[2,16,128]{2,1,0:T(8,128)S(1)} %get-tuple-element.39.rows_ref, ...), custom_call_target="tpu_custom_call" | custom-call | bytes 6000000 | tf_op jit(solution)/shard_map/merge_heads/pallas_call | solution.py:53
  30.2 5.3 %all-to-all-done.pieces_ref = f32[32,2,128]{2,1,0:T(2,128)S(1)} async-done(((f32[32,2,128]{2,1,0:T(2,128)}), f32[32,2,128]{2,1,0:T(2,128)S(1)}, u32[]{:S(2)}, u32[]{:S(2)}) %all-to-all-start) | async-done | bytes 32800 | tf_op jit(solution)/shard_map/all_to_all | solution.py:466
  35.5 1.1 %key_gradient.1 = (bf16[1,128,16,128]{3,2,1,0:T(8,128)(2,1)}, f32[16,16]{1,0:T(8,128)}) custom-call(f32[128,16,128]{2,1,0:T(8,128)S(1)} %get-tuple-element.52.base_ref, f32[128,16,128]{2,1,0:T(8,128)S(1)} %get-tuple-element.53.rise_ref, f32[32,2,128]{2,1,0:T(2,128)S(1)} %all-to-all-done.pieces_ref), custom_call_target="tpu_custom_call" | custom-call | bytes 3000000 | tf_op jit(solution)/shard_map/key_gradient/pallas_call | solution.py:53
  (7 shorter events, 0.0 us)
Async XLA Ops:
  0.6 5.1 %collective-permute-start = (bf16[16,16]{1,0:T(8,128)(2,1)}, bf16[16,16]{1,0:T(8,128)(2,1)S(1)}, u32[]{:S(2)}, u32[]{:S(2)}) collective-permute-start(bf16[16,16]{1,0:T(8,128)(2,1)} %gate_ref.1), channel_id=1, source_target_pairs={{0,4},{4,0},{8,12},{12,8},{16,20},{20,16},{24,28},{28,24},{1,5},{5... | collective-permute-start | bytes 1544 | tf_op jit(solution)/shard_map/ppermute | solution.py:393
  5.8 8.9 %collective-permute-start.4 = (bf16[4,8,128,128]{3,2,1,0:T(8,128)(2,1)S(1)}, bf16[4,8,128,128]{3,2,1,0:T(8,128)(2,1)S(1)}, u32[]{:S(2)}, u32[]{:S(2)}) collective-permute-start(bf16[4,8,128,128]{3,2,1,0:T(8,128)(2,1)S(1)} %get-tuple-element.37), channel_id=1, source_target_pairs={{0,1},{1,0},{2,3},{3,2},{4,5},{5,4},{6,7},{7,6},{8,9},{9,8},{10,11... | collective-permute-start | bytes 3145736 | tf_op jit(solution)/shard_map/ppermute | solution.py:402
  5.9 4.7 %collective-permute-start.1 = (bf16[2,16,16]{2,1,0:T(8,128)(2,1)S(1)}, bf16[2,16,16]{2,1,0:T(8,128)(2,1)S(1)}, u32[]{:S(2)}, u32[]{:S(2)}) collective-permute-start(bf16[2,16,16]{2,1,0:T(8,128)(2,1)S(1)} %pad_maximum_fusion.refs_0_), channel_id=1, source_target_pairs={{0,8},{4,12},{8,0},{12,4},{16,24},{20,28},{24,16},{28,20},{1,9},{5... | collective-permute-start | bytes 3080 | tf_op jit(solution)/shard_map/ppermute | solution.py:397
  7.6 5.4 %collective-permute-start.2 = (bf16[2,16,16]{2,1,0:T(8,128)(2,1)S(1)}, bf16[2,16,16]{2,1,0:T(8,128)(2,1)S(1)}, u32[]{:S(2)}, u32[]{:S(2)}) collective-permute-start(bf16[2,16,16]{2,1,0:T(8,128)(2,1)S(1)} %pad_maximum_fusion.refs_0_), channel_id=1, source_target_pairs={{0,24},{4,28},{8,16},{12,20},{16,8},{20,12},{24,0},{28,4},{1,25},{... | collective-permute-start | bytes 3080 | tf_op jit(solution)/shard_map/ppermute | solution.py:397
  10.1 4.5 %collective-permute-start.3 = (bf16[2,16,16]{2,1,0:T(8,128)(2,1)S(1)}, bf16[2,16,16]{2,1,0:T(8,128)(2,1)S(1)}, u32[]{:S(2)}, u32[]{:S(2)}) collective-permute-start(bf16[2,16,16]{2,1,0:T(8,128)(2,1)S(1)} %pad_maximum_fusion.refs_0_), channel_id=1, source_target_pairs={{0,16},{4,20},{8,24},{12,28},{16,0},{20,4},{24,8},{28,12},{1,17},{... | collective-permute-start | bytes 3080 | tf_op jit(solution)/shard_map/ppermute | solution.py:397
  10.5 4.1 %copy-start = (bf16[16]{0:T(256)(128)(2,1)S(1)}, bf16[16]{0:T(256)(128)(2,1)}, u32[]{:S(2)}) copy-start(bf16[16]{0:T(256)(128)(2,1)} %param.11) | copy-start | bytes 100
  15.5 7.1 %collective-permute-start.5 = (bf16[1,8,128,128]{3,2,1,0:T(8,128)(2,1)S(1)}, bf16[1,8,128,128]{3,2,1,0:T(8,128)(2,1)S(1)}, u32[]{:S(2)}, u32[]{:S(2)}) collective-permute-start(bf16[1,8,128,128]{3,2,1,0:T(8,128)(2,1)S(1)} %get-tuple-element.40), channel_id=1, source_target_pairs={{0,2},{1,3},{2,0},{3,1},{4,6},{5,7},{6,4},{7,5},{8,10},{9,11},{10,... | collective-permute-start | bytes 786440 | tf_op jit(solution)/shard_map/ppermute | solution.py:442
  17.3 5.3 %collective-permute-start.6 = (f32[8,128]{1,0:T(8,128)S(1)}, f32[8,128]{1,0:T(8,128)S(1)}, u32[]{:S(2)}, u32[]{:S(2)}) collective-permute-start(f32[8,128]{1,0:T(8,128)S(1)} %kappa.1), channel_id=1, source_target_pairs={{0,2},{1,3},{2,0},{3,1},{4,6},{5,7},{6,4},{7,5},{8,10},{9,11},{10,... | collective-permute-start | bytes 12296 | tf_op jit(solution)/shard_map/ppermute | solution.py:445
  20.2 8.0 %collective-permute-start.7 = (bf16[1,9,128,128]{3,2,1,0:T(8,128)(2,1)S(1)}, bf16[1,9,128,128]{3,2,1,0:T(8,128)(2,1)S(1)}, u32[]{:S(2)}, u32[]{:S(2)}) collective-permute-start(bf16[1,9,128,128]{3,2,1,0:T(8,128)(2,1)S(1)} %get-tuple-element.48), channel_id=1, source_target_pairs={{0,1},{1,0},{2,3},{3,2},{4,5},{5,4},{6,7},{7,6},{8,9},{9,8},{10,11... | collective-permute-start | bytes 884744 | tf_op jit(solution)/shard_map/ppermute | solution.py:446
  24.4 3.8 %collective-permute-start.8 = (bf16[1,9,128,128]{3,2,1,0:T(8,128)(2,1)S(1)}, bf16[1,9,128,128]{3,2,1,0:T(8,128)(2,1)S(1)}, u32[]{:S(2)}, u32[]{:S(2)}) collective-permute-start(bf16[1,9,128,128]{3,2,1,0:T(8,128)(2,1)S(1)} %get-tuple-element.50), channel_id=1, source_target_pairs={{0,1},{1,0},{2,3},{3,2},{4,5},{5,4},{6,7},{7,6},{8,9},{9,8},{10,11... | collective-permute-start | bytes 884744 | tf_op jit(solution)/shard_map/ppermute | solution.py:467
  24.4 11.1 %all-to-all-start = ((f32[32,2,128]{2,1,0:T(2,128)}), f32[32,2,128]{2,1,0:T(2,128)S(1)}, u32[]{:S(2)}, u32[]{:S(2)}) async-start(f32[32,2,128]{2,1,0:T(2,128)} %get-tuple-element.54), calls=%async_computation | async-start | bytes 65536 | tf_op jit(solution)/shard_map/all_to_all | solution.py:466

commit v5 on v4

--- a/solution.py
+++ b/solution.py
@@ -43,9 +43,13 @@
     return lax.rem(mine, 2), lax.div(mine, 2)
 
 
+def split_two(rows):
+    hi = rows.astype(BF16)
+    return hi, (rows - hi.astype(F32)).astype(BF16)
+
+
 def hi_lo(rows):
-    hi = rows.astype(BF16)
-    return jnp.concatenate([hi, (rows - hi.astype(F32)).astype(BF16)], 0)
+    return jnp.concatenate(split_two(rows), 0)
 
 
 def call(kernel, name, out_shape, operands, scratch=(), micros=1.0, in_specs=None, out_specs=None, limit=LIMIT):
@@ -107,8 +111,9 @@
     return full
 
 
-def gate_kernel(direct, pair, *refs):
-    *gates, bias_ref, keep_ref, recv_ref, total_ref, near_ref, rows_ref, gate_ref, scale_ref = refs
+def gate_kernel(direct, pair, chunks, *refs):
+    gates, refs = refs[:-chunks - 7], refs[-chunks - 7 :]
+    bias_ref, keep_ref, recv_ref, *total_refs, near_ref, rows_ref, gate_ref, scale_ref = refs
     par, chip = place()
     _, half, width, count = keep_ref.shape
     gate_ref[0] = whole_gate(direct, gates)
@@ -144,7 +149,8 @@
                 jnp.where(enters, ends[half + j : half + j + 1], 1.0) * own
                 + jnp.where(enters, 1.0, ends[j : j + 1]) * other
             )
-            total_ref[at, j] = passed.astype(total_ref.dtype)
+            size = half // chunks
+            total_refs[j // size][at, j % size] = passed.astype(total_refs[0].dtype)
             near_ref[at, j] = jnp.where(enters, own, other).astype(near_ref.dtype)
 
 
@@ -176,9 +182,9 @@
     kappa_ref[...] = weighted_keys(keep_ref, recv_ref, rows_ref[1, :half, :], rows_ref[1, half:, :])
 
 
-def inside_kernel(pair, keep_ref, recv_ref, rows_ref, near_ref, product_ref, attn_ref, *refs):
+def inside_kernel(pair, keep_ref, recv_ref, rows_ref, near_ref, product_ref, attn_ref, run_ref, dg_ref, *refs):
     if pair:
-        other_ref, mine_ref, send_ref, dg_ref, scale_ref = refs
+        other_ref, mine_ref, send_ref, scale_ref = refs
     else:
         (scale_ref,) = refs
     par, chip = place()
@@ -190,6 +196,7 @@
     scale_ref[0] = tail
     scale_ref[1] = head
     causal = iota((count, count), 0) >= iota((count, count), 1)
+    until = jnp.where(iota((count, count), 0) <= iota((count, count), 1), 1.0, 0.0).astype(BF16)
     both = (keep_ref, recv_ref)
     side = chip
     if pair:
@@ -219,64 +226,90 @@
                 factor = jnp.where(block == side, 0.0, const) * scale_ref[1 - side, at : at + 1, :]
                 full = jnp.where(side == 0, query, key) + factor * cross
                 (mine_ref if rel == 0 else send_ref)[0, j] = full.astype(BF16)
-                slopes.append(slope_row(ref, side, j, full))
+                rest = jnp.where(side == 0, key, query)
+                slopes.append(slope_row(ref, side, j, full) + slope_row(ref, 1 - side, j, rest))
             else:
                 attn_ref[0, rel, j] = query
                 attn_ref[1, rel, j] = key
-        if pair:
-            dg_ref[rel] = jnp.concatenate(slopes, 0)
-
-
-def outside_kernel(pair, keep_ref, recv_ref, rows_ref, state_ref, near_ref, attn_ref, kappa_ref, *refs):
-    if pair:
-        dg_ref, mine_ref, send_ref, suffix_ref, pieces_ref, scale_ref = refs
+                slopes.append(slope_row(ref, 0, j, query) + slope_row(ref, 1, j, key))
+            run = nn(hi_lo(ref[0, j].astype(F32) * rows_ref[1, at : at + 1, :]), until)
+            hi, lo = split_two(run[:width] + run[width:])
+            run_ref[0, rel, j] = hi
+            run_ref[1, rel, j] = lo
+        dg_ref[rel] = jnp.concatenate(slopes, 0)
+
+
+def run_keys(run_ref, own, other):
+    half, count = own.shape
+    width = run_ref.shape[3]
+    lhs = jnp.concatenate([hi_lo(own), hi_lo(other)], 1)
+    row = iota((half, width), 0)
+    total = jnp.zeros((half, width), F32)
+    for j in range(0, half, 2):
+        planes = [
+            jnp.concatenate([run_ref[p, rel, j : j + 2].reshape(2 * width, count) for rel in range(2)], 1)
+            for p in range(2)
+        ]
+        got = nt(lhs, planes[0])
+        got = got[:half] + (got[half:] + nt(lhs[:half], planes[1]))
+        total = total + jnp.where(row == j, got[:, :width], 0.0) + jnp.where(row == j + 1, got[:, width:], 0.0)
+    return total
+
+
+def outside_kernel(pair, group, groups, keep_ref, recv_ref, rows_ref, state_ref, near_ref, attn_ref, dg_ref, *refs):
+    final = group == groups - 1
+    earlier, refs = (refs[:3], refs[3:]) if group else ((), refs)
+    if final:
+        kappa_ref, run_ref, mine_ref, send_ref, suffix_ref, pieces_ref, scale_ref = refs
     else:
-        mine_ref, send_ref, suffix_ref, pieces_ref, scale_ref = refs
+        mine_ref, send_ref, slope_ref, scale_ref = refs
     par, chip = place()
     _, half, width, count = keep_ref.shape
+    size = half // groups
+    start = group * size
     const = 1.0 / width
     cumul = rows_ref[0]
     tail, head, ends = scales(cumul)
     scale_ref[0] = tail
     scale_ref[1] = head
-    both = (keep_ref, recv_ref)
+    sides = mine_ref.shape[0]
+    for at in range(sides if group else 0):
+        mine_ref[at, :start] = earlier[0][at, :start]
+        send_ref[at, :start] = earlier[1][at, :start]
     all_slopes = []
-    for rel, ref in enumerate(both):
+    for rel, ref in enumerate((keep_ref, recv_ref)):
         block = par if rel == 0 else 1 - par
-        slopes = dg_ref[rel] if pair else jnp.zeros((half, count), F32)
+        slopes = dg_ref[rel, start : start + size]
         for at, side in enumerate((1 - chip,) if pair else (0, 1)):
             enters = block == side
             lines = []
-            for j in range(half):
+            for j in range(start, start + size):
                 passed = (1 - rel) * half + j
-                moved = ends[passed : passed + 1] * state_ref[at, j].astype(F32) + near_ref[at, j]
-                known = jnp.where(enters, state_ref[at, j].astype(F32), moved)
+                come = state_ref[at, j - start].astype(F32)
+                moved = ends[passed : passed + 1] * come + near_ref[at, j]
+                known = jnp.where(enters, come, moved)
                 cross = nt(known.astype(BF16), ref[3 - side, j])
                 factor = const * scale_ref[1 - side, rel * half + j : rel * half + j + 1, :]
+                lines.append(factor * slope_row(ref, side, j, cross))
                 full = attn_ref[at, rel, j] + factor * cross
                 (mine_ref if rel == 0 else send_ref)[at, j] = full.astype(BF16)
-                lines.append(slope_row(ref, side, j, full))
             slopes = slopes + jnp.concatenate(lines, 0)
         all_slopes.append(slopes)
+    if not final:
+        for rel in range(2):
+            slope_ref[rel] = all_slopes[rel]
+        return
+    if group:
+        all_slopes = [jnp.concatenate([earlier[2][rel], all_slopes[rel]], 0) for rel in range(2)]
     slope = jnp.concatenate(all_slopes, 0)
-    suffix = exact(slope, iota((count, count), 0) >= iota((count, count), 1))
-    sums = jnp.broadcast_to(suffix[:, :1], suffix.shape)
+    sums = jnp.broadcast_to(jnp.sum(slope, 1, keepdims=True), slope.shape)
     first = jnp.where(par == 0, 1.0, 0.0)
-    mine = suffix[:half] + first * sums[half:]
-    other = suffix[half:] + (1.0 - first) * sums[:half]
-    suffix_ref[...] = mine
-    sides = send_ref.shape[0]
-    for at in range(sides):
-        send_ref[at, half] = jnp.zeros((width, count), BF16)
-    if sides == 2:
-        send_ref[0, half, : 2 * half] = hi_lo(rows_ref[1, half:, :])
-    send_ref[sides - 1, half, : 2 * half] = hi_lo(other)
+    end = iota((half, count), 1) == count - 1
+    own = slope[:half] + jnp.where(end, first * sums[half:], 0.0)
+    other = slope[half:] + jnp.where(end, (1.0 - first) * sums[:half], 0.0)
     total = sums[:half] + sums[half:]
     before = jnp.where(chip == 1, 1.0, 0.0) if pair else 1.0
-    partial = (
-        weighted_keys(keep_ref, recv_ref, mine * rows_ref[1, :half, :], other * rows_ref[1, half:, :])
-        + before * (total * kappa_ref[...])
-    )
+    partial = run_keys(run_ref, own, other) + before * (total * kappa_ref[...])
     parts = lax.axis_size("dp")
     ranks = pieces_ref.shape[0] // parts
     piece, slot = width // parts, width // half
@@ -288,6 +321,13 @@
         line = jnp.sum(jnp.where(here, turned, 0.0), 0, keepdims=True)
         sent = jnp.concatenate([line, totals], 0)
         pieces_ref[pl.ds(i * ranks, ranks)] = jnp.broadcast_to(sent[None], (ranks, 2, width))
+    suffix = exact(jnp.concatenate([own, other], 0), iota((count, count), 0) >= iota((count, count), 1))
+    suffix_ref[...] = suffix[:half]
+    for at in range(sides):
+        send_ref[at, half] = jnp.zeros((width, count), BF16)
+    if sides == 2:
+        send_ref[0, half, : 2 * half] = hi_lo(rows_ref[1, half:, :])
+    send_ref[sides - 1, half, : 2 * half] = hi_lo(suffix[half:])
 
 
 def merge_kernel(pair, gate_ref, suffix_ref, rows_ref, *refs):
@@ -309,7 +349,7 @@
     line_ref[0, pl.ds(par * half, half), :] = rows_ref[1, :half, :]
     line_ref[1, pl.ds(par * half, half), :] = suffix_ref[...]
     first = chip if pair else 0
-    query_ref[0] = tmp[first].reshape(count, heads, width).astype(BF16)
+    query_ref[0] = tmp[first, : count * heads].reshape(count, heads, width).astype(BF16)
     rise = line_ref[0]
     slope = rise * line_ref[1]
     gate = gate_ref[0]
@@ -410,10 +450,12 @@
     sides = 1 if pair else 2
     lines = pltpu.VMEM((2, heads, count), F32)
     state = shape(sides, half, width, width, dtype=BF16 if pair else F32)
-    total, near, rows, gate_full = call(
-        functools.partial(gate_kernel, direct, pair),
+    chunks = 1 if pair else 1
+    part = shape(sides, half // chunks, width, width, dtype=state.dtype)
+    *totals, near, rows, gate_full = call(
+        functools.partial(gate_kernel, direct, pair, chunks),
         "gate_states",
-        (state, state, shape(2, heads, count, dtype=F32), shape(2, heads, width, dtype=F32)),
+        (part,) * chunks + (state, shape(2, heads, count, dtype=F32), shape(2, heads, width, dtype=F32)),
         (*gates, bias, keep, recv),
         [lines],
         1.3,
@@ -422,13 +464,13 @@
     attn_shape = shape(sides, 2, half, width, count, dtype=F32)
     mine_shape = shape(sides, half, width, count)
     send_shape = shape(sides, half + 1, width, count)
-    slope_shape = shape(2, half, count, dtype=F32)
+    run_shape = shape(2, 2, half, width, count)
 
     def inside(*outs):
         return call(
             functools.partial(inside_kernel, pair),
             "inside_block",
-            (attn_shape, *outs),
+            (attn_shape, run_shape, shape(2, half, count, dtype=F32), *outs),
             (keep, recv, rows, near, products),
             [lines],
             4.0,
@@ -439,30 +481,38 @@
     )
     if pair:
         opposite = [(i, i ^ 2) for i in range(ranks)]
-        states = lax.ppermute(total, "ctx", opposite)
+        states = [lax.ppermute(total, "ctx", opposite) for total in totals]
         near_shape = shape(1, half, width, width, dtype=F32)
-        attn, near, mine_local, send_local, slopes = inside(near_shape, mine_shape, send_shape, slope_shape)
+        attn, runs, slopes, near, mine_local, send_local = inside(near_shape, mine_shape, send_shape)
         kappa = lax.ppermute(kappa, "ctx", opposite)
         recv_local = lax.ppermute(send_local, "ctx", swap)
-        more = (slopes,)
         local = (mine_local, recv_local)
     else:
         ends = jnp.exp(rows[0, :half, -1] + rows[0, half:, -1])[:, None, None]
-        states = jnp.stack(
-            [across_chips(total[0], ends, ranks, False), across_chips(total[1], ends, ranks, True)]
+        (total,) = totals
+        states = [
+            jnp.stack([across_chips(total[0], ends, ranks, False), across_chips(total[1], ends, ranks, True)])
+        ]
+        attn, runs, slopes = inside()
+        kappa = across_chips(kappa, jnp.ones((half, 1), F32), ranks, False)
+        local = ()
+    earlier = ()
+    for group, come in enumerate(states):
+        final = group == chunks - 1
+        outs = (
+            (shape(half, count, dtype=F32), shape(parts * ranks, 2, width, dtype=F32))
+            if final
+            else (shape(2, half // chunks, count, dtype=F32),)
         )
-        (attn,) = inside()
-        kappa = across_chips(kappa, jnp.ones((half, 1), F32), ranks, False)
-        more = ()
-        local = ()
-    mine, send, suffix, pieces = call(
-        functools.partial(outside_kernel, pair),
-        "outside_block",
-        (mine_shape, send_shape, shape(half, count, dtype=F32), shape(parts * ranks, 2, width, dtype=F32)),
-        (keep, recv, rows, states, near, attn, kappa, *more),
-        [lines],
-        1.5,
-    )
+        earlier = call(
+            functools.partial(outside_kernel, pair, group, chunks),
+            "outside_block",
+            (mine_shape, send_shape, *outs),
+            (keep, recv, rows, come, near, attn, slopes, *earlier) + ((kappa, runs) if final else ()),
+            [lines],
+            1.0,
+        )
+    mine, send, suffix, pieces = earlier
     pieces = lax.all_to_all(pieces, ("dp", "ctx"), 0, 0, tiled=True)
     recv_out = lax.ppermute(send, "ctx", swap)
     whole = shape(1, count, heads, width)
@@ -472,7 +522,7 @@
         "merge_heads",
         (whole, plain, plain),
         (gate_full, suffix, rows, *local, mine, recv_out),
-        [pltpu.VMEM((2, heads, count), F32), pltpu.VMEM((2, count * heads, width), F32)],
+        [pltpu.VMEM((2, heads, count), F32), pltpu.VMEM((2, (count + 1) * heads, width), F32)],
         2.0,
     )
     key_grad, gate_grad = call(

time: 36.7 us -> 36.7 us (level)
  no operation moved by 1% of the time
where the time goes in v5:
time: 36.7 us; the launch traced here: 36.6 us
  starting transfers between devices  13.4 us (37%)
  waiting for transfers between devices  11.6 us (32%)
  Pallas kernels  10.8 us (29%)
  between operations  0.73 us (2%)
    pallas_call x8, Pallas kernels, call(): pl.pallas_call(kernel, out_shape=out_shape, in_specs=in_specs or [VMEM] *...  10.8 us
    all_to_all x1, waiting for transfers between devices, per_device(): pieces = lax.all_to_all(pieces, ('dp', 'ctx'), 0, 0, tiled=True)  5.29 us
    ppermute x3, starting transfers between devices, per_device(): lax.ppermute(two, 'dp', [(i, i ^ far) for i in range(parts)])  4.35 us
    ppermute x3, waiting for transfers between devices, per_device(): lax.ppermute(two, 'dp', [(i, i ^ far) for i in range(parts)])  4.12 us
    all_to_all x1, starting transfers between devices, per_device(): pieces = lax.all_to_all(pieces, ('dp', 'ctx'), 0, 0, tiled=True)  3.81 us
    ppermute x1, starting transfers between devices, per_device(): nearby = lax.ppermute(gate_weight, 'dp', [(i, i ^ 1) for i in range(parts)])  3.03 us
    ppermute x1, waiting for transfers between devices, per_device(): kappa = lax.ppermute(kappa, 'ctx', opposite)  2.14 us
    ppermute x1, starting transfers between devices, per_device(): states = [lax.ppermute(total, 'ctx', opposite) for total in totals]  1.55 us
  transfers between devices with their start and end apart: 10, of which 4 were waited for; matrix products, arithmetic and copies ran while one was open for 0% of the time, Pallas kernels for 24%

profile of v5, /device:TPU:0, one launch (start us, length us, event | category | flops | bytes accessed | tf_op | source)
XLA Modules:
  0.0 36.6 jit_solution(9379007553337404121)
XLA Ops:
  0.6 3.0 %collective-permute-start = (bf16[16,16]{1,0:T(8,128)(2,1)}, bf16[16,16]{1,0:T(8,128)(2,1)S(1)}, u32[]{:S(2)}, u32[]{:S(2)}) collective-permute-start(bf16[16,16]{1,0:T(8,128)(2,1)} %gate_ref.1), channel_id=1, source_target_pairs={{0,4},{4,0},{8,12},{12,8},{16,20},{20,16},{24,28},{28,24},{1,5},{5... | collective-permute-start | bytes 1544 | tf_op jit(solution)/shard_map/ppermute | solution.py:433
  3.7 2.1 %split_heads.1 = (bf16[4,8,128,128]{3,2,1,0:T(8,128)(2,1)S(1)}, bf16[4,8,128,128]{3,2,1,0:T(8,128)(2,1)S(1)}, bf16[16,16]{1,0:T(8,128)(2,1)S(1)}) custom-call(bf16[1,128,16,128]{3,2,1,0:T(8,128)(2,1)} %k_ref.1, bf16[1,128,16,128]{3,2,1,0:T(8,128)(2,1)} %q_ref.1, bf16[1,128,16,128]{3,2,1,0:T(8,128)(2,1)} %v_ref.1, bf16[1,128,16,128]{3,2,1,0:T(8,128)(2,1)} %g_ref.1, ...), custom_call_target="tpu_custom_call" | custom-call | bytes 9000000 | tf_op jit(solution)/shard_map/split_heads/pallas_call | solution.py:57
  5.8 0.1 collective-permute-start.4
  5.9 1.8 %collective-permute-start.1 = (bf16[2,16,16]{2,1,0:T(8,128)(2,1)S(1)}, bf16[2,16,16]{2,1,0:T(8,128)(2,1)S(1)}, u32[]{:S(2)}, u32[]{:S(2)}) collective-permute-start(bf16[2,16,16]{2,1,0:T(8,128)(2,1)S(1)} %pad_maximum_fusion.refs_0_), channel_id=1, source_target_pairs={{0,8},{4,12},{8,0},{12,4},{16,24},{20,28},{24,16},{28,20},{1,9},{5... | collective-permute-start | bytes 3080 | tf_op jit(solution)/shard_map/ppermute | solution.py:437
  7.6 2.5 %collective-permute-start.2 = (bf16[2,16,16]{2,1,0:T(8,128)(2,1)S(1)}, bf16[2,16,16]{2,1,0:T(8,128)(2,1)S(1)}, u32[]{:S(2)}, u32[]{:S(2)}) collective-permute-start(bf16[2,16,16]{2,1,0:T(8,128)(2,1)S(1)} %pad_maximum_fusion.refs_0_), channel_id=1, source_target_pairs={{0,24},{4,28},{8,16},{12,20},{16,8},{20,12},{24,0},{28,4},{1,25},{... | collective-permute-start | bytes 3080 | tf_op jit(solution)/shard_map/ppermute | solution.py:437
  10.1 0.1 collective-permute-start.3
  10.2 0.3 products.1.product_ref
  10.5 0.0 copy-start
  10.5 0.0 collective-permute-done.1.refs_1_
  10.5 2.5 %collective-permute-done.2.refs_3_ = bf16[2,16,16]{2,1,0:T(8,128)(2,1)S(1)} collective-permute-done((bf16[2,16,16]{2,1,0:T(8,128)(2,1)S(1)}, bf16[2,16,16]{2,1,0:T(8,128)(2,1)S(1)}, u32[]{:S(2)}, u32[]{:S(2)}) %collective-permute-start.2) | collective-permute-done | bytes 1056 | tf_op jit(solution)/shard_map/ppermute | solution.py:437
  13.1 1.6 %collective-permute-done.3.refs_2_ = bf16[2,16,16]{2,1,0:T(8,128)(2,1)S(1)} collective-permute-done((bf16[2,16,16]{2,1,0:T(8,128)(2,1)S(1)}, bf16[2,16,16]{2,1,0:T(8,128)(2,1)S(1)}, u32[]{:S(2)}, u32[]{:S(2)}) %collective-permute-start.3) | collective-permute-done | bytes 1056 | tf_op jit(solution)/shard_map/ppermute | solution.py:437
  14.6 0.0 collective-permute-done.4.refs_6_.recv_ref
  14.6 0.9 %gate_states.1 = (bf16[1,8,128,128]{3,2,1,0:T(8,128)(2,1)S(1)}, bf16[1,8,128,128]{3,2,1,0:T(8,128)(2,1)S(1)}, f32[2,16,128]{2,1,0:T(8,128)S(1)}, f32[2,16,128]{2,1,0:T(8,128)S(1)}) custom-call(bf16[2,16,16]{2,1,0:T(8,128)(2,1)S(1)} %pad_maximum_fusion.refs_0_, bf16[2,16,16]{2,1,0:T(8,128)(2,1)S(1)} %collective-permute-done.1.refs_1_, ...), custom_call_target="tpu_custom_call" | custom-call | bytes 3900000 | tf_op jit(solution)/shard_map/gate_states/pallas_call | solution.py:57
  15.5 1.6 %collective-permute-start.5 = (bf16[1,8,128,128]{3,2,1,0:T(8,128)(2,1)S(1)}, bf16[1,8,128,128]{3,2,1,0:T(8,128)(2,1)S(1)}, u32[]{:S(2)}, u32[]{:S(2)}) collective-permute-start(bf16[1,8,128,128]{3,2,1,0:T(8,128)(2,1)S(1)} %get-tuple-element.41), channel_id=1, source_target_pairs={{0,2},{1,3},{2,0},{3,1},{4,6},{5,7},{6,4},{7,5},{8,10},{9,11},{10,... | collective-permute-start | bytes 786440 | tf_op jit(solution)/shard_map/ppermute | solution.py:484
  17.1 0.3 kappa.1
  17.3 0.6 %collective-permute-start.6 = (f32[8,128]{1,0:T(8,128)S(1)}, f32[8,128]{1,0:T(8,128)S(1)}, u32[]{:S(2)}, u32[]{:S(2)}) collective-permute-start(f32[8,128]{1,0:T(8,128)S(1)} %kappa.1), channel_id=1, source_target_pairs={{0,2},{1,3},{2,0},{3,1},{4,6},{5,7},{6,4},{7,5},{8,10},{9,11},{10,... | collective-permute-start | bytes 12296 | tf_op jit(solution)/shard_map/ppermute | solution.py:487
  17.9 2.5 %inside_block.1 = (f32[1,2,8,128,128]{4,3,2,1,0:T(8,128)S(1)}, bf16[2,2,8,128,128]{4,3,2,1,0:T(8,128)(2,1)S(1)}, f32[2,8,128]{2,1,0:T(8,128)S(1)}, f32[1,8,128,1...) custom-call(bf16[4,8,128,128]{3,2,1,0:T(8,128)(2,1)S(1)} %get-tuple-element.34.keep_ref, ...), custom_call_target="tpu_custom_call" | custom-call | bytes 12000000 | tf_op jit(solution)/shard_map/inside_block/pallas_call | solution.py:57
  20.4 0.1 collective-permute-start.7
  20.5 2.1 %collective-permute-done.6.refs_0_ = f32[8,128]{1,0:T(8,128)S(1)} collective-permute-done((f32[8,128]{1,0:T(8,128)S(1)}, f32[8,128]{1,0:T(8,128)S(1)}, u32[]{:S(2)}, u32[]{:S(2)}) %collective-permute-start.6) | collective-permute-done | bytes 4128 | tf_op jit(solution)/shard_map/ppermute | solution.py:487
  22.6 1.8 %outside_block.1 = (bf16[1,8,128,128]{3,2,1,0:T(8,128)(2,1)S(1)}, bf16[1,9,128,128]{3,2,1,0:T(8,128)(2,1)S(1)}, f32[8,128]{1,0:T(8,128)S(1)}, f32[32,2,128]{2,1,0:T(2,128)}) custom-call(bf16[4,8,128,128]{3,2,1,0:T(8,128)(2,1)S(1)} %get-tuple-element.34.keep_ref.refs_5_, bf16[4,8,128,128]{3,2,1,0:T(8,128)(2,1)S(1)} %collective-permute-done.4.refs_6_.recv_ref, ...), custom_call_target="tpu_custom_call" | custom-call | bytes 3000000 | tf_op jit(solution)/shard_map/outside_block/pallas_call | solution.py:57
  24.4 3.8 %all-to-all-start = ((f32[32,2,128]{2,1,0:T(2,128)}), f32[32,2,128]{2,1,0:T(2,128)S(1)}, u32[]{:S(2)}, u32[]{:S(2)}) async-start(f32[32,2,128]{2,1,0:T(2,128)} %get-tuple-element.56), calls=%async_computation | async-start | bytes 65536 | tf_op jit(solution)/shard_map/all_to_all | solution.py:516
  28.3 1.9 %merge_heads.1 = (bf16[1,128,16,128]{3,2,1,0:T(8,128)(2,1)}, f32[128,16,128]{2,1,0:T(8,128)S(1)}, f32[128,16,128]{2,1,0:T(8,128)S(1)}) custom-call(f32[2,16,128]{2,1,0:T(8,128)S(1)} %get-tuple-element.39.gate_ref, f32[8,128]{1,0:T(8,128)S(1)} %get-tuple-element.48.suffix_ref, f32[2,16,128]{2,1,0:T(8,128)S(1)} %get-tuple-element.40.rows_ref, ...), custom_call_target="tpu_custom_call" | custom-call | bytes 6000000 | tf_op jit(solution)/shard_map/merge_heads/pallas_call | solution.py:57
  30.2 5.3 %all-to-all-done.pieces_ref = f32[32,2,128]{2,1,0:T(2,128)S(1)} async-done(((f32[32,2,128]{2,1,0:T(2,128)}), f32[32,2,128]{2,1,0:T(2,128)S(1)}, u32[]{:S(2)}, u32[]{:S(2)}) %all-to-all-start) | async-done | bytes 32800 | tf_op jit(solution)/shard_map/all_to_all | solution.py:516
  35.5 1.1 %key_gradient.1 = (bf16[1,128,16,128]{3,2,1,0:T(8,128)(2,1)}, f32[16,16]{1,0:T(8,128)}) custom-call(f32[128,16,128]{2,1,0:T(8,128)S(1)} %get-tuple-element.54.base_ref, f32[128,16,128]{2,1,0:T(8,128)S(1)} %get-tuple-element.55.rise_ref, f32[32,2,128]{2,1,0:T(2,128)S(1)} %all-to-all-done.pieces_ref), custom_call_target="tpu_custom_call" | custom-call | bytes 3000000 | tf_op jit(solution)/shard_map/key_gradient/pallas_call | solution.py:57
  (7 shorter events, 0.0 us)
Async XLA Ops:
  0.6 5.1 %collective-permute-start = (bf16[16,16]{1,0:T(8,128)(2,1)}, bf16[16,16]{1,0:T(8,128)(2,1)S(1)}, u32[]{:S(2)}, u32[]{:S(2)}) collective-permute-start(bf16[16,16]{1,0:T(8,128)(2,1)} %gate_ref.1), channel_id=1, source_target_pairs={{0,4},{4,0},{8,12},{12,8},{16,20},{20,16},{24,28},{28,24},{1,5},{5... | collective-permute-start | bytes 1544 | tf_op jit(solution)/shard_map/ppermute | solution.py:433
  5.8 8.9 %collective-permute-start.4 = (bf16[4,8,128,128]{3,2,1,0:T(8,128)(2,1)S(1)}, bf16[4,8,128,128]{3,2,1,0:T(8,128)(2,1)S(1)}, u32[]{:S(2)}, u32[]{:S(2)}) collective-permute-start(bf16[4,8,128,128]{3,2,1,0:T(8,128)(2,1)S(1)} %get-tuple-element.38), channel_id=1, source_target_pairs={{0,1},{1,0},{2,3},{3,2},{4,5},{5,4},{6,7},{7,6},{8,9},{9,8},{10,11... | collective-permute-start | bytes 3145736 | tf_op jit(solution)/shard_map/ppermute | solution.py:442
  5.9 4.7 %collective-permute-start.1 = (bf16[2,16,16]{2,1,0:T(8,128)(2,1)S(1)}, bf16[2,16,16]{2,1,0:T(8,128)(2,1)S(1)}, u32[]{:S(2)}, u32[]{:S(2)}) collective-permute-start(bf16[2,16,16]{2,1,0:T(8,128)(2,1)S(1)} %pad_maximum_fusion.refs_0_), channel_id=1, source_target_pairs={{0,8},{4,12},{8,0},{12,4},{16,24},{20,28},{24,16},{28,20},{1,9},{5... | collective-permute-start | bytes 3080 | tf_op jit(solution)/shard_map/ppermute | solution.py:437
  7.6 5.4 %collective-permute-start.2 = (bf16[2,16,16]{2,1,0:T(8,128)(2,1)S(1)}, bf16[2,16,16]{2,1,0:T(8,128)(2,1)S(1)}, u32[]{:S(2)}, u32[]{:S(2)}) collective-permute-start(bf16[2,16,16]{2,1,0:T(8,128)(2,1)S(1)} %pad_maximum_fusion.refs_0_), channel_id=1, source_target_pairs={{0,24},{4,28},{8,16},{12,20},{16,8},{20,12},{24,0},{28,4},{1,25},{... | collective-permute-start | bytes 3080 | tf_op jit(solution)/shard_map/ppermute | solution.py:437
  10.1 4.5 %collective-permute-start.3 = (bf16[2,16,16]{2,1,0:T(8,128)(2,1)S(1)}, bf16[2,16,16]{2,1,0:T(8,128)(2,1)S(1)}, u32[]{:S(2)}, u32[]{:S(2)}) collective-permute-start(bf16[2,16,16]{2,1,0:T(8,128)(2,1)S(1)} %pad_maximum_fusion.refs_0_), channel_id=1, source_target_pairs={{0,16},{4,20},{8,24},{12,28},{16,0},{20,4},{24,8},{28,12},{1,17},{... | collective-permute-start | bytes 3080 | tf_op jit(solution)/shard_map/ppermute | solution.py:437
  10.5 4.1 %copy-start = (bf16[16]{0:T(256)(128)(2,1)S(1)}, bf16[16]{0:T(256)(128)(2,1)}, u32[]{:S(2)}) copy-start(bf16[16]{0:T(256)(128)(2,1)} %param.11) | copy-start | bytes 100
  15.5 7.1 %collective-permute-start.5 = (bf16[1,8,128,128]{3,2,1,0:T(8,128)(2,1)S(1)}, bf16[1,8,128,128]{3,2,1,0:T(8,128)(2,1)S(1)}, u32[]{:S(2)}, u32[]{:S(2)}) collective-permute-start(bf16[1,8,128,128]{3,2,1,0:T(8,128)(2,1)S(1)} %get-tuple-element.41), channel_id=1, source_target_pairs={{0,2},{1,3},{2,0},{3,1},{4,6},{5,7},{6,4},{7,5},{8,10},{9,11},{10,... | collective-permute-start | bytes 786440 | tf_op jit(solution)/shard_map/ppermute | solution.py:484
  17.3 5.3 %collective-permute-start.6 = (f32[8,128]{1,0:T(8,128)S(1)}, f32[8,128]{1,0:T(8,128)S(1)}, u32[]{:S(2)}, u32[]{:S(2)}) collective-permute-start(f32[8,128]{1,0:T(8,128)S(1)} %kappa.1), channel_id=1, source_target_pairs={{0,2},{1,3},{2,0},{3,1},{4,6},{5,7},{6,4},{7,5},{8,10},{9,11},{10,... | collective-permute-start | bytes 12296 | tf_op jit(solution)/shard_map/ppermute | solution.py:487
  20.4 7.8 %collective-permute-start.7 = (bf16[1,9,128,128]{3,2,1,0:T(8,128)(2,1)S(1)}, bf16[1,9,128,128]{3,2,1,0:T(8,128)(2,1)S(1)}, u32[]{:S(2)}, u32[]{:S(2)}) collective-permute-start(bf16[1,9,128,128]{3,2,1,0:T(8,128)(2,1)S(1)} %get-tuple-element.50), channel_id=1, source_target_pairs={{0,1},{1,0},{2,3},{3,2},{4,5},{5,4},{6,7},{7,6},{8,9},{9,8},{10,11... | collective-permute-start | bytes 884744 | tf_op jit(solution)/shard_map/ppermute | solution.py:488
  24.4 3.8 %collective-permute-start.8 = (bf16[1,9,128,128]{3,2,1,0:T(8,128)(2,1)S(1)}, bf16[1,9,128,128]{3,2,1,0:T(8,128)(2,1)S(1)}, u32[]{:S(2)}, u32[]{:S(2)}) collective-permute-start(bf16[1,9,128,128]{3,2,1,0:T(8,128)(2,1)S(1)} %get-tuple-element.52), channel_id=1, source_target_pairs={{0,1},{1,0},{2,3},{3,2},{4,5},{5,4},{6,7},{7,6},{8,9},{9,8},{10,11... | collective-permute-start | bytes 884744 | tf_op jit(solution)/shard_map/ppermute | solution.py:517
  24.4 11.1 %all-to-all-start = ((f32[32,2,128]{2,1,0:T(2,128)}), f32[32,2,128]{2,1,0:T(2,128)S(1)}, u32[]{:S(2)}, u32[]{:S(2)}) async-start(f32[32,2,128]{2,1,0:T(2,128)} %get-tuple-element.56), calls=%async_computation | async-start | bytes 65536 | tf_op jit(solution)/shard_map/all_to_all | solution.py:516

commit v6 on v5

--- a/solution.py
+++ b/solution.py
@@ -196,7 +196,7 @@
     scale_ref[0] = tail
     scale_ref[1] = head
     causal = iota((count, count), 0) >= iota((count, count), 1)
-    until = jnp.where(iota((count, count), 0) <= iota((count, count), 1), 1.0, 0.0).astype(BF16)
+    until = jnp.where(causal, 1.0, 0.0).astype(BF16)
     both = (keep_ref, recv_ref)
     side = chip
     if pair:
@@ -232,10 +232,10 @@
                 attn_ref[0, rel, j] = query
                 attn_ref[1, rel, j] = key
                 slopes.append(slope_row(ref, 0, j, query) + slope_row(ref, 1, j, key))
-            run = nn(hi_lo(ref[0, j].astype(F32) * rows_ref[1, at : at + 1, :]), until)
-            hi, lo = split_two(run[:width] + run[width:])
-            run_ref[0, rel, j] = hi
-            run_ref[1, rel, j] = lo
+            run = nt(until, hi_lo(ref[0, j].astype(F32) * rows_ref[1, at : at + 1, :]))
+            hi, lo = split_two(run[:, :width] + run[:, width:])
+            run_ref[0, j, rel * count : (rel + 1) * count] = hi
+            run_ref[1, j, rel * count : (rel + 1) * count] = lo
         dg_ref[rel] = jnp.concatenate(slopes, 0)
 
 
@@ -246,12 +246,9 @@
     row = iota((half, width), 0)
     total = jnp.zeros((half, width), F32)
     for j in range(0, half, 2):
-        planes = [
-            jnp.concatenate([run_ref[p, rel, j : j + 2].reshape(2 * width, count) for rel in range(2)], 1)
-            for p in range(2)
-        ]
-        got = nt(lhs, planes[0])
-        got = got[:half] + (got[half:] + nt(lhs[:half], planes[1]))
+        planes = [jnp.concatenate([run_ref[p, j], run_ref[p, j + 1]], 1) for p in range(2)]
+        got = nn(lhs, planes[0])
+        got = got[:half] + (got[half:] + nn(lhs[:half], planes[1]))
         total = total + jnp.where(row == j, got[:, :width], 0.0) + jnp.where(row == j + 1, got[:, width:], 0.0)
     return total
 
@@ -260,7 +257,7 @@
     final = group == groups - 1
     earlier, refs = (refs[:3], refs[3:]) if group else ((), refs)
     if final:
-        kappa_ref, run_ref, mine_ref, send_ref, suffix_ref, pieces_ref, scale_ref = refs
+        kappa_ref, run_ref, mine_ref, send_ref, suffix_ref, *total_refs, pieces_ref, scale_ref = refs
     else:
         mine_ref, send_ref, slope_ref, scale_ref = refs
     par, chip = place()
@@ -315,12 +312,15 @@
     piece, slot = width // parts, width // half
     here = iota((half, width), 1) // slot == iota((half, width), 0)
     totals = jnp.sum(jnp.where(here, total, 0.0), 0, keepdims=True)
+    for ref in total_refs:
+        ref[...] = total
     for i in range(parts):
         turned = partial if i == 0 else pltpu.roll(partial, width - i * piece, 1)
         turned = pltpu.roll(turned, 0, 1, stride=slot, stride_axis=0)
-        line = jnp.sum(jnp.where(here, turned, 0.0), 0, keepdims=True)
-        sent = jnp.concatenate([line, totals], 0)
-        pieces_ref[pl.ds(i * ranks, ranks)] = jnp.broadcast_to(sent[None], (ranks, 2, width))
+        sent = jnp.sum(jnp.where(here, turned, 0.0), 0, keepdims=True)
+        if not pair:
+            sent = jnp.concatenate([sent, totals], 0)
+        pieces_ref[pl.ds(i * ranks, ranks)] = jnp.broadcast_to(sent[None], (ranks, *sent.shape))
     suffix = exact(jnp.concatenate([own, other], 0), iota((count, count), 0) >= iota((count, count), 1))
     suffix_ref[...] = suffix[:half]
     for at in range(sides):
@@ -359,31 +359,46 @@
         rise_ref[t] = rise[:, t : t + 1] * gate
 
 
-def last_kernel(base_ref, rise_ref, pieces_ref, out_ref, grad_ref, buf, small, sems):
-    _, chip = place()
+def sum_pieces(pieces_ref, piece, half):
+    everyone, rows, width = pieces_ref.shape
+    slot = width // half
+    here = iota((half, width), 1) // slot == iota((half, width), 0)
+    total = jnp.sum(pieces_ref[...].reshape(everyone // 2, 2, rows, width)[:, :, 0], 0)
+    fold = iota((width, slot), 0) % slot == iota((width, slot), 1)
+    lines = [jnp.where(here, total[c : c + 1], 0.0) for c in range(2)]
+    return exact(jnp.concatenate(lines, 0), fold)[:, :piece]
+
+
+def gate_gradient_kernel(pieces_ref, grad_ref):
+    heads, piece = grad_ref.shape
+    grad_ref[...] = sum_pieces(pieces_ref, piece, heads // 2)
+
+
+def key_gradient_kernel(pair, base_ref, rise_ref, *refs):
+    par, chip = place()
     count, heads, width = base_ref.shape
     half = heads // 2
-    parts, ranks = lax.axis_size("dp"), lax.axis_size("ctx")
-    groups, slot = ranks // 2, width // half
-    own = pieces_ref[pl.ds(lax.axis_index("dp") * ranks, ranks)].reshape(groups, 2, 2, width)
-    beyond = sum(jnp.where(m > chip, 1.0, 0.0) * own[m, :, 1] for m in range(groups))
-    lane, sub = iota((half, width), 1), iota((half, width), 0)
-    chosen = [
-        jnp.sum(jnp.where(lane == sub * slot, beyond[c : c + 1], 0.0), 1, keepdims=True) for c in range(2)
-    ]
-    after = jnp.broadcast_to(jnp.concatenate(chosen, 0), (heads, width))
+    if pair:
+        ahead_ref, across_ref, out_ref, buf, line_ref, sems = refs
+        line_ref[pl.ds(par * half, half), :] = ahead_ref[...]
+        line_ref[pl.ds((1 - par) * half, half), :] = across_ref[...]
+        after = jnp.where(chip == 0, 1.0, 0.0) * line_ref[...]
+    else:
+        pieces_ref, out_ref, buf, sems = refs
+        ranks = lax.axis_size("ctx")
+        groups, slot = ranks // 2, width // half
+        lane, sub = iota((half, width), 1), iota((half, width), 0)
+        own = pieces_ref[pl.ds(lax.axis_index("dp") * ranks, ranks)].reshape(groups, 2, 2, width)
+        beyond = sum(jnp.where(m > chip, 1.0, 0.0) * own[m, :, 1] for m in range(groups))
+        chosen = [
+            jnp.sum(jnp.where(lane == sub * slot, beyond[c : c + 1], 0.0), 1, keepdims=True) for c in range(2)
+        ]
+        after = jnp.broadcast_to(jnp.concatenate(chosen, 0), (heads, width))
     for t in range(count):
         buf[t] = (base_ref[t] + after * rise_ref[t]).astype(BF16)
-    key_copy = pltpu.make_async_copy(buf, out_ref.at[0], sems.at[0])
-    key_copy.start()
-    total = jnp.sum(pieces_ref[...].reshape(parts * groups, 2, 2, width)[:, :, 0], 0)
-    fold = iota((width, slot), 0) % slot == iota((width, slot), 1)
-    lines = [jnp.where(lane // slot == sub, total[c : c + 1], 0.0) for c in range(2)]
-    small[...] = exact(jnp.concatenate(lines, 0), fold)[:, : width // parts]
-    grad_copy = pltpu.make_async_copy(small, grad_ref, sems.at[1])
-    grad_copy.start()
-    key_copy.wait()
-    grad_copy.wait()
+    copy = pltpu.make_async_copy(buf, out_ref.at[0], sems.at[0])
+    copy.start()
+    copy.wait()
 
 
 def across_chips(total, ends, ranks, reverse):
@@ -464,7 +479,7 @@
     attn_shape = shape(sides, 2, half, width, count, dtype=F32)
     mine_shape = shape(sides, half, width, count)
     send_shape = shape(sides, half + 1, width, count)
-    run_shape = shape(2, 2, half, width, count)
+    run_shape = shape(2, half, 2 * count, width)
 
     def inside(*outs):
         return call(
@@ -500,7 +515,9 @@
     for group, come in enumerate(states):
         final = group == chunks - 1
         outs = (
-            (shape(half, count, dtype=F32), shape(parts * ranks, 2, width, dtype=F32))
+            (shape(half, count, dtype=F32),)
+            + ((shape(half, width, dtype=F32),) if pair else ())
+            + (shape(parts * ranks, 1 if pair else 2, width, dtype=F32),)
             if final
             else (shape(2, half // chunks, count, dtype=F32),)
         )
@@ -512,7 +529,9 @@
             [lines],
             1.0,
         )
-    mine, send, suffix, pieces = earlier
+    mine, send, suffix, *totals, pieces = earlier
+    if pair:
+        totals = [lax.ppermute(totals[0], "ctx", [(i, i ^ far) for i in range(ranks)]) for far in (2, 3)]
     pieces = lax.all_to_all(pieces, ("dp", "ctx"), 0, 0, tiled=True)
     recv_out = lax.ppermute(send, "ctx", swap)
     whole = shape(1, count, heads, width)
@@ -525,18 +544,25 @@
         [pltpu.VMEM((2, heads, count), F32), pltpu.VMEM((2, (count + 1) * heads, width), F32)],
         2.0,
     )
-    key_grad, gate_grad = call(
-        last_kernel,
+    (key_grad,) = call(
+        functools.partial(key_gradient_kernel, pair),
         "key_gradient",
-        (whole, shape(heads, width // parts, dtype=F32)),
-        (base, rise, pieces),
-        [
-            pltpu.VMEM((count, heads, width), BF16),
-            pltpu.VMEM((heads, width // parts), F32),
-            pltpu.SemaphoreType.DMA((2,)),
-        ],
+        (whole,),
+        (base, rise, *(totals if pair else (pieces,))),
+        [pltpu.VMEM((count, heads, width), BF16)]
+        + ([pltpu.VMEM((heads, width), F32)] if pair else [])
+        + [pltpu.SemaphoreType.DMA((1,))],
         1.0,
-        out_specs=(ANY, ANY),
+        out_specs=(ANY,),
+    )
+    pieces, key_grad = lax.optimization_barrier((pieces, key_grad))
+    (gate_grad,) = call(
+        gate_gradient_kernel,
+        "gate_gradient",
+        (shape(heads, width // parts, dtype=F32),),
+        (pieces,),
+        (),
+        0.5,
     )
     return query_grad, key_grad, gate_grad
 

time: 36.7 us -> 36.2 us (0.986)
  waiting for transfers between devices: 11.6 us -> 8.35 us
  starting transfers between devices: 13.4 us -> 15.3 us
  Pallas kernels: 10.8 us -> 11.6 us
    all_to_all x1, waiting for transfers between devices: 5.29 us -> 1.33 us  [per_device(): pieces = lax.all_to_all(pieces, ('dp', 'ctx'), 0, 0, tiled=True)]
    ppermute x0 -> x2, starting transfers between devices: none -> 1.84 us  [per_device(): lax.ppermute(totals[0], 'ctx', [(i, i ^ far) for i in range(ranks)])]
    ppermute x0 -> x2, waiting for transfers between devices: none -> 1.08 us  [per_device(): lax.ppermute(totals[0], 'ctx', [(i, i ^ far) for i in range(ranks)])]
    pallas_call x8 -> x9, Pallas kernels: 10.8 us -> 11.6 us  [call(): pl.pallas_call(kernel, out_shape=out_shape, in_specs=in_specs or [VMEM] *...]
  transfers between devices with their start and end apart: 10 -> 12, of which waited for: 4 -> 5; matrix products, arithmetic and copies ran while one was open for 0% -> 0% of each run, Pallas kernels for 24% -> 28%
where the time goes in v6:
time: 36.2 us; the launch traced here: 36 us
  starting transfers between devices  15.3 us (42%)
  Pallas kernels  11.6 us (32%)
  waiting for transfers between devices  8.35 us (23%)
  between operations  0.73 us (2%)
    pallas_call x9, Pallas kernels, call(): pl.pallas_call(kernel, out_shape=out_shape, in_specs=in_specs or [VMEM] *...  11.6 us
    ppermute x3, starting transfers between devices, per_device(): lax.ppermute(two, 'dp', [(i, i ^ far) for i in range(parts)])  4.35 us
    ppermute x3, waiting for transfers between devices, per_device(): lax.ppermute(two, 'dp', [(i, i ^ far) for i in range(parts)])  4.12 us
    all_to_all x1, starting transfers between devices, per_device(): pieces = lax.all_to_all(pieces, ('dp', 'ctx'), 0, 0, tiled=True)  3.8 us
    ppermute x1, starting transfers between devices, per_device(): nearby = lax.ppermute(gate_weight, 'dp', [(i, i ^ 1) for i in range(parts)])  3.03 us
    ppermute x2, starting transfers between devices, per_device(): lax.ppermute(totals[0], 'ctx', [(i, i ^ far) for i in range(ranks)])  1.84 us
    ppermute x1, waiting for transfers between devices, per_device(): kappa = lax.ppermute(kappa, 'ctx', opposite)  1.82 us
    ppermute x1, starting transfers between devices, per_device(): states = [lax.ppermute(total, 'ctx', opposite) for total in totals]  1.55 us
  transfers between devices with their start and end apart: 12, of which 5 were waited for; matrix products, arithmetic and copies ran while one was open for 0% of the time, Pallas kernels for 28%

profile of v6, /device:TPU:0, one launch (start us, length us, event | category | flops | bytes accessed | tf_op | source)
XLA Modules:
  0.0 36.0 jit_solution(2187688046308313080)
XLA Ops:
  0.6 3.0 %collective-permute-start = (bf16[16,16]{1,0:T(8,128)(2,1)}, bf16[16,16]{1,0:T(8,128)(2,1)S(1)}, u32[]{:S(2)}, u32[]{:S(2)}) collective-permute-start(bf16[16,16]{1,0:T(8,128)(2,1)} %gate_ref.1), channel_id=1, source_target_pairs={{0,4},{4,0},{8,12},{12,8},{16,20},{20,16},{24,28},{28,24},{1,5},{5... | collective-permute-start | bytes 1544 | tf_op jit(solution)/shard_map/ppermute | solution.py:448
  3.7 2.1 %split_heads.1 = (bf16[4,8,128,128]{3,2,1,0:T(8,128)(2,1)S(1)}, bf16[4,8,128,128]{3,2,1,0:T(8,128)(2,1)S(1)}, bf16[16,16]{1,0:T(8,128)(2,1)S(1)}) custom-call(bf16[1,128,16,128]{3,2,1,0:T(8,128)(2,1)} %k_ref.1, bf16[1,128,16,128]{3,2,1,0:T(8,128)(2,1)} %q_ref.1, bf16[1,128,16,128]{3,2,1,0:T(8,128)(2,1)} %v_ref.1, bf16[1,128,16,128]{3,2,1,0:T(8,128)(2,1)} %g_ref.1, ...), custom_call_target="tpu_custom_call" | custom-call | bytes 9000000 | tf_op jit(solution)/shard_map/split_heads/pallas_call | solution.py:57
  5.8 0.1 collective-permute-start.4
  5.9 1.8 %collective-permute-start.1 = (bf16[2,16,16]{2,1,0:T(8,128)(2,1)S(1)}, bf16[2,16,16]{2,1,0:T(8,128)(2,1)S(1)}, u32[]{:S(2)}, u32[]{:S(2)}) collective-permute-start(bf16[2,16,16]{2,1,0:T(8,128)(2,1)S(1)} %pad_maximum_fusion.refs_0_), channel_id=1, source_target_pairs={{0,8},{4,12},{8,0},{12,4},{16,24},{20,28},{24,16},{28,20},{1,9},{5... | collective-permute-start | bytes 3080 | tf_op jit(solution)/shard_map/ppermute | solution.py:452
  7.6 2.5 %collective-permute-start.2 = (bf16[2,16,16]{2,1,0:T(8,128)(2,1)S(1)}, bf16[2,16,16]{2,1,0:T(8,128)(2,1)S(1)}, u32[]{:S(2)}, u32[]{:S(2)}) collective-permute-start(bf16[2,16,16]{2,1,0:T(8,128)(2,1)S(1)} %pad_maximum_fusion.refs_0_), channel_id=1, source_target_pairs={{0,24},{4,28},{8,16},{12,20},{16,8},{20,12},{24,0},{28,4},{1,25},{... | collective-permute-start | bytes 3080 | tf_op jit(solution)/shard_map/ppermute | solution.py:452
  10.1 0.1 collective-permute-start.3
  10.2 0.3 products.1.product_ref
  10.5 2.5 %collective-permute-done.2.refs_3_ = bf16[2,16,16]{2,1,0:T(8,128)(2,1)S(1)} collective-permute-done((bf16[2,16,16]{2,1,0:T(8,128)(2,1)S(1)}, bf16[2,16,16]{2,1,0:T(8,128)(2,1)S(1)}, u32[]{:S(2)}, u32[]{:S(2)}) %collective-permute-start.2) | collective-permute-done | bytes 1056 | tf_op jit(solution)/shard_map/ppermute | solution.py:452
  13.1 1.6 %collective-permute-done.3.refs_2_ = bf16[2,16,16]{2,1,0:T(8,128)(2,1)S(1)} collective-permute-done((bf16[2,16,16]{2,1,0:T(8,128)(2,1)S(1)}, bf16[2,16,16]{2,1,0:T(8,128)(2,1)S(1)}, u32[]{:S(2)}, u32[]{:S(2)}) %collective-permute-start.3) | collective-permute-done | bytes 1056 | tf_op jit(solution)/shard_map/ppermute | solution.py:452
  14.6 0.9 %gate_states.1 = (bf16[1,8,128,128]{3,2,1,0:T(8,128)(2,1)S(1)}, bf16[1,8,128,128]{3,2,1,0:T(8,128)(2,1)S(1)}, f32[2,16,128]{2,1,0:T(8,128)S(1)}, f32[2,16,128]{2,1,0:T(8,128)S(1)}) custom-call(bf16[2,16,16]{2,1,0:T(8,128)(2,1)S(1)} %pad_maximum_fusion.refs_0_, bf16[2,16,16]{2,1,0:T(8,128)(2,1)S(1)} %collective-permute-done.1.refs_1_, ...), custom_call_target="tpu_custom_call" | custom-call | bytes 3900000 | tf_op jit(solution)/shard_map/gate_states/pallas_call | solution.py:57
  15.5 1.6 %collective-permute-start.5 = (bf16[1,8,128,128]{3,2,1,0:T(8,128)(2,1)S(1)}, bf16[1,8,128,128]{3,2,1,0:T(8,128)(2,1)S(1)}, u32[]{:S(2)}, u32[]{:S(2)}) collective-permute-start(bf16[1,8,128,128]{3,2,1,0:T(8,128)(2,1)S(1)} %get-tuple-element.42), channel_id=1, source_target_pairs={{0,2},{1,3},{2,0},{3,1},{4,6},{5,7},{6,4},{7,5},{8,10},{9,11},{10,... | collective-permute-start | bytes 786440 | tf_op jit(solution)/shard_map/ppermute | solution.py:499
  17.1 0.3 kappa.1
  17.3 0.6 %collective-permute-start.6 = (f32[8,128]{1,0:T(8,128)S(1)}, f32[8,128]{1,0:T(8,128)S(1)}, u32[]{:S(2)}, u32[]{:S(2)}) collective-permute-start(f32[8,128]{1,0:T(8,128)S(1)} %kappa.1), channel_id=1, source_target_pairs={{0,2},{1,3},{2,0},{3,1},{4,6},{5,7},{6,4},{7,5},{8,10},{9,11},{10,... | collective-permute-start | bytes 12296 | tf_op jit(solution)/shard_map/ppermute | solution.py:502
  17.9 2.8 %inside_block.1 = (f32[1,2,8,128,128]{4,3,2,1,0:T(8,128)S(1)}, bf16[2,8,256,128]{3,2,1,0:T(8,128)(2,1)S(1)}, f32[2,8,128]{2,1,0:T(8,128)S(1)}, f32[1,8,128,128]{...) custom-call(bf16[4,8,128,128]{3,2,1,0:T(8,128)(2,1)S(1)} %get-tuple-element.35.keep_ref.ref, ...), custom_call_target="tpu_custom_call" | custom-call | bytes 12000000 | tf_op jit(solution)/shard_map/inside_block/pallas_call | solution.py:57
  20.7 0.1 collective-permute-start.7
  20.8 1.8 %collective-permute-done.6.refs_0_ = f32[8,128]{1,0:T(8,128)S(1)} collective-permute-done((f32[8,128]{1,0:T(8,128)S(1)}, f32[8,128]{1,0:T(8,128)S(1)}, u32[]{:S(2)}, u32[]{:S(2)}) %collective-permute-start.6) | collective-permute-done | bytes 4128 | tf_op jit(solution)/shard_map/ppermute | solution.py:502
  22.6 1.7 %outside_block.1 = (bf16[1,8,128,128]{3,2,1,0:T(8,128)(2,1)S(1)}, bf16[1,9,128,128]{3,2,1,0:T(8,128)(2,1)S(1)}, f32[8,128]{1,0:T(8,128)S(1)}, f32[8,128]{1,0:T(8,128)S(1)}, f32[32,1,128]{2,1,0:T(1,128)}) custom-call(bf16[4,8,128,128]{3,2,1,0:T(8,128)(2,1)S(1)} %get-tuple-element.35.keep_ref.refs_5_, ...), custom_call_target="tpu_custom_call" | custom-call | bytes 3000000 | tf_op jit(solution)/shard_map/outside_block/pallas_call | solution.py:57
  24.3 3.8 %all-to-all-start = ((f32[32,1,128]{2,1,0:T(1,128)}), f32[32,1,128]{2,1,0:T(1,128)S(1)}, u32[]{:S(2)}, u32[]{:S(2)}) async-start(f32[32,1,128]{2,1,0:T(1,128)} %get-tuple-element.55), calls=%async_computation | async-start | bytes 32768 | tf_op jit(solution)/shard_map/all_to_all | solution.py:535
  28.1 1.8 %collective-permute-start.9 = (f32[8,128]{1,0:T(8,128)S(1)}, f32[8,128]{1,0:T(8,128)S(1)}, u32[]{:S(2)}, u32[]{:S(2)}) collective-permute-start(f32[8,128]{1,0:T(8,128)S(1)} %get-tuple-element.58), channel_id=1, source_target_pairs={{0,2},{1,3},{2,0},{3,1},{4,6},{5,7},{6,4},{7,5},{8,10},{9,11},{10,... | collective-permute-start | bytes 12296 | tf_op jit(solution)/shard_map/ppermute | solution.py:534
  30.0 1.9 %merge_heads.1 = (bf16[1,128,16,128]{3,2,1,0:T(8,128)(2,1)}, f32[128,16,128]{2,1,0:T(8,128)S(1)}, f32[128,16,128]{2,1,0:T(8,128)S(1)}) custom-call(f32[2,16,128]{2,1,0:T(8,128)S(1)} %get-tuple-element.40.gate_ref, f32[8,128]{1,0:T(8,128)S(1)} %get-tuple-element.49.suffix_ref, f32[2,16,128]{2,1,0:T(8,128)S(1)} %get-tuple-element.41.rows_ref, ...), custom_call_target="tpu_custom_call" | custom-call | bytes 6000000 | tf_op jit(solution)/shard_map/merge_heads/pallas_call | solution.py:57
  31.9 1.1 %collective-permute-done.10.refs_1_ = f32[8,128]{1,0:T(8,128)S(1)} collective-permute-done((f32[8,128]{1,0:T(8,128)S(1)}, f32[8,128]{1,0:T(8,128)S(1)}, u32[]{:S(2)}, u32[]{:S(2)}) %collective-permute-start.10) | collective-permute-done | bytes 4128 | tf_op jit(solution)/shard_map/ppermute | solution.py:534
  33.0 0.9 %key_gradient.1 = bf16[1,128,16,128]{3,2,1,0:T(8,128)(2,1)} custom-call(f32[128,16,128]{2,1,0:T(8,128)S(1)} %get-tuple-element.56.base_ref, f32[128,16,128]{2,1,0:T(8,128)S(1)} %get-tuple-element.57.rise_ref, f32[8,128]{1,0:T(8,128)S(1)} %collective-permute-done.9.refs_0_, f32[8,128]{1,0:T(8,128)S(1)} %collective-permute-done.10.refs_1_), custom_call_target="tpu_custom_call" | custom-call | bytes 3000000 | tf_op jit(solution)/shard_map/key_gradient/pallas_call | solution.py:57
  33.9 1.3 %all-to-all-done.pieces_ref = f32[32,1,128]{2,1,0:T(1,128)S(1)} async-done(((f32[32,1,128]{2,1,0:T(1,128)}), f32[32,1,128]{2,1,0:T(1,128)S(1)}, u32[]{:S(2)}, u32[]{:S(2)}) %all-to-all-start) | async-done | bytes 16416 | tf_op jit(solution)/shard_map/all_to_all | solution.py:535
  35.3 0.8 %gate_gradient.1 = f32[16,16]{1,0:T(8,128)} custom-call(f32[32,1,128]{2,1,0:T(1,128)S(1)} %all-to-all-done.pieces_ref), custom_call_target="tpu_custom_call" | custom-call | bytes 1500000 | tf_op jit(solution)/shard_map/gate_gradient/pallas_call | solution.py:57
  (12 shorter events, 0.0 us)
Async XLA Ops:
  0.6 5.1 %collective-permute-start = (bf16[16,16]{1,0:T(8,128)(2,1)}, bf16[16,16]{1,0:T(8,128)(2,1)S(1)}, u32[]{:S(2)}, u32[]{:S(2)}) collective-permute-start(bf16[16,16]{1,0:T(8,128)(2,1)} %gate_ref.1), channel_id=1, source_target_pairs={{0,4},{4,0},{8,12},{12,8},{16,20},{20,16},{24,28},{28,24},{1,5},{5... | collective-permute-start | bytes 1544 | tf_op jit(solution)/shard_map/ppermute | solution.py:448
  5.8 8.9 %collective-permute-start.4 = (bf16[4,8,128,128]{3,2,1,0:T(8,128)(2,1)S(1)}, bf16[4,8,128,128]{3,2,1,0:T(8,128)(2,1)S(1)}, u32[]{:S(2)}, u32[]{:S(2)}) collective-permute-start(bf16[4,8,128,128]{3,2,1,0:T(8,128)(2,1)S(1)} %get-tuple-element.39), channel_id=1, source_target_pairs={{0,1},{1,0},{2,3},{3,2},{4,5},{5,4},{6,7},{7,6},{8,9},{9,8},{10,11... | collective-permute-start | bytes 3145736 | tf_op jit(solution)/shard_map/ppermute | solution.py:457
  5.9 4.7 %collective-permute-start.1 = (bf16[2,16,16]{2,1,0:T(8,128)(2,1)S(1)}, bf16[2,16,16]{2,1,0:T(8,128)(2,1)S(1)}, u32[]{:S(2)}, u32[]{:S(2)}) collective-permute-start(bf16[2,16,16]{2,1,0:T(8,128)(2,1)S(1)} %pad_maximum_fusion.refs_0_), channel_id=1, source_target_pairs={{0,8},{4,12},{8,0},{12,4},{16,24},{20,28},{24,16},{28,20},{1,9},{5... | collective-permute-start | bytes 3080 | tf_op jit(solution)/shard_map/ppermute | solution.py:452
  7.6 5.4 %collective-permute-start.2 = (bf16[2,16,16]{2,1,0:T(8,128)(2,1)S(1)}, bf16[2,16,16]{2,1,0:T(8,128)(2,1)S(1)}, u32[]{:S(2)}, u32[]{:S(2)}) collective-permute-start(bf16[2,16,16]{2,1,0:T(8,128)(2,1)S(1)} %pad_maximum_fusion.refs_0_), channel_id=1, source_target_pairs={{0,24},{4,28},{8,16},{12,20},{16,8},{20,12},{24,0},{28,4},{1,25},{... | collective-permute-start | bytes 3080 | tf_op jit(solution)/shard_map/ppermute | solution.py:452
  10.1 4.5 %collective-permute-start.3 = (bf16[2,16,16]{2,1,0:T(8,128)(2,1)S(1)}, bf16[2,16,16]{2,1,0:T(8,128)(2,1)S(1)}, u32[]{:S(2)}, u32[]{:S(2)}) collective-permute-start(bf16[2,16,16]{2,1,0:T(8,128)(2,1)S(1)} %pad_maximum_fusion.refs_0_), channel_id=1, source_target_pairs={{0,16},{4,20},{8,24},{12,28},{16,0},{20,4},{24,8},{28,12},{1,17},{... | collective-permute-start | bytes 3080 | tf_op jit(solution)/shard_map/ppermute | solution.py:452
  10.5 4.1 %copy-start = (bf16[16]{0:T(256)(128)(2,1)S(1)}, bf16[16]{0:T(256)(128)(2,1)}, u32[]{:S(2)}) copy-start(bf16[16]{0:T(256)(128)(2,1)} %param.11) | copy-start | bytes 100
  15.5 7.1 %collective-permute-start.5 = (bf16[1,8,128,128]{3,2,1,0:T(8,128)(2,1)S(1)}, bf16[1,8,128,128]{3,2,1,0:T(8,128)(2,1)S(1)}, u32[]{:S(2)}, u32[]{:S(2)}) collective-permute-start(bf16[1,8,128,128]{3,2,1,0:T(8,128)(2,1)S(1)} %get-tuple-element.42), channel_id=1, source_target_pairs={{0,2},{1,3},{2,0},{3,1},{4,6},{5,7},{6,4},{7,5},{8,10},{9,11},{10,... | collective-permute-start | bytes 786440 | tf_op jit(solution)/shard_map/ppermute | solution.py:499
  17.3 5.3 %collective-permute-start.6 = (f32[8,128]{1,0:T(8,128)S(1)}, f32[8,128]{1,0:T(8,128)S(1)}, u32[]{:S(2)}, u32[]{:S(2)}) collective-permute-start(f32[8,128]{1,0:T(8,128)S(1)} %kappa.1), channel_id=1, source_target_pairs={{0,2},{1,3},{2,0},{3,1},{4,6},{5,7},{6,4},{7,5},{8,10},{9,11},{10,... | collective-permute-start | bytes 12296 | tf_op jit(solution)/shard_map/ppermute | solution.py:502
  20.7 9.2 %collective-permute-start.7 = (bf16[1,9,128,128]{3,2,1,0:T(8,128)(2,1)S(1)}, bf16[1,9,128,128]{3,2,1,0:T(8,128)(2,1)S(1)}, u32[]{:S(2)}, u32[]{:S(2)}) collective-permute-start(bf16[1,9,128,128]{3,2,1,0:T(8,128)(2,1)S(1)} %get-tuple-element.51), channel_id=1, source_target_pairs={{0,1},{1,0},{2,3},{3,2},{4,5},{5,4},{6,7},{7,6},{8,9},{9,8},{10,11... | collective-permute-start | bytes 884744 | tf_op jit(solution)/shard_map/ppermute | solution.py:503
  24.3 5.7 %collective-permute-start.8 = (bf16[1,9,128,128]{3,2,1,0:T(8,128)(2,1)S(1)}, bf16[1,9,128,128]{3,2,1,0:T(8,128)(2,1)S(1)}, u32[]{:S(2)}, u32[]{:S(2)}) collective-permute-start(bf16[1,9,128,128]{3,2,1,0:T(8,128)(2,1)S(1)} %get-tuple-element.53), channel_id=1, source_target_pairs={{0,1},{1,0},{2,3},{3,2},{4,5},{5,4},{6,7},{7,6},{8,9},{9,8},{10,11... | collective-permute-start | bytes 884744 | tf_op jit(solution)/shard_map/ppermute | solution.py:536
  24.3 11.0 %all-to-all-start = ((f32[32,1,128]{2,1,0:T(1,128)}), f32[32,1,128]{2,1,0:T(1,128)S(1)}, u32[]{:S(2)}, u32[]{:S(2)}) async-start(f32[32,1,128]{2,1,0:T(1,128)} %get-tuple-element.55), calls=%async_computation | async-start | bytes 32768 | tf_op jit(solution)/shard_map/all_to_all | solution.py:535
  28.1 3.8 %collective-permute-start.9 = (f32[8,128]{1,0:T(8,128)S(1)}, f32[8,128]{1,0:T(8,128)S(1)}, u32[]{:S(2)}, u32[]{:S(2)}) collective-permute-start(f32[8,128]{1,0:T(8,128)S(1)} %get-tuple-element.58), channel_id=1, source_target_pairs={{0,2},{1,3},{2,0},{3,1},{4,6},{5,7},{6,4},{7,5},{8,10},{9,11},{10,... | collective-permute-start | bytes 12296 | tf_op jit(solution)/shard_map/ppermute | solution.py:534
  29.9 3.0 %collective-permute-start.10 = (f32[8,128]{1,0:T(8,128)S(1)}, f32[8,128]{1,0:T(8,128)S(1)}, u32[]{:S(2)}, u32[]{:S(2)}) collective-permute-start(f32[8,128]{1,0:T(8,128)S(1)} %get-tuple-element.58), channel_id=1, source_target_pairs={{0,3},{1,2},{2,1},{3,0},{4,7},{5,6},{6,5},{7,4},{8,11},{9,10},{10,... | collective-permute-start | bytes 12296 | tf_op jit(solution)/shard_map/ppermute | solution.py:534

commit v7 on v6

--- a/solution.py
+++ b/solution.py
@@ -196,7 +196,7 @@
     scale_ref[0] = tail
     scale_ref[1] = head
     causal = iota((count, count), 0) >= iota((count, count), 1)
-    until = jnp.where(causal, 1.0, 0.0).astype(BF16)
+    until = jnp.where(iota((count, count), 0) <= iota((count, count), 1), 1.0, 0.0).astype(BF16)
     both = (keep_ref, recv_ref)
     side = chip
     if pair:
@@ -232,10 +232,10 @@
                 attn_ref[0, rel, j] = query
                 attn_ref[1, rel, j] = key
                 slopes.append(slope_row(ref, 0, j, query) + slope_row(ref, 1, j, key))
-            run = nt(until, hi_lo(ref[0, j].astype(F32) * rows_ref[1, at : at + 1, :]))
-            hi, lo = split_two(run[:, :width] + run[:, width:])
-            run_ref[0, j, rel * count : (rel + 1) * count] = hi
-            run_ref[1, j, rel * count : (rel + 1) * count] = lo
+            run = nn(hi_lo(ref[0, j].astype(F32) * rows_ref[1, at : at + 1, :]), until)
+            hi, lo = split_two(run[:width] + run[width:])
+            run_ref[0, rel, j] = hi
+            run_ref[1, rel, j] = lo
         dg_ref[rel] = jnp.concatenate(slopes, 0)
 
 
@@ -246,9 +246,12 @@
     row = iota((half, width), 0)
     total = jnp.zeros((half, width), F32)
     for j in range(0, half, 2):
-        planes = [jnp.concatenate([run_ref[p, j], run_ref[p, j + 1]], 1) for p in range(2)]
-        got = nn(lhs, planes[0])
-        got = got[:half] + (got[half:] + nn(lhs[:half], planes[1]))
+        planes = [
+            jnp.concatenate([run_ref[p, rel, j : j + 2].reshape(2 * width, count) for rel in range(2)], 1)
+            for p in range(2)
+        ]
+        got = nt(lhs, planes[0])
+        got = got[:half] + (got[half:] + nt(lhs[:half], planes[1]))
         total = total + jnp.where(row == j, got[:, :width], 0.0) + jnp.where(row == j + 1, got[:, width:], 0.0)
     return total
 
@@ -450,7 +453,7 @@
         two = jnp.stack([gate_copy, nearby])
         gates = [
             lax.ppermute(two, "dp", [(i, i ^ far) for i in range(parts)])
-            for far in (2, 6, 4)
+            for far in (4, 2, 6)
         ]
     else:
         gates = [lax.all_gather(gate_weight, "dp", axis=1, tiled=True)]
@@ -460,7 +463,7 @@
     )
     *gates, products = lax.optimization_barrier((*gates, products))
     if direct:
-        gates = [two, gates[0], gates[2], gates[1]]
+        gates = [two, gates[1], gates[0], gates[2]]
 
     sides = 1 if pair else 2
     lines = pltpu.VMEM((2, heads, count), F32)
@@ -479,7 +482,7 @@
     attn_shape = shape(sides, 2, half, width, count, dtype=F32)
     mine_shape = shape(sides, half, width, count)
     send_shape = shape(sides, half + 1, width, count)
-    run_shape = shape(2, half, 2 * count, width)
+    run_shape = shape(2, 2, half, width, count)
 
     def inside(*outs):
         return call(

time: 36.2 us -> 36.4 us (level)
  waiting for transfers between devices: 8.35 us -> 9.59 us
  starting transfers between devices: 15.3 us -> 14.5 us
    ppermute x3, waiting for transfers between devices: 4.12 us -> 5.03 us  [per_device(): lax.ppermute(two, 'dp', [(i, i ^ far) for i in range(parts)])]
    all_to_all x1, starting transfers between devices: 3.8 us -> 2.93 us  [per_device(): pieces = lax.all_to_all(pieces, ('dp', 'ctx'), 0, 0, tiled=True)]
  transfers between devices with their start and end apart: 12 -> 12, of which waited for: 5 -> 5; matrix products, arithmetic and copies ran while one was open for 0% -> 0% of each run, Pallas kernels for 28% -> 27%
where the time goes in v7:
time: 36.4 us; the launch traced here: 36.2 us
  starting transfers between devices  14.5 us (40%)
  Pallas kernels  11.4 us (31%)
  waiting for transfers between devices  9.59 us (26%)
  between operations  0.73 us (2%)
    pallas_call x9, Pallas kernels, call(): pl.pallas_call(kernel, out_shape=out_shape, in_specs=in_specs or [VMEM] *...  11.4 us
    ppermute x3, waiting for transfers between devices, per_device(): lax.ppermute(two, 'dp', [(i, i ^ far) for i in range(parts)])  5.03 us
    ppermute x3, starting transfers between devices, per_device(): lax.ppermute(two, 'dp', [(i, i ^ far) for i in range(parts)])  4.45 us
    ppermute x1, starting transfers between devices, per_device(): nearby = lax.ppermute(gate_weight, 'dp', [(i, i ^ 1) for i in range(parts)])  3.03 us
    all_to_all x1, starting transfers between devices, per_device(): pieces = lax.all_to_all(pieces, ('dp', 'ctx'), 0, 0, tiled=True)  2.93 us
    ppermute x1, waiting for transfers between devices, per_device(): kappa = lax.ppermute(kappa, 'ctx', opposite)  2.14 us
    ppermute x2, starting transfers between devices, per_device(): lax.ppermute(totals[0], 'ctx', [(i, i ^ far) for i in range(ranks)])  1.84 us
    ppermute x1, starting transfers between devices, per_device(): states = [lax.ppermute(total, 'ctx', opposite) for total in totals]  1.55 us
  transfers between devices with their start and end apart: 12, of which 5 were waited for; matrix products, arithmetic and copies ran while one was open for 0% of the time, Pallas kernels for 27%

profile of v7, /device:TPU:0, one launch (start us, length us, event | category | flops | bytes accessed | tf_op | source)
XLA Modules:
  0.0 36.2 jit_solution(17467546212925149356)
XLA Ops:
  0.6 3.0 %collective-permute-start = (bf16[16,16]{1,0:T(8,128)(2,1)}, bf16[16,16]{1,0:T(8,128)(2,1)S(1)}, u32[]{:S(2)}, u32[]{:S(2)}) collective-permute-start(bf16[16,16]{1,0:T(8,128)(2,1)} %gate_ref.1), channel_id=1, source_target_pairs={{0,4},{4,0},{8,12},{12,8},{16,20},{20,16},{24,28},{28,24},{1,5},{5... | collective-permute-start | bytes 1544 | tf_op jit(solution)/shard_map/ppermute | solution.py:451
  3.7 2.1 %split_heads.1 = (bf16[4,8,128,128]{3,2,1,0:T(8,128)(2,1)S(1)}, bf16[4,8,128,128]{3,2,1,0:T(8,128)(2,1)S(1)}, bf16[16,16]{1,0:T(8,128)(2,1)S(1)}) custom-call(bf16[1,128,16,128]{3,2,1,0:T(8,128)(2,1)} %k_ref.1, bf16[1,128,16,128]{3,2,1,0:T(8,128)(2,1)} %q_ref.1, bf16[1,128,16,128]{3,2,1,0:T(8,128)(2,1)} %v_ref.1, bf16[1,128,16,128]{3,2,1,0:T(8,128)(2,1)} %g_ref.1, ...), custom_call_target="tpu_custom_call" | custom-call | bytes 9000000 | tf_op jit(solution)/shard_map/split_heads/pallas_call | solution.py:57
  5.8 0.1 collective-permute-start.4
  5.9 2.8 %collective-permute-start.1 = (bf16[2,16,16]{2,1,0:T(8,128)(2,1)S(1)}, bf16[2,16,16]{2,1,0:T(8,128)(2,1)S(1)}, u32[]{:S(2)}, u32[]{:S(2)}) collective-permute-start(bf16[2,16,16]{2,1,0:T(8,128)(2,1)S(1)} %pad_maximum_fusion.refs_0_), channel_id=1, source_target_pairs={{0,16},{4,20},{8,24},{12,28},{16,0},{20,4},{24,8},{28,12},{1,17},{... | collective-permute-start | bytes 3080 | tf_op jit(solution)/shard_map/ppermute | solution.py:455
  8.6 1.6 %collective-permute-start.2 = (bf16[2,16,16]{2,1,0:T(8,128)(2,1)S(1)}, bf16[2,16,16]{2,1,0:T(8,128)(2,1)S(1)}, u32[]{:S(2)}, u32[]{:S(2)}) collective-permute-start(bf16[2,16,16]{2,1,0:T(8,128)(2,1)S(1)} %pad_maximum_fusion.refs_0_), channel_id=1, source_target_pairs={{0,8},{4,12},{8,0},{12,4},{16,24},{20,28},{24,16},{28,20},{1,9},{5... | collective-permute-start | bytes 3080 | tf_op jit(solution)/shard_map/ppermute | solution.py:455
  10.2 0.1 collective-permute-start.3
  10.3 0.3 products.1.product_ref
  10.6 1.7 %collective-permute-done.2.refs_1_ = bf16[2,16,16]{2,1,0:T(8,128)(2,1)S(1)} collective-permute-done((bf16[2,16,16]{2,1,0:T(8,128)(2,1)S(1)}, bf16[2,16,16]{2,1,0:T(8,128)(2,1)S(1)}, u32[]{:S(2)}, u32[]{:S(2)}) %collective-permute-start.2) | collective-permute-done | bytes 1056 | tf_op jit(solution)/shard_map/ppermute | solution.py:455
  12.3 3.4 %collective-permute-done.3.refs_3_ = bf16[2,16,16]{2,1,0:T(8,128)(2,1)S(1)} collective-permute-done((bf16[2,16,16]{2,1,0:T(8,128)(2,1)S(1)}, bf16[2,16,16]{2,1,0:T(8,128)(2,1)S(1)}, u32[]{:S(2)}, u32[]{:S(2)}) %collective-permute-start.3) | collective-permute-done | bytes 1056 | tf_op jit(solution)/shard_map/ppermute | solution.py:455
  15.7 0.9 %gate_states.1 = (bf16[1,8,128,128]{3,2,1,0:T(8,128)(2,1)S(1)}, bf16[1,8,128,128]{3,2,1,0:T(8,128)(2,1)S(1)}, f32[2,16,128]{2,1,0:T(8,128)S(1)}, f32[2,16,128]{2,1,0:T(8,128)S(1)}) custom-call(bf16[2,16,16]{2,1,0:T(8,128)(2,1)S(1)} %pad_maximum_fusion.refs_0_, bf16[2,16,16]{2,1,0:T(8,128)(2,1)S(1)} %collective-permute-done.2.refs_1_, ...), custom_call_target="tpu_custom_call" | custom-call | bytes 3900000 | tf_op jit(solution)/shard_map/gate_states/pallas_call | solution.py:57
  16.5 1.6 %collective-permute-start.5 = (bf16[1,8,128,128]{3,2,1,0:T(8,128)(2,1)S(1)}, bf16[1,8,128,128]{3,2,1,0:T(8,128)(2,1)S(1)}, u32[]{:S(2)}, u32[]{:S(2)}) collective-permute-start(bf16[1,8,128,128]{3,2,1,0:T(8,128)(2,1)S(1)} %get-tuple-element.42), channel_id=1, source_target_pairs={{0,2},{1,3},{2,0},{3,1},{4,6},{5,7},{6,4},{7,5},{8,10},{9,11},{10,... | collective-permute-start | bytes 786440 | tf_op jit(solution)/shard_map/ppermute | solution.py:502
  18.1 0.3 kappa.1
  18.3 0.6 %collective-permute-start.6 = (f32[8,128]{1,0:T(8,128)S(1)}, f32[8,128]{1,0:T(8,128)S(1)}, u32[]{:S(2)}, u32[]{:S(2)}) collective-permute-start(f32[8,128]{1,0:T(8,128)S(1)} %kappa.1), channel_id=1, source_target_pairs={{0,2},{1,3},{2,0},{3,1},{4,6},{5,7},{6,4},{7,5},{8,10},{9,11},{10,... | collective-permute-start | bytes 12296 | tf_op jit(solution)/shard_map/ppermute | solution.py:505
  18.9 2.5 %inside_block.1 = (f32[1,2,8,128,128]{4,3,2,1,0:T(8,128)S(1)}, bf16[2,2,8,128,128]{4,3,2,1,0:T(8,128)(2,1)S(1)}, f32[2,8,128]{2,1,0:T(8,128)S(1)}, f32[1,8,128,1...) custom-call(bf16[4,8,128,128]{3,2,1,0:T(8,128)(2,1)S(1)} %get-tuple-element.35.keep_ref, ...), custom_call_target="tpu_custom_call" | custom-call | bytes 12000000 | tf_op jit(solution)/shard_map/inside_block/pallas_call | solution.py:57
  21.4 0.1 collective-permute-start.7
  21.5 2.1 %collective-permute-done.6.refs_0_ = f32[8,128]{1,0:T(8,128)S(1)} collective-permute-done((f32[8,128]{1,0:T(8,128)S(1)}, f32[8,128]{1,0:T(8,128)S(1)}, u32[]{:S(2)}, u32[]{:S(2)}) %collective-permute-start.6) | collective-permute-done | bytes 4128 | tf_op jit(solution)/shard_map/ppermute | solution.py:505
  23.6 1.8 %outside_block.1 = (bf16[1,8,128,128]{3,2,1,0:T(8,128)(2,1)S(1)}, bf16[1,9,128,128]{3,2,1,0:T(8,128)(2,1)S(1)}, f32[8,128]{1,0:T(8,128)S(1)}, f32[8,128]{1,0:T(8,128)S(1)}, f32[32,1,128]{2,1,0:T(1,128)}) custom-call(bf16[4,8,128,128]{3,2,1,0:T(8,128)(2,1)S(1)} %get-tuple-element.35.keep_ref.refs_5_, ...), custom_call_target="tpu_custom_call" | custom-call | bytes 3000000 | tf_op jit(solution)/shard_map/outside_block/pallas_call | solution.py:57
  25.4 2.9 %all-to-all-start = ((f32[32,1,128]{2,1,0:T(1,128)}), f32[32,1,128]{2,1,0:T(1,128)S(1)}, u32[]{:S(2)}, u32[]{:S(2)}) async-start(f32[32,1,128]{2,1,0:T(1,128)} %get-tuple-element.55), calls=%async_computation | async-start | bytes 32768 | tf_op jit(solution)/shard_map/all_to_all | solution.py:538
  28.3 1.8 %collective-permute-start.9 = (f32[8,128]{1,0:T(8,128)S(1)}, f32[8,128]{1,0:T(8,128)S(1)}, u32[]{:S(2)}, u32[]{:S(2)}) collective-permute-start(f32[8,128]{1,0:T(8,128)S(1)} %get-tuple-element.58), channel_id=1, source_target_pairs={{0,2},{1,3},{2,0},{3,1},{4,6},{5,7},{6,4},{7,5},{8,10},{9,11},{10,... | collective-permute-start | bytes 12296 | tf_op jit(solution)/shard_map/ppermute | solution.py:537
  30.2 1.9 %merge_heads.1 = (bf16[1,128,16,128]{3,2,1,0:T(8,128)(2,1)}, f32[128,16,128]{2,1,0:T(8,128)S(1)}, f32[128,16,128]{2,1,0:T(8,128)S(1)}) custom-call(f32[2,16,128]{2,1,0:T(8,128)S(1)} %get-tuple-element.40.gate_ref, f32[8,128]{1,0:T(8,128)S(1)} %get-tuple-element.49.suffix_ref, f32[2,16,128]{2,1,0:T(8,128)S(1)} %get-tuple-element.41.rows_ref, ...), custom_call_target="tpu_custom_call" | custom-call | bytes 6000000 | tf_op jit(solution)/shard_map/merge_heads/pallas_call | solution.py:57
  32.1 1.1 %collective-permute-done.10.refs_1_ = f32[8,128]{1,0:T(8,128)S(1)} collective-permute-done((f32[8,128]{1,0:T(8,128)S(1)}, f32[8,128]{1,0:T(8,128)S(1)}, u32[]{:S(2)}, u32[]{:S(2)}) %collective-permute-start.10) | collective-permute-done | bytes 4128 | tf_op jit(solution)/shard_map/ppermute | solution.py:537
  33.2 0.9 %key_gradient.1 = bf16[1,128,16,128]{3,2,1,0:T(8,128)(2,1)} custom-call(f32[128,16,128]{2,1,0:T(8,128)S(1)} %get-tuple-element.56.base_ref, f32[128,16,128]{2,1,0:T(8,128)S(1)} %get-tuple-element.57.rise_ref, f32[8,128]{1,0:T(8,128)S(1)} %collective-permute-done.9.refs_0_, f32[8,128]{1,0:T(8,128)S(1)} %collective-permute-done.10.refs_1_), custom_call_target="tpu_custom_call" | custom-call | bytes 3000000 | tf_op jit(solution)/shard_map/key_gradient/pallas_call | solution.py:57
  34.2 1.3 %all-to-all-done.pieces_ref = f32[32,1,128]{2,1,0:T(1,128)S(1)} async-done(((f32[32,1,128]{2,1,0:T(1,128)}), f32[32,1,128]{2,1,0:T(1,128)S(1)}, u32[]{:S(2)}, u32[]{:S(2)}) %all-to-all-start) | async-done | bytes 16416 | tf_op jit(solution)/shard_map/all_to_all | solution.py:538
  35.5 0.8 %gate_gradient.1 = f32[16,16]{1,0:T(8,128)} custom-call(f32[32,1,128]{2,1,0:T(1,128)S(1)} %all-to-all-done.pieces_ref), custom_call_target="tpu_custom_call" | custom-call | bytes 1500000 | tf_op jit(solution)/shard_map/gate_gradient/pallas_call | solution.py:57
  (12 shorter events, 0.0 us)
Async XLA Ops:
  0.6 5.1 %collective-permute-start = (bf16[16,16]{1,0:T(8,128)(2,1)}, bf16[16,16]{1,0:T(8,128)(2,1)S(1)}, u32[]{:S(2)}, u32[]{:S(2)}) collective-permute-start(bf16[16,16]{1,0:T(8,128)(2,1)} %gate_ref.1), channel_id=1, source_target_pairs={{0,4},{4,0},{8,12},{12,8},{16,20},{20,16},{24,28},{28,24},{1,5},{5... | collective-permute-start | bytes 1544 | tf_op jit(solution)/shard_map/ppermute | solution.py:451
  5.8 9.9 %collective-permute-start.4 = (bf16[4,8,128,128]{3,2,1,0:T(8,128)(2,1)S(1)}, bf16[4,8,128,128]{3,2,1,0:T(8,128)(2,1)S(1)}, u32[]{:S(2)}, u32[]{:S(2)}) collective-permute-start(bf16[4,8,128,128]{3,2,1,0:T(8,128)(2,1)S(1)} %get-tuple-element.39), channel_id=1, source_target_pairs={{0,1},{1,0},{2,3},{3,2},{4,5},{5,4},{6,7},{7,6},{8,9},{9,8},{10,11... | collective-permute-start | bytes 3145736 | tf_op jit(solution)/shard_map/ppermute | solution.py:460
  5.9 4.8 %collective-permute-start.1 = (bf16[2,16,16]{2,1,0:T(8,128)(2,1)S(1)}, bf16[2,16,16]{2,1,0:T(8,128)(2,1)S(1)}, u32[]{:S(2)}, u32[]{:S(2)}) collective-permute-start(bf16[2,16,16]{2,1,0:T(8,128)(2,1)S(1)} %pad_maximum_fusion.refs_0_), channel_id=1, source_target_pairs={{0,16},{4,20},{8,24},{12,28},{16,0},{20,4},{24,8},{28,12},{1,17},{... | collective-permute-start | bytes 3080 | tf_op jit(solution)/shard_map/ppermute | solution.py:455
  8.6 3.7 %collective-permute-start.2 = (bf16[2,16,16]{2,1,0:T(8,128)(2,1)S(1)}, bf16[2,16,16]{2,1,0:T(8,128)(2,1)S(1)}, u32[]{:S(2)}, u32[]{:S(2)}) collective-permute-start(bf16[2,16,16]{2,1,0:T(8,128)(2,1)S(1)} %pad_maximum_fusion.refs_0_), channel_id=1, source_target_pairs={{0,8},{4,12},{8,0},{12,4},{16,24},{20,28},{24,16},{28,20},{1,9},{5... | collective-permute-start | bytes 3080 | tf_op jit(solution)/shard_map/ppermute | solution.py:455
  10.2 5.4 %collective-permute-start.3 = (bf16[2,16,16]{2,1,0:T(8,128)(2,1)S(1)}, bf16[2,16,16]{2,1,0:T(8,128)(2,1)S(1)}, u32[]{:S(2)}, u32[]{:S(2)}) collective-permute-start(bf16[2,16,16]{2,1,0:T(8,128)(2,1)S(1)} %pad_maximum_fusion.refs_0_), channel_id=1, source_target_pairs={{0,24},{4,28},{8,16},{12,20},{16,8},{20,12},{24,0},{28,4},{1,25},{... | collective-permute-start | bytes 3080 | tf_op jit(solution)/shard_map/ppermute | solution.py:455
  10.6 5.1 %copy-start = (bf16[16]{0:T(256)(128)(2,1)S(1)}, bf16[16]{0:T(256)(128)(2,1)}, u32[]{:S(2)}) copy-start(bf16[16]{0:T(256)(128)(2,1)} %param.11) | copy-start | bytes 100
  16.5 7.1 %collective-permute-start.5 = (bf16[1,8,128,128]{3,2,1,0:T(8,128)(2,1)S(1)}, bf16[1,8,128,128]{3,2,1,0:T(8,128)(2,1)S(1)}, u32[]{:S(2)}, u32[]{:S(2)}) collective-permute-start(bf16[1,8,128,128]{3,2,1,0:T(8,128)(2,1)S(1)} %get-tuple-element.42), channel_id=1, source_target_pairs={{0,2},{1,3},{2,0},{3,1},{4,6},{5,7},{6,4},{7,5},{8,10},{9,11},{10,... | collective-permute-start | bytes 786440 | tf_op jit(solution)/shard_map/ppermute | solution.py:502
  18.3 5.3 %collective-permute-start.6 = (f32[8,128]{1,0:T(8,128)S(1)}, f32[8,128]{1,0:T(8,128)S(1)}, u32[]{:S(2)}, u32[]{:S(2)}) collective-permute-start(f32[8,128]{1,0:T(8,128)S(1)} %kappa.1), channel_id=1, source_target_pairs={{0,2},{1,3},{2,0},{3,1},{4,6},{5,7},{6,4},{7,5},{8,10},{9,11},{10,... | collective-permute-start | bytes 12296 | tf_op jit(solution)/shard_map/ppermute | solution.py:505
  21.4 8.8 %collective-permute-start.7 = (bf16[1,9,128,128]{3,2,1,0:T(8,128)(2,1)S(1)}, bf16[1,9,128,128]{3,2,1,0:T(8,128)(2,1)S(1)}, u32[]{:S(2)}, u32[]{:S(2)}) collective-permute-start(bf16[1,9,128,128]{3,2,1,0:T(8,128)(2,1)S(1)} %get-tuple-element.51), channel_id=1, source_target_pairs={{0,1},{1,0},{2,3},{3,2},{4,5},{5,4},{6,7},{7,6},{8,9},{9,8},{10,11... | collective-permute-start | bytes 884744 | tf_op jit(solution)/shard_map/ppermute | solution.py:506
  25.4 4.8 %collective-permute-start.8 = (bf16[1,9,128,128]{3,2,1,0:T(8,128)(2,1)S(1)}, bf16[1,9,128,128]{3,2,1,0:T(8,128)(2,1)S(1)}, u32[]{:S(2)}, u32[]{:S(2)}) collective-permute-start(bf16[1,9,128,128]{3,2,1,0:T(8,128)(2,1)S(1)} %get-tuple-element.53), channel_id=1, source_target_pairs={{0,1},{1,0},{2,3},{3,2},{4,5},{5,4},{6,7},{7,6},{8,9},{9,8},{10,11... | collective-permute-start | bytes 884744 | tf_op jit(solution)/shard_map/ppermute | solution.py:539
  25.4 10.1 %all-to-all-start = ((f32[32,1,128]{2,1,0:T(1,128)}), f32[32,1,128]{2,1,0:T(1,128)S(1)}, u32[]{:S(2)}, u32[]{:S(2)}) async-start(f32[32,1,128]{2,1,0:T(1,128)} %get-tuple-element.55), calls=%async_computation | async-start | bytes 32768 | tf_op jit(solution)/shard_map/all_to_all | solution.py:538
  28.3 3.8 %collective-permute-start.9 = (f32[8,128]{1,0:T(8,128)S(1)}, f32[8,128]{1,0:T(8,128)S(1)}, u32[]{:S(2)}, u32[]{:S(2)}) collective-permute-start(f32[8,128]{1,0:T(8,128)S(1)} %get-tuple-element.58), channel_id=1, source_target_pairs={{0,2},{1,3},{2,0},{3,1},{4,6},{5,7},{6,4},{7,5},{8,10},{9,11},{10,... | collective-permute-start | bytes 12296 | tf_op jit(solution)/shard_map/ppermute | solution.py:537
  30.2 3.0 %collective-permute-start.10 = (f32[8,128]{1,0:T(8,128)S(1)}, f32[8,128]{1,0:T(8,128)S(1)}, u32[]{:S(2)}, u32[]{:S(2)}) collective-permute-start(f32[8,128]{1,0:T(8,128)S(1)} %get-tuple-element.58), channel_id=1, source_target_pairs={{0,3},{1,2},{2,1},{3,0},{4,7},{5,6},{6,5},{7,4},{8,11},{9,10},{10,... | collective-permute-start | bytes 12296 | tf_op jit(solution)/shard_map/ppermute | solution.py:537
